TPU v7x, 32 devices: a whole 2x2x4 slice. The times are simulated.
32 devices in a mesh: dp: 16 (over z, x, core), tensor: 2 (over y).
Axes of the slice: x: 2, y: 2, z: 4, core: 2. Of those that a mesh axis runs over, the one named last changes fastest.
Arguments:
- block_input: bfloat16 [8192, 1536], P(('dp', 'tensor')), may hold values from -6 to 6
- norm_gains: float32 [1536, 2], replicated, may hold values from 0.1 to 1.9
- router_weight: bfloat16 [1536, 8], replicated, may hold values from -0.078125 to 0.078125
- query_matrix: bfloat16 [1536, 1536], P('dp', 'tensor'), may hold values from -0.15625 to 0.15625
- key_matrix: bfloat16 [1536, 256], P('dp', 'tensor'), may hold values from -0.15625 to 0.15625
- value_matrix: bfloat16 [1536, 256], P('dp', 'tensor'), may hold values from -0.15625 to 0.15625
- output_weight: bfloat16 [1536, 1536], P('dp', 'tensor'), may hold values from -0.875 to 0.875
- gate_weight: bfloat16 [1536, 8, 768], P('dp', None, 'tensor'), may hold values from -0.15625 to 0.15625
- up_weight: bfloat16 [1536, 8, 768], P('dp', None, 'tensor'), may hold values from -0.15625 to 0.15625
- down_weight: bfloat16 [1536, 8, 768], P('dp', None, 'tensor'), may hold values from -0.4375 to 0.4375
- segment_ids: int32 [8192], P('dp'), may hold values from 0 to 15, never falling along the last dimension, each value on 1 to 2048 neighbouring positions
- routes: int32 [8192, 4], P('dp'), may hold values from 0 to 7, all different within a row
- priority: int32 [32768], P('dp'), may hold values from 0 to 2047, as said below
- cotangent: bfloat16 [8192, 1536], P(('dp', 'tensor')), may hold values from -6 to 6
Outputs:
- block_output: float32 [8192, 1536], P(('dp', 'tensor'))
- input_grad: float32 [8192, 1536], P(('dp', 'tensor'))
- gains_grad: float32 [1536, 2], P(('dp', 'tensor'))
- router_grad: float32 [1536, 8], P(('dp', 'tensor'))
- query_grad: float32 [1536, 1536], P('dp', 'tensor')
- key_grad: float32 [1536, 256], P('dp', 'tensor')
- value_grad: float32 [1536, 256], P('dp', 'tensor')
- output_weight_grad: float32 [1536, 1536], P('dp', 'tensor')
- gate_grad: float32 [1536, 8, 768], P('dp', None, 'tensor')
- up_grad: float32 [1536, 8, 768], P('dp', None, 'tensor')
- down_grad: float32 [1536, 8, 768], P('dp', None, 'tensor')
Inputs may be any that keep to these rules, and one draw needn't show every extreme that they name: `segment_ids`: segment numbers never fall along the tokens; a segment covers 1 to 2048 consecutive tokens. `routes`: each token names 4 different experts. `priority`: each aligned block of 2048 entries (one group's pairs) holds every number of 0 to 2047 once.
All inputs are finite; a program needn't handle non-finite values.
Results may differ from a plain program's by a relative error of at most 0.02.
Values may be sent and summed in bfloat16 or wider, within the bound.
No kernel may reach another device: no remote copies, remote signals or barrier semaphores. Data moves between devices by JAX's collectives and lax.ppermute only.
A program may use at most 256 MiB of HBM per device.

v0:
```python
import functools
import math

import jax
import jax.numpy as jnp
from jax import lax
from jax.experimental import pallas as pl
from jax.experimental.pallas import tpu as pltpu
from jax.sharding import Mesh
from jax.sharding import PartitionSpec as P

HEAD_SIZE = 128
TOPK = 4
EXPERTS = 8
ATTEND_SPAN = 1024
SEQ_MOST = 16384
EPSILON = 1e-06
ROPE_BASE = 10000.0
BF16 = jnp.bfloat16
F32 = jnp.float32

DP = ("outer", "x", "core")
PLANE = ("x", "core", "tensor")
ALL = ("outer", "x", "core", "tensor")


def shift_groups(x, by):
    length = lax.axis_size(DP)
    return lax.ppermute(x, DP, [(i, i + by) for i in range(length) if 0 <= i + by < length])


def swap(x, axis):
    length = lax.axis_size(axis)
    return lax.ppermute(x, axis, [(i, length - 1 - i) for i in range(length)])


def plane_parts(own):
    return [own, swap(own, "tensor"), swap(own, "x"), swap(own, ("x", "tensor"))]


def plane_stack(parts):
    return jnp.stack(parts).reshape((2, 2) + parts[0].shape)


def whole_weight(near, far):
    x, tensor = lax.axis_index("x"), lax.axis_index("tensor")
    first = lax.axis_index("core") == 0
    by_core = [jnp.where(first, near, far), jnp.where(first, far, near)]

    def piece(x_at, core_at, tensor_at):
        picked = lax.dynamic_index_in_dim(by_core[core_at], x ^ x_at, 0, keepdims=False)
        return lax.dynamic_index_in_dim(picked, tensor ^ tensor_at, 0, keepdims=False)

    places = [(x_at, core_at) for x_at in range(2) for core_at in range(2)]
    halves = [jnp.stack([piece(*place, at) for place in places], 1) for at in range(2)]
    return jnp.concatenate(halves, axis=-1).reshape(-1, 2 * near.shape[-1])


def fold_core(kept, sent):
    return (kept.astype(F32) + swap(sent, "core").astype(F32)).astype(BF16)


def fold_blocks(kept, got):
    return [
        (kept[at].astype(F32) + got[at].astype(F32)).astype(BF16) for at in range(kept.shape[0])
    ]


def in_order(own, other, axis_name, axis):
    first = lax.axis_index(axis_name) == 0
    return jnp.stack([jnp.where(first, own, other), jnp.where(first, other, own)], axis)


def fold_plane(blocks):
    return [
        blocks[0],
        swap(blocks[1], "tensor"),
        swap(blocks[2], "x"),
        swap(blocks[3], ("x", "tensor")),
    ]


def wide_sum(parts):
    return sum(part.astype(F32) for part in parts)


def outer_shift(x, by):
    length = lax.axis_size("outer")
    return lax.ppermute(x, "outer", [(i, (i + by) % length) for i in range(length)])


def outer_gather(shard):
    length, here = lax.axis_size("outer"), lax.axis_index("outer")
    if length > 4:
        return lax.all_gather(shard, "outer")
    full = jnp.zeros((length,) + shard.shape, shard.dtype)
    for by in range(length):
        piece = outer_shift(shard, by) if by else shard
        full = lax.dynamic_update_slice_in_dim(full, piece[None], (here - by) % length, 0)
    return full


def outer_scatter(parts):
    length, here = lax.axis_size("outer"), lax.axis_index("outer")
    if length > 4:
        return lax.psum_scatter(parts, "outer", scatter_dimension=0, tiled=False).astype(F32)
    pieces = [
        lax.dynamic_index_in_dim(parts, (here + by) % length, 0, keepdims=False)
        for by in range(length)
    ]
    return wide_sum([pieces[0]] + [outer_shift(pieces[by], by) for by in range(1, length)])


def core_columns(rows, core_at, shard_rows):
    count = rows.shape[0]
    split = rows.reshape(count, -1, 2, shard_rows)
    return lax.dynamic_index_in_dim(split, core_at, 2, keepdims=False).reshape(count, -1)


def fold_columns(left, right, shard_rows):
    core = lax.axis_index("core")
    sent = dot(core_columns(left, 1 - core, shard_rows), right, ((0,), (0,))).astype(BF16)
    kept = dot(core_columns(left, core, shard_rows), right, ((0,), (0,))).astype(BF16)
    return fold_core(kept, sent).reshape(-1, 2, shard_rows, right.shape[1])


def distance_blocks(total):
    x, tensor = lax.axis_index("x"), lax.axis_index("tensor")
    columns = total.shape[3] // 2
    blocks = []
    for x_by in range(2):
        for tensor_by in range(2):
            block = lax.dynamic_index_in_dim(total, x ^ x_by, 1, keepdims=False)
            start = (tensor ^ tensor_by) * columns
            blocks.append(lax.dynamic_slice_in_dim(block, start, columns, 2))
    return blocks


def rotary_tables(position):
    halfway = HEAD_SIZE // 2
    inverse = jnp.exp(
        jnp.arange(halfway, dtype=F32) * (-2.0 * math.log(ROPE_BASE) / HEAD_SIZE)
    )
    angles = position.astype(F32)[:, None] * inverse[None, :]
    cosine, sine = jnp.cos(angles), jnp.sin(angles)
    return (
        jnp.concatenate([cosine, cosine], axis=1),
        jnp.concatenate([-sine, sine], axis=1),
    )


def norm_factor(value_rows):
    return lax.rsqrt(jnp.mean(value_rows * value_rows, axis=-1, keepdims=True) + EPSILON)


def norm_back(value_rows, factor, gain, upstream):
    weighted = upstream * gain
    return factor * weighted - value_rows * (factor * factor * factor) * jnp.mean(
        weighted * value_rows, axis=-1, keepdims=True
    )


def dot(a, b, dims):
    return lax.dot_general(a, b, (dims, ((), ())), preferred_element_type=F32)


VMEM_LIMIT = 60 * 1024 * 1024
LIGHT = pl.CostEstimate(flops=1000, bytes_accessed=1000, transcendentals=0)
FROM_LAST = (((1,), (1,)), ((), ()))
PLAIN = (((1,), (0,)), ((), ()))


def mxu(a, b, dims=PLAIN):
    return lax.dot_general(a, b, dims, preferred_element_type=F32)


def turn(rows, cosine, sine):
    return rows * cosine + pltpu.roll(rows, HEAD_SIZE // 2, 1) * sine


def project_kernel(rows_ref, weight_ref, cosine_ref, sine_ref, out_ref, *, turned):
    product = mxu(rows_ref[...], weight_ref[...])
    for at, turns in enumerate(turned):
        part = product[:, at * HEAD_SIZE : (at + 1) * HEAD_SIZE]
        if turns:
            part = turn(part, cosine_ref[...], sine_ref[...])
        out_ref[:, at * HEAD_SIZE : (at + 1) * HEAD_SIZE] = part.astype(BF16)


def project(rows, weight, cosine, sine, first, count, turned):
    high, width = rows.shape
    columns = len(turned) * HEAD_SIZE
    return pl.pallas_call(
        functools.partial(project_kernel, turned=turned),
        grid=(count,),
        in_specs=[
            pl.BlockSpec((high, width), lambda j: (0, 0)),
            pl.BlockSpec((width, columns), lambda j: (0, first + j)),
            pl.BlockSpec((high, HEAD_SIZE), lambda j: (0, 0)),
            pl.BlockSpec((high, HEAD_SIZE), lambda j: (0, 0)),
        ],
        out_specs=pl.BlockSpec((high, columns), lambda j: (0, j)),
        out_shape=jax.ShapeDtypeStruct((high, count * columns), BF16),
        compiler_params=pltpu.CompilerParams(vmem_limit_bytes=VMEM_LIMIT),
        cost_estimate=LIGHT,
        name="project",
    )(rows, weight, cosine, sine)


def mask_bias(place_ref, segment_key_ref, segment_query_ref, bias_ref, seq_len):
    span, rows = bias_ref.shape
    start = place_ref[0]
    key_at = lax.broadcasted_iota(jnp.int32, (span, rows), 0)
    query_at = lax.broadcasted_iota(jnp.int32, (span, rows), 1) + ATTEND_SPAN
    distance = query_at - key_at
    position = start + query_at - ATTEND_SPAN
    sequence_at = query_at - lax.rem(position, seq_len)
    allowed = (distance >= 0) & (distance < ATTEND_SPAN) & (key_at >= sequence_at)
    allowed = allowed & (segment_key_ref[...] == segment_query_ref[...])
    bias_ref[...] = jnp.where(allowed, 0.0, -1e30)


def attention_kernel(
    place_ref,
    segment_key_ref,
    segment_query_ref,
    q_ref,
    kv_ref,
    heads_ref,
    lse_ref,
    bias_ref,
    *,
    seq_len,
    scale,
):
    @pl.when(pl.program_id(0) == 0)
    def _():
        mask_bias(place_ref, segment_key_ref, segment_query_ref, bias_ref, seq_len)

    rows = q_ref.shape[0]
    span = kv_ref.shape[0]
    count = q_ref.shape[1] // HEAD_SIZE
    value_t = kv_ref[:, HEAD_SIZE:].T
    chunks = span // rows
    for head in range(count):
        columns = slice(head * HEAD_SIZE, (head + 1) * HEAD_SIZE)
        query = q_ref[:, columns]
        scores = []
        for c in range(chunks):
            part = slice(c * rows, (c + 1) * rows)
            raw = mxu(kv_ref[part, :HEAD_SIZE], query, FROM_LAST)
            scores.append(raw * scale + bias_ref[part, :])
        top = functools.reduce(jnp.maximum, scores)
        top = jnp.max(top, axis=0, keepdims=True)
        total = jnp.zeros_like(top)
        out_t = jnp.zeros((HEAD_SIZE, rows), F32)
        for c in range(chunks):
            weight = jnp.exp(scores[c] - top)
            total = total + jnp.sum(weight, axis=0, keepdims=True)
            out_t = out_t + mxu(value_t[:, c * rows : (c + 1) * rows], weight.astype(BF16))
        heads_ref[:, columns] = (out_t / total).T.astype(BF16)
        lse_ref[0, head : head + 1, :] = top + jnp.log(total)


def attention(place, segment_key, segment_query, queries, key_value, seq_len):
    rows, all_columns = queries.shape
    span = key_value.shape[0]
    pairs = key_value.shape[1] // (2 * HEAD_SIZE)
    columns = all_columns // pairs
    return pl.pallas_call(
        functools.partial(attention_kernel, seq_len=seq_len, scale=1.0 / math.sqrt(HEAD_SIZE)),
        grid=(pairs,),
        in_specs=[
            pl.BlockSpec(memory_space=pltpu.SMEM),
            pl.BlockSpec((span, 1), lambda j: (0, 0)),
            pl.BlockSpec((1, rows), lambda j: (0, 0)),
            pl.BlockSpec((rows, columns), lambda j: (0, j)),
            pl.BlockSpec((span, 2 * HEAD_SIZE), lambda j: (0, j)),
        ],
        out_specs=[
            pl.BlockSpec((rows, columns), lambda j: (0, j)),
            pl.BlockSpec((1, columns // HEAD_SIZE, rows), lambda j: (j, 0, 0)),
        ],
        out_shape=[
            jax.ShapeDtypeStruct((rows, all_columns), BF16),
            jax.ShapeDtypeStruct((pairs, columns // HEAD_SIZE, rows), F32),
        ],
        scratch_shapes=[pltpu.VMEM((span, rows), F32)],
        compiler_params=pltpu.CompilerParams(vmem_limit_bytes=VMEM_LIMIT),
        cost_estimate=LIGHT,
        name="attention",
    )(place, segment_key, segment_query, queries, key_value)


def attention_back_kernel(
    place_ref,
    segment_key_ref,
    segment_query_ref,
    q_ref,
    kv_ref,
    lse_ref,
    dout_ref,
    cosine_ref,
    sine_ref,
    dq_ref,
    dkv_far_ref,
    dkv_own_ref,
    bias_ref,
    dkv_ref,
    *,
    seq_len,
    scale,
):
    @pl.when(pl.program_id(0) == 0)
    def _():
        mask_bias(place_ref, segment_key_ref, segment_query_ref, bias_ref, seq_len)

    rows = q_ref.shape[0]
    span = kv_ref.shape[0]
    count = q_ref.shape[1] // HEAD_SIZE
    key_t = kv_ref[:, :HEAD_SIZE].T
    chunks = span // rows
    dkv_ref[...] = jnp.zeros_like(dkv_ref)
    for head in range(count):
        columns = slice(head * HEAD_SIZE, (head + 1) * HEAD_SIZE)
        query = q_ref[:, columns]
        dout = dout_ref[:, columns]
        lse = lse_ref[0, head : head + 1, :]
        probs, dprobs = [], []
        row_dot = jnp.zeros_like(lse)
        for c in range(chunks):
            part = slice(c * rows, (c + 1) * rows)
            raw = mxu(kv_ref[part, :HEAD_SIZE], query, FROM_LAST)
            prob = jnp.exp(raw * scale + bias_ref[part, :] - lse)
            dprob = mxu(kv_ref[part, HEAD_SIZE:], dout, FROM_LAST)
            row_dot = row_dot + jnp.sum(prob * dprob, axis=0, keepdims=True)
            probs.append(prob)
            dprobs.append(dprob)
        dq_t = jnp.zeros((HEAD_SIZE, rows), F32)
        for c in range(chunks):
            part = slice(c * rows, (c + 1) * rows)
            dscore = (probs[c] * (dprobs[c] - row_dot)).astype(BF16)
            dkv_ref[part, :HEAD_SIZE] += mxu(dscore, query)
            dkv_ref[part, HEAD_SIZE:] += mxu(probs[c].astype(BF16), dout)
            dq_t = dq_t + mxu(key_t[:, part], dscore)
        dq_ref[:, columns] = turn(dq_t.T * scale, cosine_ref[...], -sine_ref[...]).astype(BF16)
    dkv_ref[:, :HEAD_SIZE] = dkv_ref[:, :HEAD_SIZE] * scale
    dkv_far_ref[...] = dkv_ref[: span - rows, :].astype(BF16)
    dkv_own_ref[...] = dkv_ref[span - rows :, :]


def attention_back(
    place, segment_key, segment_query, queries, key_value, lse, dout, cosine, sine, seq_len
):
    rows, all_columns = queries.shape
    span = key_value.shape[0]
    pairs = key_value.shape[1] // (2 * HEAD_SIZE)
    columns = all_columns // pairs
    return pl.pallas_call(
        functools.partial(
            attention_back_kernel, seq_len=seq_len, scale=1.0 / math.sqrt(HEAD_SIZE)
        ),
        grid=(pairs,),
        in_specs=[
            pl.BlockSpec(memory_space=pltpu.SMEM),
            pl.BlockSpec((span, 1), lambda j: (0, 0)),
            pl.BlockSpec((1, rows), lambda j: (0, 0)),
            pl.BlockSpec((rows, columns), lambda j: (0, j)),
            pl.BlockSpec((span, 2 * HEAD_SIZE), lambda j: (0, j)),
            pl.BlockSpec((1, columns // HEAD_SIZE, rows), lambda j: (j, 0, 0)),
            pl.BlockSpec((rows, columns), lambda j: (0, j)),
            pl.BlockSpec((rows, HEAD_SIZE), lambda j: (0, 0)),
            pl.BlockSpec((rows, HEAD_SIZE), lambda j: (0, 0)),
        ],
        out_specs=[
            pl.BlockSpec((rows, columns), lambda j: (0, j)),
            pl.BlockSpec((span - rows, 2 * HEAD_SIZE), lambda j: (0, j)),
            pl.BlockSpec((rows, 2 * HEAD_SIZE), lambda j: (0, j)),
        ],
        out_shape=[
            jax.ShapeDtypeStruct((rows, all_columns), BF16),
            jax.ShapeDtypeStruct((span - rows, key_value.shape[1]), BF16),
            jax.ShapeDtypeStruct((rows, key_value.shape[1]), F32),
        ],
        scratch_shapes=[
            pltpu.VMEM((span, rows), F32),
            pltpu.VMEM((span, 2 * HEAD_SIZE), F32),
        ],
        compiler_params=pltpu.CompilerParams(vmem_limit_bytes=VMEM_LIMIT),
        cost_estimate=pl.CostEstimate(
            flops=70_000_000_000, bytes_accessed=10_000_000, transcendentals=0
        ),
        name="attention_back",
    )(place, segment_key, segment_query, queries, key_value, lse, dout, cosine, sine)


def expert_kernel(
    slot_row_ref,
    slot_column_ref,
    routed_ref,
    own_ref,
    router_ref,
    tokens_ref,
    cotangent_ref,
    gate_ref,
    up_ref,
    down_ref,
    grad_ref,
    moe_ref,
    rows_in_ref,
    grad_out_ref,
    hidden_ref,
    grad_gate_ref,
    grad_up_ref,
    router_grad_ref,
    gate_full_ref,
    up_full_ref,
    down_full_ref,
    *,
    capacity,
):
    whole = ((gate_ref, gate_full_ref), (up_ref, up_full_ref), (down_ref, down_full_ref))

    @pl.when(pl.program_id(0) == 0)
    def _():
        for held, full in whole:
            columns = held.shape[3]
            for half in range(held.shape[1]):
                full[:, half * columns : (half + 1) * columns] = held[:, half].reshape(-1, columns)

    group_rows = tokens_ref.shape[1]
    tokens = tokens_ref[0]
    gate_weight, up_weight, down_weight = (full[...] for _, full in whole)
    cotangent = cotangent_ref[0]
    routed = routed_ref[0] > 0.0
    logits = jnp.where(routed, mxu(router_ref[...], tokens, FROM_LAST), -1e30)
    weights = jnp.exp(logits - jnp.max(logits, axis=0, keepdims=True))
    weights = jnp.where(routed, weights, 0.0)
    gates = weights / jnp.sum(weights, axis=0, keepdims=True)
    own = own_ref[...]
    gate_own = jnp.sum(gates * own, axis=0, keepdims=True)
    place = slot_row_ref[0] == lax.broadcasted_iota(jnp.int32, (capacity, group_rows), 0)
    place_wide = jnp.where(place, 1.0, 0.0)
    place_low = place_wide.astype(BF16)
    back = slot_column_ref[0] == lax.broadcasted_iota(jnp.int32, (group_rows, capacity), 1)
    back_low = jnp.where(back, 1.0, 0.0).astype(BF16)
    coefficient = jnp.sum(place_wide * gate_own, axis=1, keepdims=True)

    rows_in = mxu(place_low, tokens).astype(BF16)
    rows_in_ref[...] = rows_in
    gate_pre = mxu(rows_in, gate_weight)
    up_pre = mxu(rows_in, up_weight)
    sigmoid = 1.0 / (1.0 + jnp.exp(-gate_pre))
    silu = gate_pre * sigmoid
    hidden = (silu * up_pre).astype(BF16)
    hidden_ref[...] = hidden
    slot_cotangent = mxu(place_low, cotangent)
    grad_out = (coefficient * slot_cotangent).astype(BF16)
    grad_out_ref[...] = grad_out
    grad_hidden = mxu(grad_out, down_weight)
    grad_up = (grad_hidden * silu).astype(BF16)
    grad_gate = (grad_hidden * up_pre * sigmoid * (1.0 + gate_pre * (1.0 - sigmoid))).astype(BF16)
    grad_up_ref[...] = grad_up
    grad_gate_ref[...] = grad_gate
    expert_out = mxu(hidden, down_weight, FROM_LAST)
    grad_slot = jnp.sum(slot_cotangent * expert_out, axis=1, keepdims=True)
    moe_ref[0] = mxu(back_low, (coefficient * expert_out).astype(BF16)).astype(BF16)

    grad_token = jnp.sum(place_wide * grad_slot, axis=0, keepdims=True)
    share = (grad_token * gate_own) * (own - gates)
    share_high = share.astype(BF16)
    share_low = (share - share_high.astype(F32)).astype(BF16)
    router_grad = mxu(share_high, tokens) + mxu(share_low, tokens)

    @pl.when(pl.program_id(0) == 0)
    def _():
        router_grad_ref[...] = router_grad

    @pl.when(pl.program_id(0) > 0)
    def _():
        router_grad_ref[...] += router_grad

    grad_in = mxu(grad_gate, gate_weight, FROM_LAST) + mxu(grad_up, up_weight, FROM_LAST)
    grad_ref[0] = (
        mxu(back_low, grad_in.astype(BF16)) + mxu(share.T.astype(BF16), router_ref[...])
    ).astype(BF16)


def expert_groups(slot, routed, own, router_t, tokens, cotangent, weights, capacity):
    count, group_rows, width = tokens.shape
    ff = weights[0].shape[1] * weights[0].shape[3]
    experts = router_t.shape[0]
    weight = pl.BlockSpec(
        weights[0].shape, lambda g: (0, 0, 0, 0), pipeline_mode=pl.Buffered(1)
    )
    whole = lambda g: (0, 0)
    by_group = lambda g: (g, 0, 0)
    slots = lambda columns: pl.BlockSpec((capacity, columns), lambda g: (g, 0))
    slots_shape = lambda columns: jax.ShapeDtypeStruct((count * capacity, columns), BF16)
    return pl.pallas_call(
        functools.partial(expert_kernel, capacity=capacity),
        grid=(count,),
        in_specs=[
            pl.BlockSpec((1, 1, group_rows), by_group),
            pl.BlockSpec((1, group_rows, 1), by_group),
            pl.BlockSpec((1, experts, group_rows), by_group),
            pl.BlockSpec((experts, 1), whole),
            pl.BlockSpec((experts, width), whole),
            pl.BlockSpec((1, group_rows, width), by_group),
            pl.BlockSpec((1, group_rows, width), by_group),
            weight,
            weight,
            weight,
        ],
        out_specs=[
            pl.BlockSpec((1, group_rows, width), by_group),
            pl.BlockSpec((1, group_rows, width), by_group),
            slots(width),
            slots(width),
            slots(ff),
            slots(ff),
            slots(ff),
            pl.BlockSpec((experts, width), whole),
        ],
        out_shape=[
            jax.ShapeDtypeStruct(tokens.shape, BF16),
            jax.ShapeDtypeStruct(tokens.shape, BF16),
            slots_shape(width),
            slots_shape(width),
            slots_shape(ff),
            slots_shape(ff),
            slots_shape(ff),
            jax.ShapeDtypeStruct((experts, width), F32),
        ],
        scratch_shapes=[pltpu.VMEM((width, ff), BF16) for _ in range(3)],
        compiler_params=pltpu.CompilerParams(vmem_limit_bytes=VMEM_LIMIT),
        cost_estimate=LIGHT,
        name="expert",
    )(
        slot[:, None, :],
        slot[:, :, None],
        routed,
        own,
        router_t,
        tokens,
        cotangent,
        *weights,
    )


def weight_grad_kernel(*refs, halves):
    rows, grad_out, hidden, grad_gate, grad_up, router = (
        refs[at : at + 2] for at in range(0, 12, 2)
    )
    moe_kept_ref, moe_got_ref, out_ref = refs[12:15]
    for at, moe_ref in enumerate(refs[15:]):
        moe_ref[...] = (moe_kept_ref[at].astype(F32) + moe_got_ref[at].astype(F32)).astype(BF16)
    columns = hidden[0].shape[1] // halves
    over = (((0,), (0,)), ((), ()))
    left_rows = [ref[...] for ref in rows]
    left_out = [ref[...] for ref in grad_out]
    router_columns = (router[0][...] + router[1][...]).T
    router_columns = jnp.concatenate(
        [
            router_columns,
            jnp.zeros((router_columns.shape[0], HEAD_SIZE - router_columns.shape[1]), F32),
        ],
        axis=1,
    ).astype(BF16)
    for half in range(halves):
        start = half * (3 * columns + HEAD_SIZE)
        part = slice(half * columns, (half + 1) * columns)
        for at, (left, right) in enumerate(
            ((left_rows, grad_gate), (left_rows, grad_up), (left_out, hidden))
        ):
            total = mxu(left[0], right[0][:, part], over) + mxu(left[1], right[1][:, part], over)
            out_ref[:, start + at * columns : start + (at + 1) * columns] = total.astype(BF16)
        out_ref[:, start + 3 * columns : start + 3 * columns + HEAD_SIZE] = router_columns


def weight_grads(near, far, moe_kept, moe_got, halves, block=256):
    rows_at, grad_out_at, hidden_at, grad_gate_at, grad_up_at, router_at = range(6)
    slots, width = near[rows_at].shape
    ff = near[hidden_at].shape[1]
    experts = near[router_at].shape[0]
    specs, operands = [], []
    for at in (rows_at, grad_out_at, hidden_at, grad_gate_at, grad_up_at, router_at):
        if at in (rows_at, grad_out_at):
            spec = pl.BlockSpec((slots, block), lambda i: (0, i))
        elif at == router_at:
            spec = pl.BlockSpec((experts, block), lambda i: (0, i))
        else:
            spec = pl.BlockSpec((slots, ff), lambda i: (0, 0))
        specs += [spec, spec]
        operands += [near[at], far[at]]
    columns = 3 * ff + halves * HEAD_SIZE
    moe_count, moe_rows, _ = moe_kept.shape
    moe_spec = pl.BlockSpec((moe_count, moe_rows, block), lambda i: (0, 0, i))
    moe_out_spec = pl.BlockSpec((moe_rows, block), lambda i: (0, i))
    return pl.pallas_call(
        functools.partial(weight_grad_kernel, halves=halves),
        grid=(width // block,),
        in_specs=specs + [moe_spec, moe_spec],
        out_specs=[pl.BlockSpec((block, columns), lambda i: (i, 0))] + [moe_out_spec] * moe_count,
        out_shape=[jax.ShapeDtypeStruct((width, columns), BF16)]
        + [jax.ShapeDtypeStruct((moe_rows, width), BF16)] * moe_count,
        compiler_params=pltpu.CompilerParams(vmem_limit_bytes=VMEM_LIMIT),
        cost_estimate=pl.CostEstimate(
            flops=15_000_000_000, bytes_accessed=50_000_000, transcendentals=0
        ),
        name="weight_grads",
    )(*operands, moe_kept, moe_got)


def on_device(
    block_input,
    norm_gains,
    router_weight,
    query_matrix,
    key_matrix,
    value_matrix,
    output_weight,
    gate_weight,
    up_weight,
    down_weight,
    segment_ids,
    routes,
    priority,
    cotangent,
):
    tensor_index = lax.axis_index("tensor")
    own_rows, width = block_input.shape
    group_rows = segment_ids.shape[0]
    halves = lax.axis_size("tensor")
    outer = lax.axis_size("outer")
    groups = lax.axis_size("x") * lax.axis_size("core")
    plane = groups * halves
    shard_rows = query_matrix.shape[0]
    dp_size = outer * groups
    seq_len = min(SEQ_MOST, group_rows * dp_size)
    own_start = lax.axis_index(ALL) * own_rows
    capacity = group_rows * TOPK // EXPERTS
    reach = ATTEND_SPAN // own_rows
    half_ff = gate_weight.shape[2]
    ff = half_ff * halves

    query_columns = query_matrix.shape[1]
    pair_columns = 2 * halves * HEAD_SIZE
    first = tensor_index == 0
    key_value_weight = jnp.concatenate([key_matrix, value_matrix], axis=1)
    other_weight = swap(key_value_weight, "tensor")
    early = jnp.concatenate(
        [
            jnp.where(first, key_value_weight, other_weight),
            jnp.where(first, other_weight, key_value_weight),
            query_matrix,
            output_weight,
        ],
        axis=1,
    )
    early, gate_own, up_own, down_own, cotangent_own = lax.optimization_barrier(
        (early, gate_weight, up_weight, down_weight, cotangent)
    )
    early = outer_gather(early)

    expert_shard = jnp.transpose(jnp.stack([gate_own, up_own, down_own]), (2, 0, 1, 3))
    expert_shard = lax.all_to_all(expert_shard, PLANE, 0, 0, tiled=True)
    expert_shard = expert_shard.reshape(groups, halves, 3, shard_rows, half_ff)
    expert_shard = [
        jnp.swapaxes(expert_shard[:, :, at], 0, 1).reshape(-1, half_ff) for at in range(3)
    ]
    early, expert_shard, segment_here, priority_here = lax.optimization_barrier(
        (early, expert_shard, segment_ids, priority)
    )
    pair_count = group_rows * TOPK
    rank = (
        jnp.zeros((pair_count,), jnp.int32)
        .at[priority_here]
        .set(jnp.arange(pair_count, dtype=jnp.int32))
        .reshape(group_rows, TOPK)
    )
    expert_ids = jnp.arange(EXPERTS, dtype=jnp.int32)
    named = routes[:, :, None] == expert_ids[None, None, :]
    ranked = jnp.sum(jnp.where(named, rank[:, :, None] + 1, 0), axis=1)
    ranked = jnp.where(ranked > 0, ranked, pair_count + 1)
    ranked_own = lax.dynamic_slice_in_dim(ranked, tensor_index * own_rows, own_rows, 0)
    digits = jnp.concatenate([ranked_own // 64, ranked_own % 64], axis=1).astype(BF16)
    digits = jnp.pad(digits, ((0, 0), (0, HEAD_SIZE - digits.shape[1])))
    cotangent_sent = jnp.concatenate([cotangent_own, digits], axis=1)
    segment_near = jnp.concatenate(
        [shift_groups(segment_here, 2), shift_groups(segment_here, 1), segment_here]
    )
    expert_full = [
        lax.all_gather(shard, "outer").reshape(outer, halves, groups * shard_rows, half_ff)
        for shard in expert_shard
    ]

    key_value_full = early[:, :, :pair_columns]
    key_value_full = in_order(key_value_full, swap(key_value_full, "x"), "x", 1)
    key_value_full = in_order(key_value_full, swap(key_value_full, "core"), "core", 2)
    key_value_full = key_value_full.reshape(width, pair_columns)
    query_parts = plane_parts(early[:, :, pair_columns : pair_columns + query_columns])

    input_wide = block_input.astype(F32)
    first_gain = norm_gains[:, 0]
    second_gain = norm_gains[:, 1]
    first_factor = norm_factor(input_wide)
    normed_in = (input_wide * first_factor * first_gain).astype(BF16)
    positions = own_start + jnp.arange(own_rows, dtype=jnp.int32)
    cosine, sine = rotary_tables(positions % seq_len)
    query_blocks = halves * query_columns // (2 * HEAD_SIZE)
    key_value_sent = project(
        normed_in, key_value_full, cosine, sine, 0, halves, (True, False)
    )
    one_back, two_back = shift_groups(key_value_sent, 1), shift_groups(key_value_sent, 2)
    query_parts, one_back, two_back, segment_near, cotangent_sent, expert_full[0] = (
        lax.optimization_barrier(
            (query_parts, one_back, two_back, segment_near, cotangent_sent, expert_full[0])
        )
    )
    cotangent_parts = plane_parts(cotangent_sent)
    output_own = early[:, :, pair_columns + query_columns :]
    pair_sent = jnp.where(
        first,
        jnp.stack([one_back, key_value_sent]),
        jnp.stack([two_back, one_back]),
    )
    pair_got = swap(pair_sent, "tensor")
    query_near = plane_stack(query_parts)
    query_far, pair_got = lax.optimization_barrier((swap(query_near, "core"), pair_got))
    pieces = [two_back, pair_got[0], one_back, pair_got[1], key_value_sent]
    query_full = whole_weight(query_near, query_far)
    queries = project(normed_in, query_full, cosine, sine, 0, query_blocks, (True, True))
    output_parts = plane_parts(output_own)
    expert = lax.axis_index(PLANE)

    def slots_of(cotangents):
        digits = cotangents[..., width:].reshape(2, group_rows, HEAD_SIZE).astype(jnp.int32)
        ranked_all = digits[..., :EXPERTS] * 64 + digits[..., EXPERTS : 2 * EXPERTS]
        routed = jnp.swapaxes((ranked_all <= pair_count).astype(F32), 1, 2)
        rank_own = jnp.sum(jnp.where(expert_ids == expert, ranked_all, 0), axis=-1)
        earlier = (rank_own[:, None, :] < rank_own[:, :, None]).astype(jnp.int32)
        slot = jnp.where(rank_own <= pair_count, jnp.sum(earlier, axis=-1), capacity)
        return slot, routed

    key_value = jnp.concatenate(pieces, axis=0)
    span = ATTEND_SPAN + own_rows
    segment_ext = lax.dynamic_slice_in_dim(segment_near, tensor_index * own_rows, span)
    view = (
        jnp.reshape(own_start, (1,)),
        segment_ext[:, None],
        segment_ext[None, ATTEND_SPAN:],
        queries,
        key_value,
    )
    heads_low, log_total = attention(*view, seq_len)
    heads_late, output_parts, cotangent_parts = lax.optimization_barrier(
        (heads_low, output_parts, cotangent_parts)
    )
    output_near = plane_stack(output_parts)
    output_far = swap(output_near, "core")
    output_full, expert_full[1] = lax.optimization_barrier(
        (whole_weight(output_near, output_far), expert_full[1])
    )
    hidden_state = input_wide + dot(heads_low, output_full, ((1,), (1,)))
    second_factor = norm_factor(hidden_state)
    normed_mid_own = (hidden_state * second_factor * second_gain).astype(BF16)

    cotangent_near = plane_stack(cotangent_parts)
    cotangent_far = swap(cotangent_near, "core")
    near_slots, far_slots = slots_of(cotangent_near), slots_of(cotangent_far)
    normed_parts, near_slots, far_slots, expert_full[2] = lax.optimization_barrier(
        (plane_parts(normed_mid_own), near_slots, far_slots, expert_full[2])
    )
    normed_near = plane_stack(normed_parts)
    normed_far = swap(normed_near, "core")
    own_expert = (expert_ids == expert).astype(F32)[:, None]
    router_t = router_weight.T

    def experts_on(tokens, cotangents, slots):
        slot, routed = slots
        return expert_groups(
            slot,
            routed,
            own_expert,
            router_t,
            tokens.reshape(2, group_rows, width),
            cotangents.reshape(2, group_rows, -1),
            expert_full,
            capacity,
        )

    on_near = experts_on(normed_near, cotangent_near, near_slots)
    on_far = experts_on(normed_far, cotangent_far, far_slots)
    blocks = (2 * halves, own_rows, width)
    (grad_near, moe_near), (grad_far, moe_far) = (
        [array.reshape(blocks) for array in side[:2]] for side in (on_near, on_far)
    )
    grad_blocks = fold_blocks(grad_near, swap(grad_far, "core"))
    grad_blocks, moe_far, on_near, on_far = lax.optimization_barrier(
        (grad_blocks, moe_far, on_near[2:], on_far[2:])
    )
    grad_mid_parts = fold_plane(grad_blocks)
    expert_part, *moe_blocks = weight_grads(
        on_near, on_far, moe_near, swap(moe_far, "core"), halves
    )
    expert_sum = lax.psum_scatter(expert_part, "outer", scatter_dimension=0, tiled=True)
    grad_mid_parts, moe_blocks = lax.optimization_barrier((grad_mid_parts, moe_blocks))
    moe_parts = fold_plane(moe_blocks)
    grad_mid = wide_sum(grad_mid_parts)

    norm_input_part = norm_back(hidden_state, second_factor, second_gain, grad_mid)
    grad_state = cotangent.astype(F32) + norm_input_part
    grad_attn = grad_state.astype(BF16)
    grad_heads = dot(grad_attn, output_full, ((1,), (0,))).astype(BF16)
    output_total = fold_columns(grad_attn, heads_late, shard_rows)
    grad_query_pre, grad_far_kv, grad_own = attention_back(
        *view, log_total, grad_heads, cosine, sine, seq_len
    )
    grad_query_pre, output_total, moe_parts = lax.optimization_barrier(
        (grad_query_pre, output_total, moe_parts)
    )
    output_parts = fold_plane(distance_blocks(output_total))
    query_total = fold_columns(normed_in, grad_query_pre, shard_rows)
    two_back, pair_old, one_back, pair_new = grad_far_kv.reshape(reach, own_rows, -1)
    pair_got, output_parts, query_total = lax.optimization_barrier(
        (swap(jnp.stack([pair_old, pair_new]), "tensor"), output_parts, query_total)
    )
    query_parts = fold_plane(distance_blocks(query_total))
    pair_old, pair_new = pair_got.astype(F32)
    one_back = one_back.astype(F32) + jnp.where(first, pair_old, pair_new)
    two_back = two_back.astype(F32) + jnp.where(first, 0.0, pair_old)
    grad_own = grad_own + jnp.where(first, pair_new, 0.0)
    grad_own = grad_own + shift_groups(one_back.astype(BF16), -1).astype(F32)
    grad_own = grad_own + shift_groups(two_back.astype(BF16), -2).astype(F32)
    query_parts, output_parts = lax.optimization_barrier((query_parts, output_parts))
    output_weight_grad = outer_scatter(wide_sum(output_parts).astype(BF16))
    grad_key_value = []
    for half in range(halves):
        start = half * 2 * HEAD_SIZE
        key_part = grad_own[:, start : start + HEAD_SIZE]
        turned = jnp.concatenate(
            [key_part[:, HEAD_SIZE // 2 :], key_part[:, : HEAD_SIZE // 2]], axis=1
        )
        grad_key_value.append(key_part * cosine - turned * sine)
        grad_key_value.append(grad_own[:, start + HEAD_SIZE : start + 2 * HEAD_SIZE])
    grad_key_value_pre = jnp.concatenate(grad_key_value, axis=1).astype(BF16)
    key_value_total = fold_columns(normed_in, grad_key_value_pre, shard_rows)
    key_value_parts = fold_plane(distance_blocks(key_value_total))
    grad_in = dot(grad_query_pre, query_full, ((1,), (1,))) + dot(
        grad_key_value_pre, key_value_full, ((1,), (1,))
    )
    grad_in, expert_sum = lax.optimization_barrier((grad_in, expert_sum))
    input_grad = grad_state + norm_back(input_wide, first_factor, first_gain, grad_in)
    qkv_grad = outer_scatter(
        jnp.concatenate([wide_sum(query_parts), wide_sum(key_value_parts)], axis=2).astype(BF16)
    )
    block_output = hidden_state + wide_sum(moe_parts)
    expert_sum = expert_sum.reshape(groups, shard_rows, halves, -1)
    expert_sum = jnp.swapaxes(expert_sum, 1, 2).reshape(plane, shard_rows, -1)
    expert_sum = lax.all_to_all(expert_sum, PLANE, 0, 0, tiled=True)
    gate_grad, up_grad, down_grad = (
        jnp.swapaxes(expert_sum[:, :, at * half_ff : (at + 1) * half_ff], 0, 1).astype(F32)
        for at in range(3)
    )
    router_grad = jnp.sum(expert_sum[:, :, 3 * half_ff : 3 * half_ff + EXPERTS].astype(F32), axis=0)
    router_grad = lax.dynamic_slice_in_dim(
        router_grad, tensor_index * (shard_rows // 2), shard_rows // 2, 0
    )
    query_grad = qkv_grad[:, :query_columns]
    key_grad = qkv_grad[:, query_columns : query_columns + HEAD_SIZE]
    value_grad = qkv_grad[:, query_columns + HEAD_SIZE :]

    half_rows = shard_rows // 2
    own_gains = lax.dynamic_slice_in_dim(
        norm_gains, lax.axis_index(DP) * shard_rows, shard_rows, 0
    )
    qkv_own = jnp.concatenate([query_matrix, key_value_weight], axis=1)
    first_sum = jnp.sum(qkv_grad * qkv_own.astype(F32), axis=-1)
    second_sum = jnp.sum(
        gate_grad * gate_weight.astype(F32) + up_grad * up_weight.astype(F32), axis=(1, 2)
    )
    gain_sums = jnp.stack([first_sum, second_sum], axis=1) / own_gains
    kept = lax.dynamic_slice_in_dim(gain_sums, tensor_index * half_rows, half_rows, 0)
    sent = lax.dynamic_slice_in_dim(gain_sums, (1 - tensor_index) * half_rows, half_rows, 0)
    own_router = lax.dynamic_slice_in_dim(
        router_weight, lax.axis_index(ALL) * half_rows, half_rows, 0
    )
    router_sum = jnp.sum(router_grad * own_router.astype(F32), axis=-1)
    half_gains = lax.dynamic_slice_in_dim(own_gains, tensor_index * half_rows, half_rows, 0)
    router_sum = router_sum / half_gains[:, 1]
    gains_grad = (
        kept
        + swap(sent, "tensor")
        + jnp.stack([jnp.zeros_like(router_sum), router_sum], axis=1)
    )
    return (
        block_output,
        input_grad,
        gains_grad,
        router_grad,
        query_grad,
        key_grad,
        value_grad,
        output_weight_grad,
        gate_grad,
        up_grad,
        down_grad,
    )


def solution(mesh):
    dp_size, tensor_size = mesh.shape["dp"], mesh.shape["tensor"]
    split = Mesh(mesh.devices.reshape(dp_size // 4, 2, 2, tensor_size), ALL)
    return jax.shard_map(
        on_device,
        mesh=split,
        in_specs=(
            P(ALL, None),
            P(),
            P(),
            P(DP, "tensor"),
            P(DP, "tensor"),
            P(DP, "tensor"),
            P(DP, "tensor"),
            P(DP, None, "tensor"),
            P(DP, None, "tensor"),
            P(DP, None, "tensor"),
            P(DP),
            P(DP, None),
            P(DP),
            P(ALL, None),
        ),
        out_specs=(
            P(ALL, None),
            P(ALL, None),
            P(ALL, None),
            P(ALL, None),
            P(DP, "tensor"),
            P(DP, "tensor"),
            P(DP, "tensor"),
            P(DP, "tensor"),
            P(DP, None, "tensor"),
            P(DP, None, "tensor"),
            P(DP, None, "tensor"),
        ),
        check_vma=False,
    )
```

profile of v0, /device:TPU:0, one launch (start us, length us, event | category | flops | bytes accessed | tf_op | source)
XLA Modules:
  0.0 568.8 jit_solution(14730813831825136683)
XLA Ops:
  8.8 3.0 collective-permute-start
  15.6 2.1 collective-permute-start.1
  17.7 2.6 collective-permute-start.2
  24.4 3.7 all-to-all-start
  31.2 13.8 %collective-permute-done.2 = bf16[96,2048]{1,0:T(8,128)(2,1)} collective-permute-done((bf16[96,2048]{1,0:T(8,128)(2,1)}, bf16[96,2048]{1,0:T(8,128)(2,1)}, u32[]{:S(2)}, u32[]{:S(2)}) %collective-permute-start.2) | collective-permute-done | bytes 393248 | tf_op jit(solution)/shard_map/ppermute | solution.py:89
  47.0 3.3 all-to-all-done
  64.7 2.8 collective-permute-done.7
  67.7 8.0 %scatter_custom_fusion = s32[2048]{0:T(1024)S(1)} fusion(s32[2048]{0:T(1024)S(1)} %compare_select_fusion.1, s32[2048]{0:T(1024)S(1)} %iota.24, s32[]{:T(128)} %constant.894.clone.1), kind=kCustom, calls=%fused_computation.211 | custom fusion | bytes 8196 | tf_op jit(solution)/shard_map/scatter | solution.py:679
  76.4 5.5 collective-permute-start.11
  84.4 3.1 project.2
  87.4 4.6 collective-permute-start.9
  92.1 4.3 collective-permute-start.10
  98.1 5.4 collective-permute-done.10
  103.5 4.9 all-gather.7.cloned.1.call-done
  113.3 6.3 %collective-permute-start.16 = (bf16[4,96,768]{2,1,0:T(8,128)(2,1)}, bf16[4,96,768]{2,1,0:T(8,128)(2,1)}, u32[]{:S(2)}, u32[]{:S(2)}) collective-permute-start(bf16[4,96,768]{2,1,0:T(8,128)(2,1)} %get-tuple-element.146), channel_id=1, source_target_pairs={{0,4},{4,0},{1,5},{5,1},{2,6},{6,2},{3,7},{7,3},{8,12},{12,8},{9,1... | collective-permute-start | bytes 1769480 | tf_op jit(solution)/shard_map/ppermute | solution.py:34
  126.3 6.3 %collective-permute-start.19 = (bf16[256,1664]{1,0:T(8,128)(2,1)}, bf16[256,1664]{1,0:T(8,128)(2,1)}, u32[]{:S(2)}, u32[]{:S(2)}) collective-permute-start(bf16[256,1664]{1,0:T(8,128)(2,1)} %fusion.8), channel_id=1, source_target_pairs={{0,4},{4,0},{1,5},{5,1},{2,6},{6,2},{3,7},{7,3},{8,12},{12,8},{9,1... | collective-permute-start | bytes 2555912 | tf_op jit(solution)/shard_map/ppermute | solution.py:34
  133.6 2.0 broadcast_select_fusion.3
  135.9 2.5 maximum_maximum_fusion
  139.0 7.2 %collective-permute-start.17 = (bf16[4,96,768]{2,1,0:T(8,128)(2,1)S(1)}, bf16[4,96,768]{2,1,0:T(8,128)(2,1)S(1)}, u32[]{:S(2)}, u32[]{:S(2)}) collective-permute-start(bf16[4,96,768]{2,1,0:T(8,128)(2,1)S(1)} %copy-done.12), channel_id=1, source_target_pairs={{0,5},{1,4},{4,1},{5,0},{2,7},{3,6},{6,3},{7,2},{8,13},{9,12},{12,... | collective-permute-start | bytes 1769480 | tf_op jit(solution)/shard_map/ppermute | solution.py:34
  147.9 6.6 %project.3.q_ref = bf16[256,1536]{1,0:T(8,128)(2,1)} custom-call(bf16[256,1536]{1,0:T(8,128)(2,1)} %fusion.3.rows_ref, bf16[1536,1536]{1,0:T(8,128)(2,1)} %bitcast.251, f32[256,128]{1,0:T(8,128)} %get-tuple-element.374.cosine_ref, f32[256,128]{1,0:T(8,128)} %get-tuple-element.375.sine_ref), custom_call_target="tpu_custom_call" | custom-call | flops 1000 | bytes 1000 | tf_op jit(solution)/shard_map/project/pallas_call | solution.py:193
  157.6 10.3 %attention.1 = (bf16[256,1536]{1,0:T(8,128)(2,1)}, f32[2,6,256]{2,1,0:T(8,128)}) custom-call(s32[1]{0:T(128)} %bitcast.place_ref, s32[1280,1]{1,0:T(8,128)} %broadcast_in_dim.105.segment_key_ref, s32[1,256]{1,0:T(1,128)} %bitcast.302, bf16[256,1536]{1,0:T(8,128)(2,1)} %project.3.q_ref, bf16[1280,512]{1,0:T(8,128)(2,1)} %constant_dynamic-update-slice_fusion.2.kv_ref), custom_call_target="tpu_custom_call" | custom-call | flops 1000 | bytes 1000 | tf_op jit(solution)/shard_map/attention/pallas_call | solution.py:270
  167.9 15.6 %collective-permute-done.17 = bf16[4,96,768]{2,1,0:T(8,128)(2,1)S(1)} collective-permute-done((bf16[4,96,768]{2,1,0:T(8,128)(2,1)S(1)}, bf16[4,96,768]{2,1,0:T(8,128)(2,1)S(1)}, u32[]{:S(2)}, u32[]{:S(2)}) %collective-permute-start.17) | collective-permute-done | bytes 589856 | tf_op jit(solution)/shard_map/ppermute | solution.py:34
  183.5 4.2 collective-permute-done.18
  190.0 3.4 pad_maximum_fusion
  199.1 2.0 broadcast_select_fusion.1
  201.5 2.6 maximum_maximum_fusion.1
  204.1 4.0 multiply_reduce_fusion.1
  210.7 6.2 %collective-permute-start.23 = (bf16[256,1536]{1,0:T(8,128)(2,1)}, bf16[256,1536]{1,0:T(8,128)(2,1)}, u32[]{:S(2)}, u32[]{:S(2)}) collective-permute-start(bf16[256,1536]{1,0:T(8,128)(2,1)} %multiply_convert_fusion), channel_id=1, source_target_pairs={{0,4},{4,0},{1,5},{5,1},{2,6},{6,2},{3,7},{7,3},{8,12},{12,8},{9,1... | collective-permute-start | bytes 2359304 | tf_op jit(solution)/shard_map/ppermute | solution.py:34
  223.1 23.8 %all-gather.11.cloned.1.call-done = bf16[3072,384]{1,0:T(8,128)(2,1)} async-done(((bf16[768,384]{1,0:T(8,128)(2,1)}), bf16[3072,384]{1,0:T(8,128)(2,1)}) %all-gather.11.cloned.1.call-update) | async-done | bytes 2359312 | tf_op jit(solution)/shard_map/all_gather | solution.py:694
  246.9 4.6 collective-permute-done.24
  251.6 3.3 pad_maximum_fusion.1
  257.0 3.8 collective-permute-done.26
  260.8 20.6 %expert.3 = (bf16[2,512,1536]{2,1,0:T(8,128)(2,1)}, bf16[2,512,1536]{2,1,0:T(8,128)(2,1)}, bf16[512,1536]{1,0:T(8,128)(2,1)}, bf16[512,1536]{1,0:T(8,128)(2,1)},...) custom-call(s32[2,1,512]{2,1,0:T(1,128)} %broadcast_in_dim.102.slot_row_ref,, ...), custom_call_target="tpu_custom_call" | custom-call | flops 1000 | bytes 1000 | tf_op jit(solution)/shard_map/expert/pallas_call | solution.py:500
  283.3 21.0 %expert.2 = (bf16[2,512,1536]{2,1,0:T(8,128)(2,1)}, bf16[2,512,1536]{2,1,0:T(8,128)(2,1)}, bf16[512,1536]{1,0:T(8,128)(2,1)}, bf16[512,1536]{1,0:T(8,128)(2,1)},...) custom-call(s32[2,1,512]{2,1,0:T(1,128)} %copy.126.slot_row_ref, ...), custom_call_target="tpu_custom_call" | custom-call | flops 1000 | bytes 1000 | tf_op jit(solution)/shard_map/expert/pallas_call | solution.py:500
  304.4 5.1 fusion.12
  316.4 16.7 %weight_grads.1 = (bf16[1536,2560]{1,0:T(8,128)(2,1)}, bf16[256,1536]{1,0:T(8,128)(2,1)}, bf16[256,1536]{1,0:T(8,128)(2,1)}, bf16[256,1536]{1,0:T(8,128)(2,1)}, bf16[256,1536]{1,0:T(8,128)(2,1)}) custom-call(bf16[512,1536]{1,0:T(8,128)(2,1)} %get-tuple-element.188.refs_0_, bf16[512,1536]{1,0:T(8,128)(2,1)} %get-tuple-element.189.refs_1_, ...), custom_call_target="tpu_custom_call" | custom-call | flops 15000000512 | bytes 50000000 | tf_op jit(solution)/shard_map/weight_grads/pallas_call | solution.py:600
  333.1 2.0 collective-permute-done.29
  335.1 15.7 %collective-permute-done.30 = bf16[256,1536]{1,0:T(8,128)(2,1)} collective-permute-done((bf16[256,1536]{1,0:T(8,128)(2,1)}, bf16[256,1536]{1,0:T(8,128)(2,1)}, u32[]{:S(2)}, u32[]{:S(2)}) %collective-permute-start.30) | collective-permute-done | bytes 786464 | tf_op jit(solution)/shard_map/ppermute | solution.py:34
  350.8 2.3 multiply_reduce_fusion
  353.2 3.8 fusion.52
  357.9 2.3 convolution_convert_fusion.4.dout_ref
  363.7 3.2 convolution_convert_fusion.2
  370.3 17.7 %attention_back.1 = (bf16[256,1536]{1,0:T(8,128)(2,1)}, bf16[1024,512]{1,0:T(8,128)(2,1)}, f32[256,512]{1,0:T(8,128)}) custom-call(s32[1]{0:T(128)} %bitcast.place_ref, s32[1280,1]{1,0:T(8,128)} %broadcast_in_dim.105.segment_key_ref, s32[1,256]{1,0:T(1,128)} %bitcast.303, bf16[256,1536]{1,0:T(8,128)(2,1)} %project.3.q_ref, ...), custom_call_target="tpu_custom_call" | custom-call | flops 70000001024 | bytes 10000000 | tf_op jit(solution)/shard_map/attention_back/pallas_call | solution.py:359
  388.9 3.8 add_convert_fusion.1
  392.6 12.5 %collective-permute-done.35 = bf16[256,1536]{1,0:T(8,128)(2,1)} collective-permute-done((bf16[256,1536]{1,0:T(8,128)(2,1)}, bf16[256,1536]{1,0:T(8,128)(2,1)}, u32[]{:S(2)}, u32[]{:S(2)}) %collective-permute-start.35) | collective-permute-done | bytes 786464 | tf_op jit(solution)/shard_map/ppermute | solution.py:34
  405.1 2.2 convolution_convert_fusion
  411.6 2.8 dynamic-slice_bitcast_fusion.4
  418.8 2.3 add_convert_fusion
  421.1 3.8 collective-permute-done.36
  424.8 24.9 %collective-permute-done.37 = bf16[4,96,768]{2,1,0:T(8,128)(2,1)S(1)} collective-permute-done((bf16[4,96,768]{2,1,0:T(8,128)(2,1)S(1)}, bf16[4,96,768]{2,1,0:T(8,128)(2,1)S(1)}, u32[]{:S(2)}, u32[]{:S(2)}) %collective-permute-start.37) | collective-permute-done | bytes 589856 | tf_op jit(solution)/shard_map/ppermute | solution.py:34
  452.7 3.4 add_add_fusion
  458.8 3.3 collective-permute-start.44
  466.1 2.6 convolution_add_fusion
  468.6 4.7 collective-permute-done.43
  473.3 6.8 %collective-permute-done.44 = bf16[4,96,768]{2,1,0:T(8,128)(2,1)S(1)} collective-permute-done((bf16[4,96,768]{2,1,0:T(8,128)(2,1)S(1)}, bf16[4,96,768]{2,1,0:T(8,128)(2,1)S(1)}, u32[]{:S(2)}, u32[]{:S(2)}) %collective-permute-start.44) | collective-permute-done | bytes 589856 | tf_op jit(solution)/shard_map/ppermute | solution.py:34
  480.1 13.4 %collective-permute-done.45 = bf16[4,96,768]{2,1,0:T(8,128)(2,1)S(1)} collective-permute-done((bf16[4,96,768]{2,1,0:T(8,128)(2,1)S(1)}, bf16[4,96,768]{2,1,0:T(8,128)(2,1)S(1)}, u32[]{:S(2)}, u32[]{:S(2)}) %collective-permute-start.45) | collective-permute-done | bytes 589856 | tf_op jit(solution)/shard_map/ppermute | solution.py:34
  495.3 4.1 collective-permute-start.55
  500.0 6.0 %collective-permute-start.49 = (bf16[4,96,256]{2,1,0:T(8,128)(2,1)S(1)}, bf16[4,96,256]{2,1,0:T(8,128)(2,1)S(1)}, u32[]{:S(2)}, u32[]{:S(2)}) collective-permute-start(bf16[4,96,256]{2,1,0:T(8,128)(2,1)S(1)} %get-tuple-element.336), channel_id=1, source_target_pairs={{0,5},{1,4},{4,1},{5,0},{2,7},{3,6},{6,3},{7,2},{8,13},{9,12},{12,... | collective-permute-start | bytes 589832 | tf_op jit(solution)/shard_map/ppermute | solution.py:34
  507.0 4.8 collective-permute-done.49
  511.8 2.3 collective-permute-done.48
  517.0 4.5 reshape.345
  523.0 4.1 all-to-all-start.1
  530.2 7.6 %collective-permute-done.51 = bf16[96,1024]{1,0:T(8,128)(2,1)S(1)} collective-permute-done((bf16[96,1024]{1,0:T(8,128)(2,1)}, bf16[96,1024]{1,0:T(8,128)(2,1)S(1)}, u32[]{:S(2)}, u32[]{:S(2)}) %collective-permute-start.51) | collective-permute-done | bytes 196640 | tf_op jit(solution)/shard_map/ppermute | solution.py:89
  542.3 9.2 %all-to-all-done.1 = bf16[8,96,1280]{2,1,0:T(8,128)(2,1)S(1)} async-done(((bf16[8,96,1280]{2,1,0:T(8,128)(2,1)}), bf16[8,96,1280]{2,1,0:T(8,128)(2,1)S(1)}, u32[]{:S(2)}, u32[]{:S(2)}) %all-to-all-start.1) | async-done | bytes 1966112 | tf_op jit(solution)/shard_map/all_to_all | solution.py:861
  (321 shorter events, 132.6 us)
Async XLA Ops:
  8.8 5.0 collective-permute-start
  12.6 41.7 %copy-start.33 = (f32[1536]{0:T(1024)}, f32[1536]{0:T(1024)S(1)}, u32[]{:S(2)}) copy-start(f32[1536]{0:T(1024)S(1)} %get-tuple-element.275) | copy-start | bytes 18436
  15.6 14.6 %collective-permute-start.1 = (bf16[96,2048]{1,0:T(8,128)(2,1)}, bf16[96,2048]{1,0:T(8,128)(2,1)}, u32[]{:S(2)}, u32[]{:S(2)}) collective-permute-start(bf16[96,2048]{1,0:T(8,128)(2,1)} %pad_maximum_fusion.7), channel_id=1, source_target_pairs={{0,8},{8,16},{16,24},{24,0},{1,9},{9,17},{17,25},{25,1},{2,10},{10... | collective-permute-start | bytes 1179656 | tf_op jit(solution)/shard_map/ppermute | solution.py:89
  17.7 27.3 %collective-permute-start.2 = (bf16[96,2048]{1,0:T(8,128)(2,1)}, bf16[96,2048]{1,0:T(8,128)(2,1)}, u32[]{:S(2)}, u32[]{:S(2)}) collective-permute-start(bf16[96,2048]{1,0:T(8,128)(2,1)} %pad_maximum_fusion.7), channel_id=1, source_target_pairs={{0,16},{8,24},{16,0},{24,8},{1,17},{9,25},{17,1},{25,9},{2,18},{10... | collective-permute-start | bytes 1179656 | tf_op jit(solution)/shard_map/ppermute | solution.py:89
  20.3 25.7 %collective-permute-start.3 = (bf16[96,2048]{1,0:T(8,128)(2,1)}, bf16[96,2048]{1,0:T(8,128)(2,1)}, u32[]{:S(2)}, u32[]{:S(2)}) collective-permute-start(bf16[96,2048]{1,0:T(8,128)(2,1)} %pad_maximum_fusion.7), channel_id=1, source_target_pairs={{0,24},{8,0},{16,8},{24,16},{1,25},{9,1},{17,9},{25,17},{2,26},{10... | collective-permute-start | bytes 1179656 | tf_op jit(solution)/shard_map/ppermute | solution.py:89
  24.4 26.0 %all-to-all-start = ((bf16[8,3,96,384]{3,2,1,0:T(8,128)(2,1)}), bf16[8,3,96,384]{3,2,1,0:T(8,128)(2,1)S(1)}, u32[]{:S(2)}, u32[]{:S(2)}) async-start(bf16[8,3,96,384]{3,2,1,0:T(8,128)(2,1)} %maximum_bitcast_fusion), calls=%async_computation | async-start | bytes 3538944 | tf_op jit(solution)/shard_map/all_to_all | solution.py:667
  28.1 80.2 %all-gather.7.cloned.1.call-start = ((), (), s32[]{:S(2)}) async-start(), calls=%async_computation.4 | async-start | bytes 2949120 | tf_op jit(solution)/shard_map/all_gather | solution.py:694
  53.4 150.6 %all-gather.9.cloned.1.call-start = ((), (), s32[]{:S(2)}) async-start(), calls=%async_computation.5 | async-start | bytes 2949120 | tf_op jit(solution)/shard_map/all_gather | solution.py:694
  55.4 12.0 %collective-permute-start.7 = (bf16[4,96,512]{2,1,0:T(8,128)(2,1)S(1)}, bf16[4,96,512]{2,1,0:T(8,128)(2,1)S(1)}, u32[]{:S(2)}, u32[]{:S(2)}) collective-permute-start(bf16[4,96,512]{2,1,0:T(8,128)(2,1)S(1)} %slice.138), channel_id=1, source_target_pairs={{0,4},{4,0},{1,5},{5,1},{2,6},{6,2},{3,7},{7,3},{8,12},{12,8},{9,1... | collective-permute-start | bytes 1179656 | tf_op jit(solution)/shard_map/ppermute | solution.py:34
  59.4 38.7 %collective-permute-start.4 = (bf16[4,96,768]{2,1,0:T(8,128)(2,1)}, bf16[4,96,768]{2,1,0:T(8,128)(2,1)}, u32[]{:S(2)}, u32[]{:S(2)}) collective-permute-start(bf16[4,96,768]{2,1,0:T(8,128)(2,1)} %get-tuple-element.136), channel_id=1, source_target_pairs={{0,1},{1,0},{2,3},{3,2},{4,5},{5,4},{6,7},{7,6},{8,9},{9,8},{10,11... | collective-permute-start | bytes 1769480 | tf_op jit(solution)/shard_map/ppermute | solution.py:34
  60.1 38.0 %collective-permute-start.5 = (bf16[4,96,768]{2,1,0:T(8,128)(2,1)}, bf16[4,96,768]{2,1,0:T(8,128)(2,1)}, u32[]{:S(2)}, u32[]{:S(2)}) collective-permute-start(bf16[4,96,768]{2,1,0:T(8,128)(2,1)} %get-tuple-element.136), channel_id=1, source_target_pairs={{0,4},{4,0},{1,5},{5,1},{2,6},{6,2},{3,7},{7,3},{8,12},{12,8},{9,1... | collective-permute-start | bytes 1769480 | tf_op jit(solution)/shard_map/ppermute | solution.py:34
  61.5 36.5 %collective-permute-start.6 = (bf16[4,96,768]{2,1,0:T(8,128)(2,1)}, bf16[4,96,768]{2,1,0:T(8,128)(2,1)}, u32[]{:S(2)}, u32[]{:S(2)}) collective-permute-start(bf16[4,96,768]{2,1,0:T(8,128)(2,1)} %get-tuple-element.136), channel_id=1, source_target_pairs={{0,5},{1,4},{4,1},{5,0},{2,7},{3,6},{6,3},{7,2},{8,13},{9,12},{12,... | collective-permute-start | bytes 1769480 | tf_op jit(solution)/shard_map/ppermute | solution.py:34
  62.8 24.6 %collective-permute-start.12 = (s32[512]{0:T(512)}, s32[512]{0:T(512)}, u32[]{:S(2)}, u32[]{:S(2)}) collective-permute-start(s32[512]{0:T(512)} %param.24), channel_id=1, source_target_pairs={{0,2},{2,4},{4,6},{6,8},{8,10},{10,12},{12,14},{14,16},{16,18},{18... | collective-permute-start | bytes 6152 | tf_op jit(solution)/shard_map/ppermute | solution.py:29
  67.6 8.8 %collective-permute-start.8 = (bf16[4,2,96,512]{3,2,1,0:T(8,128)(2,1)S(1)}, bf16[4,2,96,512]{3,2,1,0:T(8,128)(2,1)}, u32[]{:S(2)}, u32[]{:S(2)}) collective-permute-start(bf16[4,2,96,512]{3,2,1,0:T(8,128)(2,1)S(1)} %pad_maximum_fusion.5), channel_id=1, source_target_pairs={{0,2},{2,0},{1,3},{3,1},{4,6},{6,4},{5,7},{7,5},{8,10},{10,8},{9,1... | collective-permute-start | bytes 2359304 | tf_op jit(solution)/shard_map/ppermute | solution.py:34
  76.4 15.7 %collective-permute-start.11 = (s32[512]{0:T(512)}, s32[512]{0:T(512)S(1)}, u32[]{:S(2)}, u32[]{:S(2)}) collective-permute-start(s32[512]{0:T(512)} %param.24), channel_id=1, source_target_pairs={{0,4},{2,6},{4,8},{6,10},{8,12},{10,14},{12,16},{14,18},{16,20},{1... | collective-permute-start | bytes 6152 | tf_op jit(solution)/shard_map/ppermute | solution.py:29
  87.4 10.6 %collective-permute-start.9 = (bf16[256,512]{1,0:T(8,128)(2,1)}, bf16[256,512]{1,0:T(8,128)(2,1)S(1)}, u32[]{:S(2)}, u32[]{:S(2)}) collective-permute-start(bf16[256,512]{1,0:T(8,128)(2,1)} %project.2), channel_id=1, source_target_pairs={{0,2},{2,4},{4,6},{6,8},{8,10},{10,12},{12,14},{14,16},{16,18},{18... | collective-permute-start | bytes 786440 | tf_op jit(solution)/shard_map/ppermute | solution.py:29
  92.1 11.4 %collective-permute-start.10 = (bf16[256,512]{1,0:T(8,128)(2,1)}, bf16[256,512]{1,0:T(8,128)(2,1)S(1)}, u32[]{:S(2)}, u32[]{:S(2)}) collective-permute-start(bf16[256,512]{1,0:T(8,128)(2,1)} %project.2), channel_id=1, source_target_pairs={{0,4},{2,6},{4,8},{6,10},{8,12},{10,14},{12,16},{14,18},{16,20},{1... | collective-permute-start | bytes 786440 | tf_op jit(solution)/shard_map/ppermute | solution.py:29
  110.3 22.4 %collective-permute-start.13 = (bf16[2,2,4,96,768]{4,3,2,1,0:T(8,128)(2,1)S(1)}, bf16[2,2,4,96,768]{4,3,2,1,0:T(8,128)(2,1)}, u32[]{:S(2)}, u32[]{:S(2)}) collective-permute-start(bf16[2,2,4,96,768]{4,3,2,1,0:T(8,128)(2,1)S(1)} %bitcast.265), channel_id=1, source_target_pairs={{0,2},{2,0},{1,3},{3,1},{4,6},{6,4},{5,7},{7,5},{8,10},{10,8},{9,1... | collective-permute-start | bytes 7077896 | tf_op jit(solution)/shard_map/ppermute | solution.py:34
  111.3 15.0 %collective-permute-start.14 = (bf16[2,256,512]{2,1,0:T(8,128)(2,1)}, bf16[2,256,512]{2,1,0:T(8,128)(2,1)}, u32[]{:S(2)}, u32[]{:S(2)}) collective-permute-start(bf16[2,256,512]{2,1,0:T(8,128)(2,1)} %maximum_select_fusion), channel_id=1, source_target_pairs={{0,1},{1,0},{2,3},{3,2},{4,5},{5,4},{6,7},{7,6},{8,9},{9,8},{10,11... | collective-permute-start | bytes 1572872 | tf_op jit(solution)/shard_map/ppermute | solution.py:34
  112.8 26.2 %collective-permute-start.15 = (bf16[4,96,768]{2,1,0:T(8,128)(2,1)}, bf16[4,96,768]{2,1,0:T(8,128)(2,1)}, u32[]{:S(2)}, u32[]{:S(2)}) collective-permute-start(bf16[4,96,768]{2,1,0:T(8,128)(2,1)} %get-tuple-element.146), channel_id=1, source_target_pairs={{0,1},{1,0},{2,3},{3,2},{4,5},{5,4},{6,7},{7,6},{8,9},{9,8},{10,11... | collective-permute-start | bytes 1769480 | tf_op jit(solution)/shard_map/ppermute | solution.py:34
  113.3 54.6 %collective-permute-start.16 = (bf16[4,96,768]{2,1,0:T(8,128)(2,1)}, bf16[4,96,768]{2,1,0:T(8,128)(2,1)}, u32[]{:S(2)}, u32[]{:S(2)}) collective-permute-start(bf16[4,96,768]{2,1,0:T(8,128)(2,1)} %get-tuple-element.146), channel_id=1, source_target_pairs={{0,4},{4,0},{1,5},{5,1},{2,6},{6,2},{3,7},{7,3},{8,12},{12,8},{9,1... | collective-permute-start | bytes 1769480 | tf_op jit(solution)/shard_map/ppermute | solution.py:34
  119.7 127.2 %all-gather.11.cloned.1.call-start = ((), (), s32[]{:S(2)}) async-start(), calls=%async_computation.6 | async-start | bytes 2949120 | tf_op jit(solution)/shard_map/all_gather | solution.py:694
  121.7 66.0 %collective-permute-start.18 = (bf16[256,1664]{1,0:T(8,128)(2,1)}, bf16[256,1664]{1,0:T(8,128)(2,1)}, u32[]{:S(2)}, u32[]{:S(2)}) collective-permute-start(bf16[256,1664]{1,0:T(8,128)(2,1)} %fusion.8), channel_id=1, source_target_pairs={{0,1},{1,0},{2,3},{3,2},{4,5},{5,4},{6,7},{7,6},{8,9},{9,8},{10,11... | collective-permute-start | bytes 2555912 | tf_op jit(solution)/shard_map/ppermute | solution.py:34
  126.3 61.4 %collective-permute-start.19 = (bf16[256,1664]{1,0:T(8,128)(2,1)}, bf16[256,1664]{1,0:T(8,128)(2,1)}, u32[]{:S(2)}, u32[]{:S(2)}) collective-permute-start(bf16[256,1664]{1,0:T(8,128)(2,1)} %fusion.8), channel_id=1, source_target_pairs={{0,4},{4,0},{1,5},{5,1},{2,6},{6,2},{3,7},{7,3},{8,12},{12,8},{9,1... | collective-permute-start | bytes 2555912 | tf_op jit(solution)/shard_map/ppermute | solution.py:34
  132.7 55.0 %collective-permute-start.20 = (bf16[256,1664]{1,0:T(8,128)(2,1)}, bf16[256,1664]{1,0:T(8,128)(2,1)}, u32[]{:S(2)}, u32[]{:S(2)}) collective-permute-start(bf16[256,1664]{1,0:T(8,128)(2,1)} %fusion.8), channel_id=1, source_target_pairs={{0,5},{1,4},{4,1},{5,0},{2,7},{3,6},{6,3},{7,2},{8,13},{9,12},{12,... | collective-permute-start | bytes 2555912 | tf_op jit(solution)/shard_map/ppermute | solution.py:34
  139.0 44.5 %collective-permute-start.17 = (bf16[4,96,768]{2,1,0:T(8,128)(2,1)S(1)}, bf16[4,96,768]{2,1,0:T(8,128)(2,1)S(1)}, u32[]{:S(2)}, u32[]{:S(2)}) collective-permute-start(bf16[4,96,768]{2,1,0:T(8,128)(2,1)S(1)} %copy-done.12), channel_id=1, source_target_pairs={{0,5},{1,4},{4,1},{5,0},{2,7},{3,6},{6,3},{7,2},{8,13},{9,12},{12,... | collective-permute-start | bytes 1769480 | tf_op jit(solution)/shard_map/ppermute | solution.py:34
  189.6 9.5 %collective-permute-start.21 = (bf16[2,2,4,96,768]{4,3,2,1,0:T(8,128)(2,1)S(1)}, bf16[2,2,4,96,768]{4,3,2,1,0:T(8,128)(2,1)}, u32[]{:S(2)}, u32[]{:S(2)}) collective-permute-start(bf16[2,2,4,96,768]{4,3,2,1,0:T(8,128)(2,1)S(1)} %bitcast.267), channel_id=1, source_target_pairs={{0,2},{2,0},{1,3},{3,1},{4,6},{6,4},{5,7},{7,5},{8,10},{10,8},{9,1... | collective-permute-start | bytes 7077896 | tf_op jit(solution)/shard_map/ppermute | solution.py:34
  189.7 327.3 %reduce-scatter.2.cloned.1.call-start = ((), (), s32[]{:S(2)}) async-start(), calls=%async_computation.3 | async-start | bytes 9830400 | tf_op jit(solution)/shard_map/reduce_scatter | solution.py:807
  193.4 23.5 %collective-permute-start.25 = (bf16[2,2,256,1664]{3,2,1,0:T(8,128)(2,1)}, bf16[2,2,256,1664]{3,2,1,0:T(8,128)(2,1)}, u32[]{:S(2)}, u32[]{:S(2)}) collective-permute-start(bf16[2,2,256,1664]{3,2,1,0:T(8,128)(2,1)} %bitcast.66), channel_id=1, source_target_pairs={{0,2},{2,0},{1,3},{3,1},{4,6},{6,4},{5,7},{7,5},{8,10},{10,8},{9,1... | collective-permute-start | bytes 10223624 | tf_op jit(solution)/shard_map/ppermute | solution.py:34
  209.2 37.7 %collective-permute-start.22 = (bf16[256,1536]{1,0:T(8,128)(2,1)}, bf16[256,1536]{1,0:T(8,128)(2,1)}, u32[]{:S(2)}, u32[]{:S(2)}) collective-permute-start(bf16[256,1536]{1,0:T(8,128)(2,1)} %multiply_convert_fusion), channel_id=1, source_target_pairs={{0,1},{1,0},{2,3},{3,2},{4,5},{5,4},{6,7},{7,6},{8,9},{9,8},{10,11... | collective-permute-start | bytes 2359304 | tf_op jit(solution)/shard_map/ppermute | solution.py:34
  210.7 36.2 %collective-permute-start.23 = (bf16[256,1536]{1,0:T(8,128)(2,1)}, bf16[256,1536]{1,0:T(8,128)(2,1)}, u32[]{:S(2)}, u32[]{:S(2)}) collective-permute-start(bf16[256,1536]{1,0:T(8,128)(2,1)} %multiply_convert_fusion), channel_id=1, source_target_pairs={{0,4},{4,0},{1,5},{5,1},{2,6},{6,2},{3,7},{7,3},{8,12},{12,8},{9,1... | collective-permute-start | bytes 2359304 | tf_op jit(solution)/shard_map/ppermute | solution.py:34
  216.9 34.6 %collective-permute-start.24 = (bf16[256,1536]{1,0:T(8,128)(2,1)}, bf16[256,1536]{1,0:T(8,128)(2,1)}, u32[]{:S(2)}, u32[]{:S(2)}) collective-permute-start(bf16[256,1536]{1,0:T(8,128)(2,1)} %multiply_convert_fusion), channel_id=1, source_target_pairs={{0,5},{1,4},{4,1},{5,0},{2,7},{3,6},{6,3},{7,2},{8,13},{9,12},{12,... | collective-permute-start | bytes 2359304 | tf_op jit(solution)/shard_map/ppermute | solution.py:34
  254.8 6.0 %collective-permute-start.26 = (bf16[2,2,256,1536]{3,2,1,0:T(8,128)(2,1)}, bf16[2,2,256,1536]{3,2,1,0:T(8,128)(2,1)}, u32[]{:S(2)}, u32[]{:S(2)}) collective-permute-start(bf16[2,2,256,1536]{3,2,1,0:T(8,128)(2,1)} %bitcast.85), channel_id=1, source_target_pairs={{0,2},{2,0},{1,3},{3,1},{4,6},{6,4},{5,7},{7,5},{8,10},{10,8},{9,1... | collective-permute-start | bytes 9437192 | tf_op jit(solution)/shard_map/ppermute | solution.py:34
  281.4 22.9 %collective-permute-start.27 = (bf16[4,256,1536]{2,1,0:T(8,128)(2,1)}, bf16[4,256,1536]{2,1,0:T(8,128)(2,1)}, u32[]{:S(2)}, u32[]{:S(2)}) collective-permute-start(bf16[4,256,1536]{2,1,0:T(8,128)(2,1)} %bitcast.307), channel_id=1, source_target_pairs={{0,2},{2,0},{1,3},{3,1},{4,6},{6,4},{5,7},{7,5},{8,10},{10,8},{9,1... | collective-permute-start | bytes 9437192 | tf_op jit(solution)/shard_map/ppermute | solution.py:34
  309.4 7.0 %collective-permute-start.31 = (bf16[4,256,1536]{2,1,0:T(8,128)(2,1)}, bf16[4,256,1536]{2,1,0:T(8,128)(2,1)}, u32[]{:S(2)}, u32[]{:S(2)}) collective-permute-start(bf16[4,256,1536]{2,1,0:T(8,128)(2,1)} %bitcast.93), channel_id=1, source_target_pairs={{0,2},{2,0},{1,3},{3,1},{4,6},{6,4},{5,7},{7,5},{8,10},{10,8},{9,1... | collective-permute-start | bytes 9437192 | tf_op jit(solution)/shard_map/ppermute | solution.py:34
  312.9 20.2 %collective-permute-start.28 = (bf16[256,1536]{1,0:T(8,128)(2,1)}, bf16[256,1536]{1,0:T(8,128)(2,1)}, u32[]{:S(2)}, u32[]{:S(2)}) collective-permute-start(bf16[256,1536]{1,0:T(8,128)(2,1)} %get-tuple-element.185), channel_id=1, source_target_pairs={{0,1},{1,0},{2,3},{3,2},{4,5},{5,4},{6,7},{7,6},{8,9},{9,8},{10,11... | collective-permute-start | bytes 2359304 | tf_op jit(solution)/shard_map/ppermute | solution.py:34
  314.4 20.7 %collective-permute-start.29 = (bf16[256,1536]{1,0:T(8,128)(2,1)}, bf16[256,1536]{1,0:T(8,128)(2,1)}, u32[]{:S(2)}, u32[]{:S(2)}) collective-permute-start(bf16[256,1536]{1,0:T(8,128)(2,1)} %get-tuple-element.186), channel_id=1, source_target_pairs={{0,4},{4,0},{1,5},{5,1},{2,6},{6,2},{3,7},{7,3},{8,12},{12,8},{9,1... | collective-permute-start | bytes 2359304 | tf_op jit(solution)/shard_map/ppermute | solution.py:34
  316.1 34.7 %collective-permute-start.30 = (bf16[256,1536]{1,0:T(8,128)(2,1)}, bf16[256,1536]{1,0:T(8,128)(2,1)}, u32[]{:S(2)}, u32[]{:S(2)}) collective-permute-start(bf16[256,1536]{1,0:T(8,128)(2,1)} %get-tuple-element.187), channel_id=1, source_target_pairs={{0,5},{1,4},{4,1},{5,0},{2,7},{3,6},{6,3},{7,2},{8,13},{9,12},{12,... | collective-permute-start | bytes 2359304 | tf_op jit(solution)/shard_map/ppermute | solution.py:34
  366.8 22.0 %collective-permute-start.32 = (bf16[768,1536]{1,0:T(8,128)(2,1)}, bf16[768,1536]{1,0:T(8,128)(2,1)}, u32[]{:S(2)}, u32[]{:S(2)}) collective-permute-start(bf16[768,1536]{1,0:T(8,128)(2,1)} %convolution_convert_fusion.2), channel_id=1, source_target_pairs={{0,2},{2,0},{1,3},{3,1},{4,6},{6,4},{5,7},{7,5},{8,10},{10,8},{9,1... | collective-permute-start | bytes 7077896 | tf_op jit(solution)/shard_map/ppermute | solution.py:34
  366.8 25.8 %collective-permute-start.33 = (bf16[256,1536]{1,0:T(8,128)(2,1)}, bf16[256,1536]{1,0:T(8,128)(2,1)}, u32[]{:S(2)}, u32[]{:S(2)}) collective-permute-start(bf16[256,1536]{1,0:T(8,128)(2,1)} %get-tuple-element.213), channel_id=1, source_target_pairs={{0,1},{1,0},{2,3},{3,2},{4,5},{5,4},{6,7},{7,6},{8,9},{9,8},{10,11... | collective-permute-start | bytes 2359304 | tf_op jit(solution)/shard_map/ppermute | solution.py:34
  368.3 24.3 %collective-permute-start.34 = (bf16[256,1536]{1,0:T(8,128)(2,1)}, bf16[256,1536]{1,0:T(8,128)(2,1)}, u32[]{:S(2)}, u32[]{:S(2)}) collective-permute-start(bf16[256,1536]{1,0:T(8,128)(2,1)} %get-tuple-element.214), channel_id=1, source_target_pairs={{0,4},{4,0},{1,5},{5,1},{2,6},{6,2},{3,7},{7,3},{8,12},{12,8},{9,1... | collective-permute-start | bytes 2359304 | tf_op jit(solution)/shard_map/ppermute | solution.py:34
  370.0 35.1 %collective-permute-start.35 = (bf16[256,1536]{1,0:T(8,128)(2,1)}, bf16[256,1536]{1,0:T(8,128)(2,1)}, u32[]{:S(2)}, u32[]{:S(2)}) collective-permute-start(bf16[256,1536]{1,0:T(8,128)(2,1)} %get-tuple-element.215), channel_id=1, source_target_pairs={{0,5},{1,4},{4,1},{5,0},{2,7},{3,6},{6,3},{7,2},{8,13},{9,12},{12,... | collective-permute-start | bytes 2359304 | tf_op jit(solution)/shard_map/ppermute | solution.py:34
  407.3 11.4 %collective-permute-start.40 = (bf16[768,1536]{1,0:T(8,128)(2,1)}, bf16[768,1536]{1,0:T(8,128)(2,1)}, u32[]{:S(2)}, u32[]{:S(2)}) collective-permute-start(bf16[768,1536]{1,0:T(8,128)(2,1)} %convolution_convert_fusion), channel_id=1, source_target_pairs={{0,2},{2,0},{1,3},{3,1},{4,6},{6,4},{5,7},{7,5},{8,10},{10,8},{9,1... | collective-permute-start | bytes 7077896 | tf_op jit(solution)/shard_map/ppermute | solution.py:34
  410.1 14.8 %collective-permute-start.36 = (bf16[2,256,512]{2,1,0:T(8,128)(2,1)S(1)}, bf16[2,256,512]{2,1,0:T(8,128)(2,1)S(1)}, u32[]{:S(2)}, u32[]{:S(2)}) collective-permute-start(bf16[2,256,512]{2,1,0:T(8,128)(2,1)S(1)} %pad_maximum_fusion.6), channel_id=1, source_target_pairs={{0,1},{1,0},{2,3},{3,2},{4,5},{5,4},{6,7},{7,6},{8,9},{9,8},{10,11... | collective-permute-start | bytes 1572872 | tf_op jit(solution)/shard_map/ppermute | solution.py:34
  414.4 35.3 %collective-permute-start.37 = (bf16[4,96,768]{2,1,0:T(8,128)(2,1)S(1)}, bf16[4,96,768]{2,1,0:T(8,128)(2,1)S(1)}, u32[]{:S(2)}, u32[]{:S(2)}) collective-permute-start(bf16[4,96,768]{2,1,0:T(8,128)(2,1)S(1)} %get-tuple-element.298), channel_id=1, source_target_pairs={{0,1},{1,0},{2,3},{3,2},{4,5},{5,4},{6,7},{7,6},{8,9},{9,8},{10,11... | collective-permute-start | bytes 1769480 | tf_op jit(solution)/shard_map/ppermute | solution.py:34
  415.0 34.7 %collective-permute-start.38 = (bf16[4,96,768]{2,1,0:T(8,128)(2,1)S(1)}, bf16[4,96,768]{2,1,0:T(8,128)(2,1)S(1)}, u32[]{:S(2)}, u32[]{:S(2)}) collective-permute-start(bf16[4,96,768]{2,1,0:T(8,128)(2,1)S(1)} %get-tuple-element.297), channel_id=1, source_target_pairs={{0,4},{4,0},{1,5},{5,1},{2,6},{6,2},{3,7},{7,3},{8,12},{12,8},{9,1... | collective-permute-start | bytes 1769480 | tf_op jit(solution)/shard_map/ppermute | solution.py:34
  416.7 33.0 %collective-permute-start.39 = (bf16[4,96,768]{2,1,0:T(8,128)(2,1)S(1)}, bf16[4,96,768]{2,1,0:T(8,128)(2,1)S(1)}, u32[]{:S(2)}, u32[]{:S(2)}) collective-permute-start(bf16[4,96,768]{2,1,0:T(8,128)(2,1)S(1)} %get-tuple-element.296), channel_id=1, source_target_pairs={{0,5},{1,4},{4,1},{5,0},{2,7},{3,6},{6,3},{7,2},{8,13},{9,12},{12,... | collective-permute-start | bytes 1769480 | tf_op jit(solution)/shard_map/ppermute | solution.py:34
  450.1 12.0 %collective-permute-start.42 = (bf16[256,512]{1,0:T(8,128)(2,1)S(1)}, bf16[256,512]{1,0:T(8,128)(2,1)S(1)}, u32[]{:S(2)}, u32[]{:S(2)}) collective-permute-start(bf16[256,512]{1,0:T(8,128)(2,1)S(1)} %get-tuple-element.317), channel_id=1, source_target_pairs={{4,0},{6,2},{8,4},{10,6},{12,8},{14,10},{16,12},{18,14},{20,16},{2... | collective-permute-start | bytes 786440 | tf_op jit(solution)/shard_map/ppermute | solution.py:29
  451.4 10.7 %collective-permute-start.41 = (bf16[256,512]{1,0:T(8,128)(2,1)S(1)}, bf16[256,512]{1,0:T(8,128)(2,1)S(1)}, u32[]{:S(2)}, u32[]{:S(2)}) collective-permute-start(bf16[256,512]{1,0:T(8,128)(2,1)S(1)} %get-tuple-element.316), channel_id=1, source_target_pairs={{2,0},{4,2},{6,4},{8,6},{10,8},{12,10},{14,12},{16,14},{18,16},{20... | collective-permute-start | bytes 786440 | tf_op jit(solution)/shard_map/ppermute | solution.py:29
  457.2 16.1 %collective-permute-start.43 = (bf16[4,96,768]{2,1,0:T(8,128)(2,1)S(1)}, bf16[4,96,768]{2,1,0:T(8,128)(2,1)S(1)}, u32[]{:S(2)}, u32[]{:S(2)}) collective-permute-start(bf16[4,96,768]{2,1,0:T(8,128)(2,1)S(1)} %get-tuple-element.294), channel_id=1, source_target_pairs={{0,1},{1,0},{2,3},{3,2},{4,5},{5,4},{6,7},{7,6},{8,9},{9,8},{10,11... | collective-permute-start | bytes 1769480 | tf_op jit(solution)/shard_map/ppermute | solution.py:34
  458.8 21.4 %collective-permute-start.44 = (bf16[4,96,768]{2,1,0:T(8,128)(2,1)S(1)}, bf16[4,96,768]{2,1,0:T(8,128)(2,1)S(1)}, u32[]{:S(2)}, u32[]{:S(2)}) collective-permute-start(bf16[4,96,768]{2,1,0:T(8,128)(2,1)S(1)} %get-tuple-element.293), channel_id=1, source_target_pairs={{0,4},{4,0},{1,5},{5,1},{2,6},{6,2},{3,7},{7,3},{8,12},{12,8},{9,1... | collective-permute-start | bytes 1769480 | tf_op jit(solution)/shard_map/ppermute | solution.py:34
  462.0 31.5 %collective-permute-start.45 = (bf16[4,96,768]{2,1,0:T(8,128)(2,1)S(1)}, bf16[4,96,768]{2,1,0:T(8,128)(2,1)S(1)}, u32[]{:S(2)}, u32[]{:S(2)}) collective-permute-start(bf16[4,96,768]{2,1,0:T(8,128)(2,1)S(1)} %get-tuple-element.292), channel_id=1, source_target_pairs={{0,5},{1,4},{4,1},{5,0},{2,7},{3,6},{6,3},{7,2},{8,13},{9,12},{12,... | collective-permute-start | bytes 1769480 | tf_op jit(solution)/shard_map/ppermute | solution.py:34
  465.0 34.3 %collective-permute-start.46 = (bf16[768,512]{1,0:T(8,128)(2,1)S(1)}, bf16[768,512]{1,0:T(8,128)(2,1)S(1)}, u32[]{:S(2)}, u32[]{:S(2)}) collective-permute-start(bf16[768,512]{1,0:T(8,128)(2,1)S(1)} %convolution_convert_fusion.5), channel_id=1, source_target_pairs={{0,2},{2,0},{1,3},{3,1},{4,6},{6,4},{5,7},{7,5},{8,10},{10,8},{9,1... | collective-permute-start | bytes 2359304 | tf_op jit(solution)/shard_map/ppermute | solution.py:34
  494.6 32.4 %collective-permute-start.56 = (bf16[96,768]{1,0:T(8,128)(2,1)}, bf16[96,768]{1,0:T(8,128)(2,1)}, u32[]{:S(2)}, u32[]{:S(2)}) collective-permute-start(bf16[96,768]{1,0:T(8,128)(2,1)} %get-tuple-element.345), channel_id=1, source_target_pairs={{0,24},{8,0},{16,8},{24,16},{1,25},{9,1},{17,9},{25,17},{2,26},{10... | collective-permute-start | bytes 442376 | tf_op jit(solution)/shard_map/ppermute | solution.py:89
  495.3 33.0 %collective-permute-start.55 = (bf16[96,768]{1,0:T(8,128)(2,1)}, bf16[96,768]{1,0:T(8,128)(2,1)}, u32[]{:S(2)}, u32[]{:S(2)}) collective-permute-start(bf16[96,768]{1,0:T(8,128)(2,1)} %get-tuple-element.346), channel_id=1, source_target_pairs={{0,16},{8,24},{16,0},{24,8},{1,17},{9,25},{17,1},{25,9},{2,18},{10... | collective-permute-start | bytes 442376 | tf_op jit(solution)/shard_map/ppermute | solution.py:89
  500.0 11.8 %collective-permute-start.49 = (bf16[4,96,256]{2,1,0:T(8,128)(2,1)S(1)}, bf16[4,96,256]{2,1,0:T(8,128)(2,1)S(1)}, u32[]{:S(2)}, u32[]{:S(2)}) collective-permute-start(bf16[4,96,256]{2,1,0:T(8,128)(2,1)S(1)} %get-tuple-element.336), channel_id=1, source_target_pairs={{0,5},{1,4},{4,1},{5,0},{2,7},{3,6},{6,3},{7,2},{8,13},{9,12},{12,... | collective-permute-start | bytes 589832 | tf_op jit(solution)/shard_map/ppermute | solution.py:34
  506.0 8.1 %collective-permute-start.48 = (bf16[4,96,256]{2,1,0:T(8,128)(2,1)S(1)}, bf16[4,96,256]{2,1,0:T(8,128)(2,1)S(1)}, u32[]{:S(2)}, u32[]{:S(2)}) collective-permute-start(bf16[4,96,256]{2,1,0:T(8,128)(2,1)S(1)} %get-tuple-element.337), channel_id=1, source_target_pairs={{0,4},{4,0},{1,5},{5,1},{2,6},{6,2},{3,7},{7,3},{8,12},{12,8},{9,1... | collective-permute-start | bytes 589832 | tf_op jit(solution)/shard_map/ppermute | solution.py:34
  506.0 8.8 %collective-permute-start.47 = (bf16[4,96,256]{2,1,0:T(8,128)(2,1)S(1)}, bf16[4,96,256]{2,1,0:T(8,128)(2,1)S(1)}, u32[]{:S(2)}, u32[]{:S(2)}) collective-permute-start(bf16[4,96,256]{2,1,0:T(8,128)(2,1)S(1)} %get-tuple-element.335), channel_id=1, source_target_pairs={{0,1},{1,0},{2,3},{3,2},{4,5},{5,4},{6,7},{7,6},{8,9},{9,8},{10,11... | collective-permute-start | bytes 589832 | tf_op jit(solution)/shard_map/ppermute | solution.py:34
  511.8 16.4 %collective-permute-start.54 = (bf16[96,768]{1,0:T(8,128)(2,1)}, bf16[96,768]{1,0:T(8,128)(2,1)}, u32[]{:S(2)}, u32[]{:S(2)}) collective-permute-start(bf16[96,768]{1,0:T(8,128)(2,1)} %get-tuple-element.344), channel_id=1, source_target_pairs={{0,8},{8,16},{16,24},{24,0},{1,9},{9,17},{17,25},{25,1},{2,10},{10... | collective-permute-start | bytes 442376 | tf_op jit(solution)/shard_map/ppermute | solution.py:89
  515.8 14.4 %collective-permute-start.52 = (bf16[96,1024]{1,0:T(8,128)(2,1)}, bf16[96,1024]{1,0:T(8,128)(2,1)S(1)}, u32[]{:S(2)}, u32[]{:S(2)}) collective-permute-start(bf16[96,1024]{1,0:T(8,128)(2,1)} %get-tuple-element.334), channel_id=1, source_target_pairs={{0,24},{8,0},{16,8},{24,16},{1,25},{9,1},{17,9},{25,17},{2,26},{10... | collective-permute-start | bytes 589832 | tf_op jit(solution)/shard_map/ppermute | solution.py:89
  517.0 20.8 %collective-permute-start.51 = (bf16[96,1024]{1,0:T(8,128)(2,1)}, bf16[96,1024]{1,0:T(8,128)(2,1)S(1)}, u32[]{:S(2)}, u32[]{:S(2)}) collective-permute-start(bf16[96,1024]{1,0:T(8,128)(2,1)} %get-tuple-element.333), channel_id=1, source_target_pairs={{0,16},{8,24},{16,0},{24,8},{1,17},{9,25},{17,1},{25,9},{2,18},{10... | collective-permute-start | bytes 589832 | tf_op jit(solution)/shard_map/ppermute | solution.py:89
  523.0 28.5 %all-to-all-start.1 = ((bf16[8,96,1280]{2,1,0:T(8,128)(2,1)}), bf16[8,96,1280]{2,1,0:T(8,128)(2,1)S(1)}, u32[]{:S(2)}, u32[]{:S(2)}) async-start(bf16[8,96,1280]{2,1,0:T(8,128)(2,1)} %bitcast.269), calls=%async_computation.2 | async-start | bytes 3932160 | tf_op jit(solution)/shard_map/all_to_all | solution.py:861
  527.1 10.7 %collective-permute-start.50 = (bf16[96,1024]{1,0:T(8,128)(2,1)}, bf16[96,1024]{1,0:T(8,128)(2,1)S(1)}, u32[]{:S(2)}, u32[]{:S(2)}) collective-permute-start(bf16[96,1024]{1,0:T(8,128)(2,1)} %get-tuple-element.332), channel_id=1, source_target_pairs={{0,8},{8,16},{16,24},{24,0},{1,9},{9,17},{17,25},{25,1},{2,10},{10... | collective-permute-start | bytes 589832 | tf_op jit(solution)/shard_map/ppermute | solution.py:89
  553.9 7.5 %collective-permute-start.53 = (f32[48,2]{0,1:T(2,128)S(1)}, f32[48,2]{0,1:T(2,128)S(1)}, u32[]{:S(2)}, u32[]{:S(2)}) collective-permute-start(f32[48,2]{0,1:T(2,128)S(1)} %constant_dynamic-slice_fusion.3), channel_id=1, source_target_pairs={{0,1},{1,0},{2,3},{3,2},{4,5},{5,4},{6,7},{7,6},{8,9},{9,8},{10,11... | collective-permute-start | bytes 1160 | tf_op jit(solution)/shard_map/ppermute | solution.py:34
  (46 other events, 375.2 us)
Sparse Core Ops, SparseCore 0:
  53.5 54.7 all-gather.6
  119.8 52.4 all-gather.8
  189.8 57.0 all-gather.10
  362.7 149.6 reduce-scatter.1
where the time goes:
time: 576 us; the launch traced here: 569 us
  waiting for transfers between devices  194 us (34%)
  starting transfers between devices  107 us (19%)
  Pallas kernels  96.1 us (17%)
  local copies, waits for them, and re-layouts  71.7 us (12%)
  other arithmetic  66.9 us (12%)
  matrix products  17.1 us (3%)
  between operations  15.2 us (3%)
    ppermute x42, waiting for transfers between devices, swap(): return lax.ppermute(x, axis, [(i, length - 1 - i) for i in range(length)])  126 us
    ppermute x42, starting transfers between devices, swap(): return lax.ppermute(x, axis, [(i, length - 1 - i) for i in range(length)])  67.2 us
    pallas_call x2, Pallas kernels, expert_groups(): pl.pallas_call(functools.partial(expert_kernel, capacity=capacity), grid=...  41.7 us
    all_gather x3, waiting for transfers between devices, on_device(): lax.all_gather(shard, 'outer')  28.7 us
    ppermute x9, waiting for transfers between devices, outer_shift(): lax.ppermute(x, 'outer', [(i, (i + by) % length) for i in range(length)])  22.2 us
    unnamed x110, local copies, waits for them, and re-layouts  20.5 us
    ppermute x6, starting transfers between devices, shift_groups(): lax.ppermute(x, DP, [(i, i + by) for i in range(length) if 0 <= i + by <...  18.8 us
    pallas_call x1, Pallas kernels, attention_back(): pl.pallas_call(functools.partial(attention_back_kernel, seq_len=seq_len,...  17.7 us
  transfers between devices with their start and end apart: 63, of which 27 were waited for; matrix products, arithmetic and copies ran while one was open for 21% of the time, Pallas kernels for 13%

commit v1 on v0

--- a/solution.py
+++ b/solution.py
@@ -388,7 +388,7 @@
         ],
         compiler_params=pltpu.CompilerParams(vmem_limit_bytes=VMEM_LIMIT),
         cost_estimate=pl.CostEstimate(
-            flops=70_000_000_000, bytes_accessed=10_000_000, transcendentals=0
+            flops=52_000_000_000, bytes_accessed=10_000_000, transcendentals=0
         ),
         name="attention_back",
     )(place, segment_key, segment_query, queries, key_value, lse, dout, cosine, sine)
@@ -817,14 +817,12 @@
     grad_query_pre, grad_far_kv, grad_own = attention_back(
         *view, log_total, grad_heads, cosine, sine, seq_len
     )
-    grad_query_pre, output_total, moe_parts = lax.optimization_barrier(
-        (grad_query_pre, output_total, moe_parts)
-    )
+    grad_query_pre, output_total = lax.optimization_barrier((grad_query_pre, output_total))
     output_parts = fold_plane(distance_blocks(output_total))
     query_total = fold_columns(normed_in, grad_query_pre, shard_rows)
     two_back, pair_old, one_back, pair_new = grad_far_kv.reshape(reach, own_rows, -1)
-    pair_got, output_parts, query_total = lax.optimization_barrier(
-        (swap(jnp.stack([pair_old, pair_new]), "tensor"), output_parts, query_total)
+    pair_got, output_parts, query_total, moe_parts = lax.optimization_barrier(
+        (swap(jnp.stack([pair_old, pair_new]), "tensor"), output_parts, query_total, moe_parts)
     )
     query_parts = fold_plane(distance_blocks(query_total))
     pair_old, pair_new = pair_got.astype(F32)

time: 576 us -> 589 us (1.023)
  waiting for transfers between devices: 194 us -> 214 us
  local copies, waits for them, and re-layouts: 71.7 us -> 62.3 us
    ppermute x42, waiting for transfers between devices: 126 us -> 138 us  [swap(): return lax.ppermute(x, axis, [(i, length - 1 - i) for i in range(length)])]
    unnamed x110 -> x100, local copies, waits for them, and re-layouts: 20.5 us -> 13 us
    all_gather x3, waiting for transfers between devices: 28.7 us -> 34.9 us  [on_device(): lax.all_gather(shard, 'outer')]
  transfers between devices with their start and end apart: 63 -> 63, of which waited for: 27 -> 28; matrix products, arithmetic and copies ran while one was open for 21% -> 22% of each run, Pallas kernels for 13% -> 13%
where the time goes in v1:
time: 589 us; the launch traced here: 582 us
  waiting for transfers between devices  214 us (36%)
  starting transfers between devices  106 us (18%)
  Pallas kernels  95.2 us (16%)
  other arithmetic  69.7 us (12%)
  local copies, waits for them, and re-layouts  62.3 us (11%)
  matrix products  19.8 us (3%)
  between operations  15.2 us (3%)
    ppermute x42, waiting for transfers between devices, swap(): return lax.ppermute(x, axis, [(i, length - 1 - i) for i in range(length)])  138 us
    ppermute x42, starting transfers between devices, swap(): return lax.ppermute(x, axis, [(i, length - 1 - i) for i in range(length)])  65.3 us
    pallas_call x2, Pallas kernels, expert_groups(): pl.pallas_call(functools.partial(expert_kernel, capacity=capacity), grid=...  41.6 us
    all_gather x3, waiting for transfers between devices, on_device(): lax.all_gather(shard, 'outer')  34.9 us
    ppermute x9, waiting for transfers between devices, outer_shift(): lax.ppermute(x, 'outer', [(i, (i + by) % length) for i in range(length)])  21.9 us
    dot_general x10, matrix products, dot(): return lax.dot_general(a, b, (dims, ((), ())), preferred_element_type=F32)  19.8 us
    ppermute x6, starting transfers between devices, shift_groups(): lax.ppermute(x, DP, [(i, i + by) for i in range(length) if 0 <= i + by <...  18.8 us
    pallas_call x1, Pallas kernels, attention_back(): pl.pallas_call(functools.partial(attention_back_kernel, seq_len=seq_len,...  16.9 us
  transfers between devices with their start and end apart: 63, of which 28 were waited for; matrix products, arithmetic and copies ran while one was open for 22% of the time, Pallas kernels for 13%

profile of v1, /device:TPU:0, one launch (start us, length us, event | category | flops | bytes accessed | tf_op | source)
XLA Modules:
  0.0 582.2 jit_solution(11833371024096887764)
XLA Ops:
  8.8 3.0 collective-permute-start
  15.6 2.1 collective-permute-start.1
  17.7 2.6 collective-permute-start.2
  24.4 3.7 all-to-all-start
  31.2 13.8 %collective-permute-done.2 = bf16[96,2048]{1,0:T(8,128)(2,1)} collective-permute-done((bf16[96,2048]{1,0:T(8,128)(2,1)}, bf16[96,2048]{1,0:T(8,128)(2,1)}, u32[]{:S(2)}, u32[]{:S(2)}) %collective-permute-start.2) | collective-permute-done | bytes 393248 | tf_op jit(solution)/shard_map/ppermute | solution.py:89
  47.0 3.3 all-to-all-done
  64.6 2.8 collective-permute-done.7
  67.7 8.0 %scatter_custom_fusion = s32[2048]{0:T(1024)S(1)} fusion(s32[2048]{0:T(1024)S(1)} %compare_select_fusion.1, s32[2048]{0:T(1024)S(1)} %iota.24, s32[]{:T(128)} %constant.894.clone.1), kind=kCustom, calls=%fused_computation.211 | custom fusion | bytes 8196 | tf_op jit(solution)/shard_map/scatter | solution.py:679
  76.3 5.4 collective-permute-start.11
  84.3 3.1 project.2
  87.4 4.6 collective-permute-start.9
  92.0 4.3 collective-permute-start.10
  97.2 6.3 %collective-permute-done.10 = bf16[256,512]{1,0:T(8,128)(2,1)S(1)} collective-permute-done((bf16[256,512]{1,0:T(8,128)(2,1)}, bf16[256,512]{1,0:T(8,128)(2,1)S(1)}, u32[]{:S(2)}, u32[]{:S(2)}) %collective-permute-start.10) | collective-permute-done | bytes 262176 | tf_op jit(solution)/shard_map/ppermute | solution.py:29
  103.4 4.8 all-gather.7.cloned.1.call-done
  108.2 3.4 pad_maximum_fusion.2
  114.5 6.3 %collective-permute-start.16 = (bf16[4,96,768]{2,1,0:T(8,128)(2,1)S(1)}, bf16[4,96,768]{2,1,0:T(8,128)(2,1)}, u32[]{:S(2)}, u32[]{:S(2)}) collective-permute-start(bf16[4,96,768]{2,1,0:T(8,128)(2,1)S(1)} %copy-done.12), channel_id=1, source_target_pairs={{0,4},{4,0},{1,5},{5,1},{2,6},{6,2},{3,7},{7,3},{8,12},{12,8},{9,1... | collective-permute-start | bytes 1769480 | tf_op jit(solution)/shard_map/ppermute | solution.py:34
  125.1 2.4 collective-permute-done.14
  127.5 6.3 %collective-permute-start.19 = (bf16[256,1664]{1,0:T(8,128)(2,1)S(1)}, bf16[256,1664]{1,0:T(8,128)(2,1)}, u32[]{:S(2)}, u32[]{:S(2)}) collective-permute-start(bf16[256,1664]{1,0:T(8,128)(2,1)S(1)} %fusion.8), channel_id=1, source_target_pairs={{0,4},{4,0},{1,5},{5,1},{2,6},{6,2},{3,7},{7,3},{8,12},{12,8},{9,1... | collective-permute-start | bytes 2555912 | tf_op jit(solution)/shard_map/ppermute | solution.py:34
  134.8 2.7 broadcast_select_fusion.3
  137.8 2.6 maximum_maximum_fusion
  140.5 6.9 %collective-permute-start.17 = (bf16[4,96,768]{2,1,0:T(8,128)(2,1)S(1)}, bf16[4,96,768]{2,1,0:T(8,128)(2,1)}, u32[]{:S(2)}, u32[]{:S(2)}) collective-permute-start(bf16[4,96,768]{2,1,0:T(8,128)(2,1)S(1)} %copy-done.12), channel_id=1, source_target_pairs={{0,5},{1,4},{4,1},{5,0},{2,7},{3,6},{6,3},{7,2},{8,13},{9,12},{12,... | collective-permute-start | bytes 1769480 | tf_op jit(solution)/shard_map/ppermute | solution.py:34
  149.1 6.5 %project.3.q_ref = bf16[256,1536]{1,0:T(8,128)(2,1)} custom-call(bf16[256,1536]{1,0:T(8,128)(2,1)} %fusion.3.rows_ref, bf16[1536,1536]{1,0:T(8,128)(2,1)} %bitcast.251, f32[256,128]{1,0:T(8,128)} %get-tuple-element.374.cosine_ref, f32[256,128]{1,0:T(8,128)} %get-tuple-element.375.sine_ref), custom_call_target="tpu_custom_call" | custom-call | flops 1000 | bytes 1000 | tf_op jit(solution)/shard_map/project/pallas_call | solution.py:193
  158.8 10.3 %attention.1 = (bf16[256,1536]{1,0:T(8,128)(2,1)}, f32[2,6,256]{2,1,0:T(8,128)}) custom-call(s32[1]{0:T(128)} %bitcast.place_ref, s32[1280,1]{1,0:T(8,128)} %broadcast_in_dim.105.segment_key_ref, s32[1,256]{1,0:T(1,128)} %bitcast.296, bf16[256,1536]{1,0:T(8,128)(2,1)} %project.3.q_ref, bf16[1280,512]{1,0:T(8,128)(2,1)} %constant_dynamic-update-slice_fusion.2.kv_ref), custom_call_target="tpu_custom_call" | custom-call | flops 1000 | bytes 1000 | tf_op jit(solution)/shard_map/attention/pallas_call | solution.py:270
  169.1 15.5 %collective-permute-done.17 = bf16[4,96,768]{2,1,0:T(8,128)(2,1)} collective-permute-done((bf16[4,96,768]{2,1,0:T(8,128)(2,1)S(1)}, bf16[4,96,768]{2,1,0:T(8,128)(2,1)}, u32[]{:S(2)}, u32[]{:S(2)}) %collective-permute-start.17) | collective-permute-done | bytes 589856 | tf_op jit(solution)/shard_map/ppermute | solution.py:34
  184.6 4.4 collective-permute-done.18
  188.9 3.1 pad_maximum_fusion.3
  192.4 3.3 pad_maximum_fusion
  198.4 2.7 broadcast_select_fusion.1
  201.5 2.6 maximum_maximum_fusion.1
  204.1 4.1 multiply_reduce_fusion.1
  209.9 6.2 %collective-permute-start.23 = (bf16[256,1536]{1,0:T(8,128)(2,1)S(1)}, bf16[256,1536]{1,0:T(8,128)(2,1)}, u32[]{:S(2)}, u32[]{:S(2)}) collective-permute-start(bf16[256,1536]{1,0:T(8,128)(2,1)S(1)} %multiply_convert_fusion), channel_id=1, source_target_pairs={{0,4},{4,0},{1,5},{5,1},{2,6},{6,2},{3,7},{7,3},{8,12},{12,8},{9,1... | collective-permute-start | bytes 2359304 | tf_op jit(solution)/shard_map/ppermute | solution.py:34
  219.2 30.1 %all-gather.11.cloned.1.call-done = bf16[3072,384]{1,0:T(8,128)(2,1)} async-done(((bf16[768,384]{1,0:T(8,128)(2,1)}), bf16[3072,384]{1,0:T(8,128)(2,1)}) %all-gather.11.cloned.1.call-update) | async-done | bytes 2359312 | tf_op jit(solution)/shard_map/all_gather | solution.py:694
  250.4 3.2 pad_maximum_fusion.1
  255.8 3.8 collective-permute-done.26
  259.5 20.6 %expert.3 = (bf16[2,512,1536]{2,1,0:T(8,128)(2,1)}, bf16[2,512,1536]{2,1,0:T(8,128)(2,1)}, bf16[512,1536]{1,0:T(8,128)(2,1)}, bf16[512,1536]{1,0:T(8,128)(2,1)},...) custom-call(s32[2,1,512]{2,1,0:T(1,128)} %broadcast_in_dim.102.slot_row_ref,, ...), custom_call_target="tpu_custom_call" | custom-call | flops 1000 | bytes 1000 | tf_op jit(solution)/shard_map/expert/pallas_call | solution.py:500
  282.0 21.0 %expert.2 = (bf16[2,512,1536]{2,1,0:T(8,128)(2,1)}, bf16[2,512,1536]{2,1,0:T(8,128)(2,1)}, bf16[512,1536]{1,0:T(8,128)(2,1)}, bf16[512,1536]{1,0:T(8,128)(2,1)},...) custom-call(s32[2,1,512]{2,1,0:T(1,128)} %copy.126.slot_row_ref, ...), custom_call_target="tpu_custom_call" | custom-call | flops 1000 | bytes 1000 | tf_op jit(solution)/shard_map/expert/pallas_call | solution.py:500
  303.1 4.8 fusion.12
  314.9 16.8 %weight_grads.1 = (bf16[1536,2560]{1,0:T(8,128)(2,1)}, bf16[256,1536]{1,0:T(8,128)(2,1)}, bf16[256,1536]{1,0:T(8,128)(2,1)}, bf16[256,1536]{1,0:T(8,128)(2,1)}, bf16[256,1536]{1,0:T(8,128)(2,1)}) custom-call(bf16[512,1536]{1,0:T(8,128)(2,1)} %get-tuple-element.188.refs_0_, bf16[512,1536]{1,0:T(8,128)(2,1)} %get-tuple-element.189.refs_1_, ...), custom_call_target="tpu_custom_call" | custom-call | flops 15000000512 | bytes 50000000 | tf_op jit(solution)/shard_map/weight_grads/pallas_call | solution.py:600
  333.6 15.7 %collective-permute-done.30 = bf16[256,1536]{1,0:T(8,128)(2,1)} collective-permute-done((bf16[256,1536]{1,0:T(8,128)(2,1)}, bf16[256,1536]{1,0:T(8,128)(2,1)}, u32[]{:S(2)}, u32[]{:S(2)}) %collective-permute-start.30) | collective-permute-done | bytes 786464 | tf_op jit(solution)/shard_map/ppermute | solution.py:34
  349.4 2.0 multiply_reduce_fusion
  351.4 3.5 fusion.51
  356.5 2.3 convolution_convert_fusion.2
  358.9 4.8 convolution_convert_fusion.4.dout_ref
  363.7 16.9 %attention_back.1 = (bf16[256,1536]{1,0:T(8,128)(2,1)}, bf16[1024,512]{1,0:T(8,128)(2,1)}, f32[256,512]{1,0:T(8,128)}) custom-call(s32[1]{0:T(128)} %bitcast.place_ref, s32[1280,1]{1,0:T(8,128)} %broadcast_in_dim.105.segment_key_ref, s32[1,256]{1,0:T(1,128)} %bitcast.297, bf16[256,1536]{1,0:T(8,128)(2,1)} %project.3.q_ref, ...), custom_call_target="tpu_custom_call" | custom-call | flops 51999997952 | bytes 10000000 | tf_op jit(solution)/shard_map/attention_back/pallas_call | solution.py:359
  381.4 3.9 add_convert_fusion.1
  385.3 2.2 convolution_convert_fusion
  393.8 4.1 dynamic-slice_bitcast_fusion.4
  397.9 37.9 %collective-permute-done.32 = bf16[2,256,512]{2,1,0:T(8,128)(2,1)} collective-permute-done((bf16[2,256,512]{2,1,0:T(8,128)(2,1)}, bf16[2,256,512]{2,1,0:T(8,128)(2,1)}, u32[]{:S(2)}, u32[]{:S(2)}) %collective-permute-start.32) | collective-permute-done | bytes 524320 | tf_op jit(solution)/shard_map/ppermute | solution.py:34
  441.5 2.8 add_convert_fusion
  444.3 7.0 %collective-permute-done.34 = bf16[4,96,768]{2,1,0:T(8,128)(2,1)} collective-permute-done((bf16[4,96,768]{2,1,0:T(8,128)(2,1)}, bf16[4,96,768]{2,1,0:T(8,128)(2,1)}, u32[]{:S(2)}, u32[]{:S(2)}) %collective-permute-start.34) | collective-permute-done | bytes 589856 | tf_op jit(solution)/shard_map/ppermute | solution.py:34
  451.3 2.8 collective-permute-done.35
  454.1 10.6 %collective-permute-done.36 = bf16[4,96,768]{2,1,0:T(8,128)(2,1)} collective-permute-done((bf16[4,96,768]{2,1,0:T(8,128)(2,1)}, bf16[4,96,768]{2,1,0:T(8,128)(2,1)}, u32[]{:S(2)}, u32[]{:S(2)}) %collective-permute-start.36) | collective-permute-done | bytes 589856 | tf_op jit(solution)/shard_map/ppermute | solution.py:34
  473.0 3.3 collective-permute-start.44
  479.2 3.3 add_add_fusion
  483.1 4.3 collective-permute-done.43
  487.4 8.2 %collective-permute-done.44 = bf16[4,96,768]{2,1,0:T(8,128)(2,1)S(1)} collective-permute-done((bf16[4,96,768]{2,1,0:T(8,128)(2,1)S(1)}, bf16[4,96,768]{2,1,0:T(8,128)(2,1)S(1)}, u32[]{:S(2)}, u32[]{:S(2)}) %collective-permute-start.44) | collective-permute-done | bytes 589856 | tf_op jit(solution)/shard_map/ppermute | solution.py:34
  495.6 12.3 %collective-permute-done.45 = bf16[4,96,768]{2,1,0:T(8,128)(2,1)S(1)} collective-permute-done((bf16[4,96,768]{2,1,0:T(8,128)(2,1)S(1)}, bf16[4,96,768]{2,1,0:T(8,128)(2,1)S(1)}, u32[]{:S(2)}, u32[]{:S(2)}) %collective-permute-start.45) | collective-permute-done | bytes 589856 | tf_op jit(solution)/shard_map/ppermute | solution.py:34
  510.9 2.8 collective-permute-start.55
  514.3 3.4 collective-permute-start.49
  519.1 4.5 collective-permute-done.49
  530.3 4.5 reshape.345
  536.2 3.9 all-to-all-start.1
  543.9 5.6 collective-permute-done.50
  554.4 10.2 %all-to-all-done.1 = bf16[8,96,1280]{2,1,0:T(8,128)(2,1)S(1)} async-done(((bf16[8,96,1280]{2,1,0:T(8,128)(2,1)}), bf16[8,96,1280]{2,1,0:T(8,128)(2,1)S(1)}, u32[]{:S(2)}, u32[]{:S(2)}) %all-to-all-start.1) | async-done | bytes 1966112 | tf_op jit(solution)/shard_map/all_to_all | solution.py:859
  (309 shorter events, 126.6 us)
Async XLA Ops:
  8.8 5.0 collective-permute-start
  15.6 14.6 %collective-permute-start.1 = (bf16[96,2048]{1,0:T(8,128)(2,1)}, bf16[96,2048]{1,0:T(8,128)(2,1)}, u32[]{:S(2)}, u32[]{:S(2)}) collective-permute-start(bf16[96,2048]{1,0:T(8,128)(2,1)} %pad_maximum_fusion.7), channel_id=1, source_target_pairs={{0,8},{8,16},{16,24},{24,0},{1,9},{9,17},{17,25},{25,1},{2,10},{10... | collective-permute-start | bytes 1179656 | tf_op jit(solution)/shard_map/ppermute | solution.py:89
  17.7 27.3 %collective-permute-start.2 = (bf16[96,2048]{1,0:T(8,128)(2,1)}, bf16[96,2048]{1,0:T(8,128)(2,1)}, u32[]{:S(2)}, u32[]{:S(2)}) collective-permute-start(bf16[96,2048]{1,0:T(8,128)(2,1)} %pad_maximum_fusion.7), channel_id=1, source_target_pairs={{0,16},{8,24},{16,0},{24,8},{1,17},{9,25},{17,1},{25,9},{2,18},{10... | collective-permute-start | bytes 1179656 | tf_op jit(solution)/shard_map/ppermute | solution.py:89
  20.3 25.7 %collective-permute-start.3 = (bf16[96,2048]{1,0:T(8,128)(2,1)}, bf16[96,2048]{1,0:T(8,128)(2,1)}, u32[]{:S(2)}, u32[]{:S(2)}) collective-permute-start(bf16[96,2048]{1,0:T(8,128)(2,1)} %pad_maximum_fusion.7), channel_id=1, source_target_pairs={{0,24},{8,0},{16,8},{24,16},{1,25},{9,1},{17,9},{25,17},{2,26},{10... | collective-permute-start | bytes 1179656 | tf_op jit(solution)/shard_map/ppermute | solution.py:89
  24.4 26.0 %all-to-all-start = ((bf16[8,3,96,384]{3,2,1,0:T(8,128)(2,1)}), bf16[8,3,96,384]{3,2,1,0:T(8,128)(2,1)S(1)}, u32[]{:S(2)}, u32[]{:S(2)}) async-start(bf16[8,3,96,384]{3,2,1,0:T(8,128)(2,1)} %maximum_bitcast_fusion), calls=%async_computation | async-start | bytes 3538944 | tf_op jit(solution)/shard_map/all_to_all | solution.py:667
  28.1 80.1 %all-gather.7.cloned.1.call-start = ((), (), s32[]{:S(2)}) async-start(), calls=%async_computation.4 | async-start | bytes 2949120 | tf_op jit(solution)/shard_map/all_gather | solution.py:694
  53.3 150.7 %all-gather.9.cloned.1.call-start = ((), (), s32[]{:S(2)}) async-start(), calls=%async_computation.5 | async-start | bytes 2949120 | tf_op jit(solution)/shard_map/all_gather | solution.py:694
  55.4 12.0 %collective-permute-start.7 = (bf16[4,96,512]{2,1,0:T(8,128)(2,1)S(1)}, bf16[4,96,512]{2,1,0:T(8,128)(2,1)S(1)}, u32[]{:S(2)}, u32[]{:S(2)}) collective-permute-start(bf16[4,96,512]{2,1,0:T(8,128)(2,1)S(1)} %slice.138), channel_id=1, source_target_pairs={{0,4},{4,0},{1,5},{5,1},{2,6},{6,2},{3,7},{7,3},{8,12},{12,8},{9,1... | collective-permute-start | bytes 1179656 | tf_op jit(solution)/shard_map/ppermute | solution.py:34
  59.3 37.8 %collective-permute-start.4 = (bf16[4,96,768]{2,1,0:T(8,128)(2,1)}, bf16[4,96,768]{2,1,0:T(8,128)(2,1)}, u32[]{:S(2)}, u32[]{:S(2)}) collective-permute-start(bf16[4,96,768]{2,1,0:T(8,128)(2,1)} %get-tuple-element.136), channel_id=1, source_target_pairs={{0,1},{1,0},{2,3},{3,2},{4,5},{5,4},{6,7},{7,6},{8,9},{9,8},{10,11... | collective-permute-start | bytes 1769480 | tf_op jit(solution)/shard_map/ppermute | solution.py:34
  60.0 37.2 %collective-permute-start.5 = (bf16[4,96,768]{2,1,0:T(8,128)(2,1)}, bf16[4,96,768]{2,1,0:T(8,128)(2,1)}, u32[]{:S(2)}, u32[]{:S(2)}) collective-permute-start(bf16[4,96,768]{2,1,0:T(8,128)(2,1)} %get-tuple-element.136), channel_id=1, source_target_pairs={{0,4},{4,0},{1,5},{5,1},{2,6},{6,2},{3,7},{7,3},{8,12},{12,8},{9,1... | collective-permute-start | bytes 1769480 | tf_op jit(solution)/shard_map/ppermute | solution.py:34
  61.5 35.7 %collective-permute-start.6 = (bf16[4,96,768]{2,1,0:T(8,128)(2,1)}, bf16[4,96,768]{2,1,0:T(8,128)(2,1)}, u32[]{:S(2)}, u32[]{:S(2)}) collective-permute-start(bf16[4,96,768]{2,1,0:T(8,128)(2,1)} %get-tuple-element.136), channel_id=1, source_target_pairs={{0,5},{1,4},{4,1},{5,0},{2,7},{3,6},{6,3},{7,2},{8,13},{9,12},{12,... | collective-permute-start | bytes 1769480 | tf_op jit(solution)/shard_map/ppermute | solution.py:34
  62.8 24.6 %collective-permute-start.12 = (s32[512]{0:T(512)}, s32[512]{0:T(512)}, u32[]{:S(2)}, u32[]{:S(2)}) collective-permute-start(s32[512]{0:T(512)} %param.24), channel_id=1, source_target_pairs={{0,2},{2,4},{4,6},{6,8},{8,10},{10,12},{12,14},{14,16},{16,18},{18... | collective-permute-start | bytes 6152 | tf_op jit(solution)/shard_map/ppermute | solution.py:29
  67.6 8.8 %collective-permute-start.8 = (bf16[4,2,96,512]{3,2,1,0:T(8,128)(2,1)S(1)}, bf16[4,2,96,512]{3,2,1,0:T(8,128)(2,1)}, u32[]{:S(2)}, u32[]{:S(2)}) collective-permute-start(bf16[4,2,96,512]{3,2,1,0:T(8,128)(2,1)S(1)} %pad_maximum_fusion.5), channel_id=1, source_target_pairs={{0,2},{2,0},{1,3},{3,1},{4,6},{6,4},{5,7},{7,5},{8,10},{10,8},{9,1... | collective-permute-start | bytes 2359304 | tf_op jit(solution)/shard_map/ppermute | solution.py:34
  76.3 15.7 %collective-permute-start.11 = (s32[512]{0:T(512)}, s32[512]{0:T(512)S(1)}, u32[]{:S(2)}, u32[]{:S(2)}) collective-permute-start(s32[512]{0:T(512)} %param.24), channel_id=1, source_target_pairs={{0,4},{2,6},{4,8},{6,10},{8,12},{10,14},{12,16},{14,18},{16,20},{1... | collective-permute-start | bytes 6152 | tf_op jit(solution)/shard_map/ppermute | solution.py:29
  87.4 9.8 %collective-permute-start.9 = (bf16[256,512]{1,0:T(8,128)(2,1)}, bf16[256,512]{1,0:T(8,128)(2,1)S(1)}, u32[]{:S(2)}, u32[]{:S(2)}) collective-permute-start(bf16[256,512]{1,0:T(8,128)(2,1)} %project.2), channel_id=1, source_target_pairs={{0,2},{2,4},{4,6},{6,8},{8,10},{10,12},{12,14},{14,16},{16,18},{18... | collective-permute-start | bytes 786440 | tf_op jit(solution)/shard_map/ppermute | solution.py:29
  92.0 11.4 %collective-permute-start.10 = (bf16[256,512]{1,0:T(8,128)(2,1)}, bf16[256,512]{1,0:T(8,128)(2,1)S(1)}, u32[]{:S(2)}, u32[]{:S(2)}) collective-permute-start(bf16[256,512]{1,0:T(8,128)(2,1)} %project.2), channel_id=1, source_target_pairs={{0,4},{2,6},{4,8},{6,10},{8,12},{10,14},{12,16},{14,18},{16,20},{1... | collective-permute-start | bytes 786440 | tf_op jit(solution)/shard_map/ppermute | solution.py:29
  111.6 22.3 %collective-permute-start.13 = (bf16[2,2,4,96,768]{4,3,2,1,0:T(8,128)(2,1)}, bf16[2,2,4,96,768]{4,3,2,1,0:T(8,128)(2,1)}, u32[]{:S(2)}, u32[]{:S(2)}) collective-permute-start(bf16[2,2,4,96,768]{4,3,2,1,0:T(8,128)(2,1)} %bitcast.32), channel_id=1, source_target_pairs={{0,2},{2,0},{1,3},{3,1},{4,6},{6,4},{5,7},{7,5},{8,10},{10,8},{9,1... | collective-permute-start | bytes 7077896 | tf_op jit(solution)/shard_map/ppermute | solution.py:34
  112.5 15.0 %collective-permute-start.14 = (bf16[2,256,512]{2,1,0:T(8,128)(2,1)}, bf16[2,256,512]{2,1,0:T(8,128)(2,1)}, u32[]{:S(2)}, u32[]{:S(2)}) collective-permute-start(bf16[2,256,512]{2,1,0:T(8,128)(2,1)} %maximum_select_fusion), channel_id=1, source_target_pairs={{0,1},{1,0},{2,3},{3,2},{4,5},{5,4},{6,7},{7,6},{8,9},{9,8},{10,11... | collective-permute-start | bytes 1572872 | tf_op jit(solution)/shard_map/ppermute | solution.py:34
  114.0 26.5 %collective-permute-start.15 = (bf16[4,96,768]{2,1,0:T(8,128)(2,1)S(1)}, bf16[4,96,768]{2,1,0:T(8,128)(2,1)}, u32[]{:S(2)}, u32[]{:S(2)}) collective-permute-start(bf16[4,96,768]{2,1,0:T(8,128)(2,1)S(1)} %copy-done.12), channel_id=1, source_target_pairs={{0,1},{1,0},{2,3},{3,2},{4,5},{5,4},{6,7},{7,6},{8,9},{9,8},{10,11... | collective-permute-start | bytes 1769480 | tf_op jit(solution)/shard_map/ppermute | solution.py:34
  114.5 54.6 %collective-permute-start.16 = (bf16[4,96,768]{2,1,0:T(8,128)(2,1)S(1)}, bf16[4,96,768]{2,1,0:T(8,128)(2,1)}, u32[]{:S(2)}, u32[]{:S(2)}) collective-permute-start(bf16[4,96,768]{2,1,0:T(8,128)(2,1)S(1)} %copy-done.12), channel_id=1, source_target_pairs={{0,4},{4,0},{1,5},{5,1},{2,6},{6,2},{3,7},{7,3},{8,12},{12,8},{9,1... | collective-permute-start | bytes 1769480 | tf_op jit(solution)/shard_map/ppermute | solution.py:34
  120.9 128.4 %all-gather.11.cloned.1.call-start = ((), (), s32[]{:S(2)}) async-start(), calls=%async_computation.6 | async-start | bytes 2949120 | tf_op jit(solution)/shard_map/all_gather | solution.py:694
  122.9 66.0 %collective-permute-start.18 = (bf16[256,1664]{1,0:T(8,128)(2,1)S(1)}, bf16[256,1664]{1,0:T(8,128)(2,1)}, u32[]{:S(2)}, u32[]{:S(2)}) collective-permute-start(bf16[256,1664]{1,0:T(8,128)(2,1)S(1)} %fusion.8), channel_id=1, source_target_pairs={{0,1},{1,0},{2,3},{3,2},{4,5},{5,4},{6,7},{7,6},{8,9},{9,8},{10,11... | collective-permute-start | bytes 2555912 | tf_op jit(solution)/shard_map/ppermute | solution.py:34
  127.5 61.4 %collective-permute-start.19 = (bf16[256,1664]{1,0:T(8,128)(2,1)S(1)}, bf16[256,1664]{1,0:T(8,128)(2,1)}, u32[]{:S(2)}, u32[]{:S(2)}) collective-permute-start(bf16[256,1664]{1,0:T(8,128)(2,1)S(1)} %fusion.8), channel_id=1, source_target_pairs={{0,4},{4,0},{1,5},{5,1},{2,6},{6,2},{3,7},{7,3},{8,12},{12,8},{9,1... | collective-permute-start | bytes 2555912 | tf_op jit(solution)/shard_map/ppermute | solution.py:34
  133.9 55.1 %collective-permute-start.20 = (bf16[256,1664]{1,0:T(8,128)(2,1)S(1)}, bf16[256,1664]{1,0:T(8,128)(2,1)}, u32[]{:S(2)}, u32[]{:S(2)}) collective-permute-start(bf16[256,1664]{1,0:T(8,128)(2,1)S(1)} %fusion.8), channel_id=1, source_target_pairs={{0,5},{1,4},{4,1},{5,0},{2,7},{3,6},{6,3},{7,2},{8,13},{9,12},{12,... | collective-permute-start | bytes 2555912 | tf_op jit(solution)/shard_map/ppermute | solution.py:34
  140.5 44.1 %collective-permute-start.17 = (bf16[4,96,768]{2,1,0:T(8,128)(2,1)S(1)}, bf16[4,96,768]{2,1,0:T(8,128)(2,1)}, u32[]{:S(2)}, u32[]{:S(2)}) collective-permute-start(bf16[4,96,768]{2,1,0:T(8,128)(2,1)S(1)} %copy-done.12), channel_id=1, source_target_pairs={{0,5},{1,4},{4,1},{5,0},{2,7},{3,6},{6,3},{7,2},{8,13},{9,12},{12,... | collective-permute-start | bytes 1769480 | tf_op jit(solution)/shard_map/ppermute | solution.py:34
  192.1 6.3 %collective-permute-start.21 = (bf16[2,2,4,96,768]{4,3,2,1,0:T(8,128)(2,1)}, bf16[2,2,4,96,768]{4,3,2,1,0:T(8,128)(2,1)}, u32[]{:S(2)}, u32[]{:S(2)}) collective-permute-start(bf16[2,2,4,96,768]{4,3,2,1,0:T(8,128)(2,1)} %bitcast.51), channel_id=1, source_target_pairs={{0,2},{2,0},{1,3},{3,1},{4,6},{6,4},{5,7},{7,5},{8,10},{10,8},{9,1... | collective-permute-start | bytes 7077896 | tf_op jit(solution)/shard_map/ppermute | solution.py:34
  192.1 338.2 %reduce-scatter.2.cloned.1.call-start = ((), (), s32[]{:S(2)}) async-start(), calls=%async_computation.3 | async-start | bytes 9830400 | tf_op jit(solution)/shard_map/reduce_scatter | solution.py:807
  195.7 20.4 %collective-permute-start.25 = (bf16[2,2,256,1664]{3,2,1,0:T(8,128)(2,1)}, bf16[2,2,256,1664]{3,2,1,0:T(8,128)(2,1)}, u32[]{:S(2)}, u32[]{:S(2)}) collective-permute-start(bf16[2,2,256,1664]{3,2,1,0:T(8,128)(2,1)} %bitcast.66), channel_id=1, source_target_pairs={{0,2},{2,0},{1,3},{3,1},{4,6},{6,4},{5,7},{7,5},{8,10},{10,8},{9,1... | collective-permute-start | bytes 10223624 | tf_op jit(solution)/shard_map/ppermute | solution.py:34
  208.4 40.8 %collective-permute-start.22 = (bf16[256,1536]{1,0:T(8,128)(2,1)S(1)}, bf16[256,1536]{1,0:T(8,128)(2,1)}, u32[]{:S(2)}, u32[]{:S(2)}) collective-permute-start(bf16[256,1536]{1,0:T(8,128)(2,1)S(1)} %multiply_convert_fusion), channel_id=1, source_target_pairs={{0,1},{1,0},{2,3},{3,2},{4,5},{5,4},{6,7},{7,6},{8,9},{9,8},{10,11... | collective-permute-start | bytes 2359304 | tf_op jit(solution)/shard_map/ppermute | solution.py:34
  209.9 39.4 %collective-permute-start.23 = (bf16[256,1536]{1,0:T(8,128)(2,1)S(1)}, bf16[256,1536]{1,0:T(8,128)(2,1)}, u32[]{:S(2)}, u32[]{:S(2)}) collective-permute-start(bf16[256,1536]{1,0:T(8,128)(2,1)S(1)} %multiply_convert_fusion), channel_id=1, source_target_pairs={{0,4},{4,0},{1,5},{5,1},{2,6},{6,2},{3,7},{7,3},{8,12},{12,8},{9,1... | collective-permute-start | bytes 2359304 | tf_op jit(solution)/shard_map/ppermute | solution.py:34
  216.0 34.3 %collective-permute-start.24 = (bf16[256,1536]{1,0:T(8,128)(2,1)S(1)}, bf16[256,1536]{1,0:T(8,128)(2,1)}, u32[]{:S(2)}, u32[]{:S(2)}) collective-permute-start(bf16[256,1536]{1,0:T(8,128)(2,1)S(1)} %multiply_convert_fusion), channel_id=1, source_target_pairs={{0,5},{1,4},{4,1},{5,0},{2,7},{3,6},{6,3},{7,2},{8,13},{9,12},{12,... | collective-permute-start | bytes 2359304 | tf_op jit(solution)/shard_map/ppermute | solution.py:34
  253.5 6.0 %collective-permute-start.26 = (bf16[2,2,256,1536]{3,2,1,0:T(8,128)(2,1)}, bf16[2,2,256,1536]{3,2,1,0:T(8,128)(2,1)}, u32[]{:S(2)}, u32[]{:S(2)}) collective-permute-start(bf16[2,2,256,1536]{3,2,1,0:T(8,128)(2,1)} %bitcast.85), channel_id=1, source_target_pairs={{0,2},{2,0},{1,3},{3,1},{4,6},{6,4},{5,7},{7,5},{8,10},{10,8},{9,1... | collective-permute-start | bytes 9437192 | tf_op jit(solution)/shard_map/ppermute | solution.py:34
  280.2 22.9 %collective-permute-start.27 = (bf16[4,256,1536]{2,1,0:T(8,128)(2,1)}, bf16[4,256,1536]{2,1,0:T(8,128)(2,1)}, u32[]{:S(2)}, u32[]{:S(2)}) collective-permute-start(bf16[4,256,1536]{2,1,0:T(8,128)(2,1)} %bitcast.301), channel_id=1, source_target_pairs={{0,2},{2,0},{1,3},{3,1},{4,6},{6,4},{5,7},{7,5},{8,10},{10,8},{9,1... | collective-permute-start | bytes 9437192 | tf_op jit(solution)/shard_map/ppermute | solution.py:34
  307.9 7.0 %collective-permute-start.31 = (bf16[4,256,1536]{2,1,0:T(8,128)(2,1)}, bf16[4,256,1536]{2,1,0:T(8,128)(2,1)}, u32[]{:S(2)}, u32[]{:S(2)}) collective-permute-start(bf16[4,256,1536]{2,1,0:T(8,128)(2,1)} %bitcast.93), channel_id=1, source_target_pairs={{0,2},{2,0},{1,3},{3,1},{4,6},{6,4},{5,7},{7,5},{8,10},{10,8},{9,1... | collective-permute-start | bytes 9437192 | tf_op jit(solution)/shard_map/ppermute | solution.py:34
  311.4 20.3 %collective-permute-start.28 = (bf16[256,1536]{1,0:T(8,128)(2,1)}, bf16[256,1536]{1,0:T(8,128)(2,1)S(1)}, u32[]{:S(2)}, u32[]{:S(2)}) collective-permute-start(bf16[256,1536]{1,0:T(8,128)(2,1)} %get-tuple-element.185), channel_id=1, source_target_pairs={{0,1},{1,0},{2,3},{3,2},{4,5},{5,4},{6,7},{7,6},{8,9},{9,8},{10,11... | collective-permute-start | bytes 2359304 | tf_op jit(solution)/shard_map/ppermute | solution.py:34
  312.9 20.7 %collective-permute-start.29 = (bf16[256,1536]{1,0:T(8,128)(2,1)}, bf16[256,1536]{1,0:T(8,128)(2,1)}, u32[]{:S(2)}, u32[]{:S(2)}) collective-permute-start(bf16[256,1536]{1,0:T(8,128)(2,1)} %get-tuple-element.186), channel_id=1, source_target_pairs={{0,4},{4,0},{1,5},{5,1},{2,6},{6,2},{3,7},{7,3},{8,12},{12,8},{9,1... | collective-permute-start | bytes 2359304 | tf_op jit(solution)/shard_map/ppermute | solution.py:34
  314.6 34.7 %collective-permute-start.30 = (bf16[256,1536]{1,0:T(8,128)(2,1)}, bf16[256,1536]{1,0:T(8,128)(2,1)}, u32[]{:S(2)}, u32[]{:S(2)}) collective-permute-start(bf16[256,1536]{1,0:T(8,128)(2,1)} %get-tuple-element.187), channel_id=1, source_target_pairs={{0,5},{1,4},{4,1},{5,0},{2,7},{3,6},{6,3},{7,2},{8,13},{9,12},{12,... | collective-permute-start | bytes 2359304 | tf_op jit(solution)/shard_map/ppermute | solution.py:34
  358.9 22.5 %collective-permute-start.33 = (bf16[768,1536]{1,0:T(8,128)(2,1)}, bf16[768,1536]{1,0:T(8,128)(2,1)}, u32[]{:S(2)}, u32[]{:S(2)}) collective-permute-start(bf16[768,1536]{1,0:T(8,128)(2,1)} %convolution_convert_fusion.2), channel_id=1, source_target_pairs={{0,2},{2,0},{1,3},{3,1},{4,6},{6,4},{5,7},{7,5},{8,10},{10,8},{9,1... | collective-permute-start | bytes 7077896 | tf_op jit(solution)/shard_map/ppermute | solution.py:34
  387.4 51.7 %collective-permute-start.37 = (bf16[768,1536]{1,0:T(8,128)(2,1)}, bf16[768,1536]{1,0:T(8,128)(2,1)}, u32[]{:S(2)}, u32[]{:S(2)}) collective-permute-start(bf16[768,1536]{1,0:T(8,128)(2,1)} %convolution_convert_fusion), channel_id=1, source_target_pairs={{0,2},{2,0},{1,3},{3,1},{4,6},{6,4},{5,7},{7,5},{8,10},{10,8},{9,1... | collective-permute-start | bytes 7077896 | tf_op jit(solution)/shard_map/ppermute | solution.py:34
  387.9 49.7 %collective-permute-start.38 = (bf16[256,1536]{1,0:T(8,128)(2,1)}, bf16[256,1536]{1,0:T(8,128)(2,1)}, u32[]{:S(2)}, u32[]{:S(2)}) collective-permute-start(bf16[256,1536]{1,0:T(8,128)(2,1)} %get-tuple-element.216), channel_id=1, source_target_pairs={{0,1},{1,0},{2,3},{3,2},{4,5},{5,4},{6,7},{7,6},{8,9},{9,8},{10,11... | collective-permute-start | bytes 2359304 | tf_op jit(solution)/shard_map/ppermute | solution.py:34
  390.3 45.5 %collective-permute-start.32 = (bf16[2,256,512]{2,1,0:T(8,128)(2,1)}, bf16[2,256,512]{2,1,0:T(8,128)(2,1)}, u32[]{:S(2)}, u32[]{:S(2)}) collective-permute-start(bf16[2,256,512]{2,1,0:T(8,128)(2,1)} %pad_maximum_fusion.6), channel_id=1, source_target_pairs={{0,1},{1,0},{2,3},{3,2},{4,5},{5,4},{6,7},{7,6},{8,9},{9,8},{10,11... | collective-permute-start | bytes 1572872 | tf_op jit(solution)/shard_map/ppermute | solution.py:34
  390.8 53.5 %collective-permute-start.39 = (bf16[256,1536]{1,0:T(8,128)(2,1)}, bf16[256,1536]{1,0:T(8,128)(2,1)}, u32[]{:S(2)}, u32[]{:S(2)}) collective-permute-start(bf16[256,1536]{1,0:T(8,128)(2,1)} %get-tuple-element.217), channel_id=1, source_target_pairs={{0,4},{4,0},{1,5},{5,1},{2,6},{6,2},{3,7},{7,3},{8,12},{12,8},{9,1... | collective-permute-start | bytes 2359304 | tf_op jit(solution)/shard_map/ppermute | solution.py:34
  392.5 51.8 %collective-permute-start.40 = (bf16[256,1536]{1,0:T(8,128)(2,1)}, bf16[256,1536]{1,0:T(8,128)(2,1)}, u32[]{:S(2)}, u32[]{:S(2)}) collective-permute-start(bf16[256,1536]{1,0:T(8,128)(2,1)} %get-tuple-element.218), channel_id=1, source_target_pairs={{0,5},{1,4},{4,1},{5,0},{2,7},{3,6},{6,3},{7,2},{8,13},{9,12},{12,... | collective-permute-start | bytes 2359304 | tf_op jit(solution)/shard_map/ppermute | solution.py:34
  393.8 74.8 %slice-start = ((s8[4718592]{0:T(1024)(128)(4,1)}), s8[524288]{0:T(1024)(128)(4,1)S(1)}, s32[]{:S(2)}) async-start(s8[4718592]{0:T(1024)(128)(4,1)} %bitcast.252), calls=%async_computation.7 | async-start | bytes 1048576
  435.8 15.5 %collective-permute-start.34 = (bf16[4,96,768]{2,1,0:T(8,128)(2,1)}, bf16[4,96,768]{2,1,0:T(8,128)(2,1)}, u32[]{:S(2)}, u32[]{:S(2)}) collective-permute-start(bf16[4,96,768]{2,1,0:T(8,128)(2,1)} %get-tuple-element.298), channel_id=1, source_target_pairs={{0,1},{1,0},{2,3},{3,2},{4,5},{5,4},{6,7},{7,6},{8,9},{9,8},{10,11... | collective-permute-start | bytes 1769480 | tf_op jit(solution)/shard_map/ppermute | solution.py:34
  437.6 16.6 %collective-permute-start.35 = (bf16[4,96,768]{2,1,0:T(8,128)(2,1)}, bf16[4,96,768]{2,1,0:T(8,128)(2,1)}, u32[]{:S(2)}, u32[]{:S(2)}) collective-permute-start(bf16[4,96,768]{2,1,0:T(8,128)(2,1)} %get-tuple-element.297), channel_id=1, source_target_pairs={{0,4},{4,0},{1,5},{5,1},{2,6},{6,2},{3,7},{7,3},{8,12},{12,8},{9,1... | collective-permute-start | bytes 1769480 | tf_op jit(solution)/shard_map/ppermute | solution.py:34
  439.1 25.6 %collective-permute-start.36 = (bf16[4,96,768]{2,1,0:T(8,128)(2,1)}, bf16[4,96,768]{2,1,0:T(8,128)(2,1)}, u32[]{:S(2)}, u32[]{:S(2)}) collective-permute-start(bf16[4,96,768]{2,1,0:T(8,128)(2,1)} %get-tuple-element.296), channel_id=1, source_target_pairs={{0,5},{1,4},{4,1},{5,0},{2,7},{3,6},{6,3},{7,2},{8,13},{9,12},{12,... | collective-permute-start | bytes 1769480 | tf_op jit(solution)/shard_map/ppermute | solution.py:34
  466.1 10.2 %collective-permute-start.42 = (bf16[256,512]{1,0:T(8,128)(2,1)S(1)}, bf16[256,512]{1,0:T(8,128)(2,1)S(1)}, u32[]{:S(2)}, u32[]{:S(2)}) collective-permute-start(bf16[256,512]{1,0:T(8,128)(2,1)S(1)} %get-tuple-element.317), channel_id=1, source_target_pairs={{4,0},{6,2},{8,4},{10,6},{12,8},{14,10},{16,12},{18,14},{20,16},{2... | collective-permute-start | bytes 786440 | tf_op jit(solution)/shard_map/ppermute | solution.py:29
  467.4 8.9 %collective-permute-start.41 = (bf16[256,512]{1,0:T(8,128)(2,1)S(1)}, bf16[256,512]{1,0:T(8,128)(2,1)S(1)}, u32[]{:S(2)}, u32[]{:S(2)}) collective-permute-start(bf16[256,512]{1,0:T(8,128)(2,1)S(1)} %get-tuple-element.316), channel_id=1, source_target_pairs={{2,0},{4,2},{6,4},{8,6},{10,8},{12,10},{14,12},{16,14},{18,16},{20... | collective-permute-start | bytes 786440 | tf_op jit(solution)/shard_map/ppermute | solution.py:29
  471.3 16.1 %collective-permute-start.43 = (bf16[4,96,768]{2,1,0:T(8,128)(2,1)S(1)}, bf16[4,96,768]{2,1,0:T(8,128)(2,1)S(1)}, u32[]{:S(2)}, u32[]{:S(2)}) collective-permute-start(bf16[4,96,768]{2,1,0:T(8,128)(2,1)S(1)} %get-tuple-element.294), channel_id=1, source_target_pairs={{0,1},{1,0},{2,3},{3,2},{4,5},{5,4},{6,7},{7,6},{8,9},{9,8},{10,11... | collective-permute-start | bytes 1769480 | tf_op jit(solution)/shard_map/ppermute | solution.py:34
  473.0 22.6 %collective-permute-start.44 = (bf16[4,96,768]{2,1,0:T(8,128)(2,1)S(1)}, bf16[4,96,768]{2,1,0:T(8,128)(2,1)S(1)}, u32[]{:S(2)}, u32[]{:S(2)}) collective-permute-start(bf16[4,96,768]{2,1,0:T(8,128)(2,1)S(1)} %get-tuple-element.293), channel_id=1, source_target_pairs={{0,4},{4,0},{1,5},{5,1},{2,6},{6,2},{3,7},{7,3},{8,12},{12,8},{9,1... | collective-permute-start | bytes 1769480 | tf_op jit(solution)/shard_map/ppermute | solution.py:34
  476.3 31.6 %collective-permute-start.45 = (bf16[4,96,768]{2,1,0:T(8,128)(2,1)S(1)}, bf16[4,96,768]{2,1,0:T(8,128)(2,1)S(1)}, u32[]{:S(2)}, u32[]{:S(2)}) collective-permute-start(bf16[4,96,768]{2,1,0:T(8,128)(2,1)S(1)} %get-tuple-element.292), channel_id=1, source_target_pairs={{0,5},{1,4},{4,1},{5,0},{2,7},{3,6},{6,3},{7,2},{8,13},{9,12},{12,... | collective-permute-start | bytes 1769480 | tf_op jit(solution)/shard_map/ppermute | solution.py:34
  477.9 35.8 %collective-permute-start.46 = (bf16[768,512]{1,0:T(8,128)(2,1)S(1)}, bf16[768,512]{1,0:T(8,128)(2,1)S(1)}, u32[]{:S(2)}, u32[]{:S(2)}) collective-permute-start(bf16[768,512]{1,0:T(8,128)(2,1)S(1)} %convolution_convert_fusion.5), channel_id=1, source_target_pairs={{0,2},{2,0},{1,3},{3,1},{4,6},{6,4},{5,7},{7,5},{8,10},{10,8},{9,1... | collective-permute-start | bytes 2359304 | tf_op jit(solution)/shard_map/ppermute | solution.py:34
  510.5 29.6 %collective-permute-start.56 = (bf16[96,768]{1,0:T(8,128)(2,1)}, bf16[96,768]{1,0:T(8,128)(2,1)}, u32[]{:S(2)}, u32[]{:S(2)}) collective-permute-start(bf16[96,768]{1,0:T(8,128)(2,1)} %get-tuple-element.345), channel_id=1, source_target_pairs={{0,24},{8,0},{16,8},{24,16},{1,25},{9,1},{17,9},{25,17},{2,26},{10... | collective-permute-start | bytes 442376 | tf_op jit(solution)/shard_map/ppermute | solution.py:89
  510.9 29.4 %collective-permute-start.55 = (bf16[96,768]{1,0:T(8,128)(2,1)}, bf16[96,768]{1,0:T(8,128)(2,1)}, u32[]{:S(2)}, u32[]{:S(2)}) collective-permute-start(bf16[96,768]{1,0:T(8,128)(2,1)} %get-tuple-element.346), channel_id=1, source_target_pairs={{0,16},{8,24},{16,0},{24,8},{1,17},{9,25},{17,1},{25,9},{2,18},{10... | collective-permute-start | bytes 442376 | tf_op jit(solution)/shard_map/ppermute | solution.py:89
  514.3 9.3 %collective-permute-start.49 = (bf16[4,96,256]{2,1,0:T(8,128)(2,1)S(1)}, bf16[4,96,256]{2,1,0:T(8,128)(2,1)S(1)}, u32[]{:S(2)}, u32[]{:S(2)}) collective-permute-start(bf16[4,96,256]{2,1,0:T(8,128)(2,1)S(1)} %get-tuple-element.336), channel_id=1, source_target_pairs={{0,5},{1,4},{4,1},{5,0},{2,7},{3,6},{6,3},{7,2},{8,13},{9,12},{12,... | collective-permute-start | bytes 589832 | tf_op jit(solution)/shard_map/ppermute | solution.py:34
  517.8 8.0 %collective-permute-start.48 = (bf16[4,96,256]{2,1,0:T(8,128)(2,1)S(1)}, bf16[4,96,256]{2,1,0:T(8,128)(2,1)S(1)}, u32[]{:S(2)}, u32[]{:S(2)}) collective-permute-start(bf16[4,96,256]{2,1,0:T(8,128)(2,1)S(1)} %get-tuple-element.337), channel_id=1, source_target_pairs={{0,4},{4,0},{1,5},{5,1},{2,6},{6,2},{3,7},{7,3},{8,12},{12,8},{9,1... | collective-permute-start | bytes 589832 | tf_op jit(solution)/shard_map/ppermute | solution.py:34
  517.8 8.5 %collective-permute-start.47 = (bf16[4,96,256]{2,1,0:T(8,128)(2,1)S(1)}, bf16[4,96,256]{2,1,0:T(8,128)(2,1)S(1)}, u32[]{:S(2)}, u32[]{:S(2)}) collective-permute-start(bf16[4,96,256]{2,1,0:T(8,128)(2,1)S(1)} %get-tuple-element.335), channel_id=1, source_target_pairs={{0,1},{1,0},{2,3},{3,2},{4,5},{5,4},{6,7},{7,6},{8,9},{9,8},{10,11... | collective-permute-start | bytes 589832 | tf_op jit(solution)/shard_map/ppermute | solution.py:34
  523.6 16.6 %collective-permute-start.54 = (bf16[96,768]{1,0:T(8,128)(2,1)}, bf16[96,768]{1,0:T(8,128)(2,1)}, u32[]{:S(2)}, u32[]{:S(2)}) collective-permute-start(bf16[96,768]{1,0:T(8,128)(2,1)} %get-tuple-element.344), channel_id=1, source_target_pairs={{0,8},{8,16},{16,24},{24,0},{1,9},{9,17},{17,25},{25,1},{2,10},{10... | collective-permute-start | bytes 442376 | tf_op jit(solution)/shard_map/ppermute | solution.py:89
  527.4 14.9 %collective-permute-start.52 = (bf16[96,1024]{1,0:T(8,128)(2,1)}, bf16[96,1024]{1,0:T(8,128)(2,1)}, u32[]{:S(2)}, u32[]{:S(2)}) collective-permute-start(bf16[96,1024]{1,0:T(8,128)(2,1)} %get-tuple-element.334), channel_id=1, source_target_pairs={{0,24},{8,0},{16,8},{24,16},{1,25},{9,1},{17,9},{25,17},{2,26},{10... | collective-permute-start | bytes 589832 | tf_op jit(solution)/shard_map/ppermute | solution.py:89
  528.6 15.3 %collective-permute-start.51 = (bf16[96,1024]{1,0:T(8,128)(2,1)}, bf16[96,1024]{1,0:T(8,128)(2,1)}, u32[]{:S(2)}, u32[]{:S(2)}) collective-permute-start(bf16[96,1024]{1,0:T(8,128)(2,1)} %get-tuple-element.333), channel_id=1, source_target_pairs={{0,16},{8,24},{16,0},{24,8},{1,17},{9,25},{17,1},{25,9},{2,18},{10... | collective-permute-start | bytes 589832 | tf_op jit(solution)/shard_map/ppermute | solution.py:89
  536.2 28.3 %all-to-all-start.1 = ((bf16[8,96,1280]{2,1,0:T(8,128)(2,1)}), bf16[8,96,1280]{2,1,0:T(8,128)(2,1)S(1)}, u32[]{:S(2)}, u32[]{:S(2)}) async-start(bf16[8,96,1280]{2,1,0:T(8,128)(2,1)} %bitcast.265), calls=%async_computation.2 | async-start | bytes 3932160 | tf_op jit(solution)/shard_map/all_to_all | solution.py:859
  540.2 9.4 %collective-permute-start.50 = (bf16[96,1024]{1,0:T(8,128)(2,1)}, bf16[96,1024]{1,0:T(8,128)(2,1)S(1)}, u32[]{:S(2)}, u32[]{:S(2)}) collective-permute-start(bf16[96,1024]{1,0:T(8,128)(2,1)} %get-tuple-element.332), channel_id=1, source_target_pairs={{0,8},{8,16},{16,24},{24,0},{1,9},{9,17},{17,25},{25,1},{2,10},{10... | collective-permute-start | bytes 589832 | tf_op jit(solution)/shard_map/ppermute | solution.py:89
  567.0 7.7 %collective-permute-start.53 = (f32[48,2]{0,1:T(2,128)S(1)}, f32[48,2]{0,1:T(2,128)S(1)}, u32[]{:S(2)}, u32[]{:S(2)}) collective-permute-start(f32[48,2]{0,1:T(2,128)S(1)} %constant_dynamic-slice_fusion.3), channel_id=1, source_target_pairs={{0,1},{1,0},{2,3},{3,2},{4,5},{5,4},{6,7},{7,6},{8,9},{9,8},{10,11... | collective-permute-start | bytes 1160 | tf_op jit(solution)/shard_map/ppermute | solution.py:34
  (41 other events, 360.4 us)
Sparse Core Ops, SparseCore 0:
  53.4 54.7 all-gather.6
  121.0 52.5 all-gather.8
  192.2 57.0 all-gather.10
  349.5 145.2 reduce-scatter.1

commit v2 on v0

--- a/solution.py
+++ b/solution.py
@@ -388,7 +388,7 @@
         ],
         compiler_params=pltpu.CompilerParams(vmem_limit_bytes=VMEM_LIMIT),
         cost_estimate=pl.CostEstimate(
-            flops=70_000_000_000, bytes_accessed=10_000_000, transcendentals=0
+            flops=52_000_000_000, bytes_accessed=10_000_000, transcendentals=0
         ),
         name="attention_back",
     )(place, segment_key, segment_query, queries, key_value, lse, dout, cosine, sine)
@@ -769,8 +769,8 @@
     cotangent_near = plane_stack(cotangent_parts)
     cotangent_far = swap(cotangent_near, "core")
     near_slots, far_slots = slots_of(cotangent_near), slots_of(cotangent_far)
-    normed_parts, near_slots, far_slots, expert_full[2] = lax.optimization_barrier(
-        (plane_parts(normed_mid_own), near_slots, far_slots, expert_full[2])
+    normed_parts, expert_full[2] = lax.optimization_barrier(
+        (plane_parts(normed_mid_own), expert_full[2])
     )
     normed_near = plane_stack(normed_parts)
     normed_far = swap(normed_near, "core")
@@ -846,11 +846,11 @@
         grad_key_value.append(grad_own[:, start + HEAD_SIZE : start + 2 * HEAD_SIZE])
     grad_key_value_pre = jnp.concatenate(grad_key_value, axis=1).astype(BF16)
     key_value_total = fold_columns(normed_in, grad_key_value_pre, shard_rows)
+    key_value_total, expert_sum = lax.optimization_barrier((key_value_total, expert_sum))
     key_value_parts = fold_plane(distance_blocks(key_value_total))
     grad_in = dot(grad_query_pre, query_full, ((1,), (1,))) + dot(
         grad_key_value_pre, key_value_full, ((1,), (1,))
     )
-    grad_in, expert_sum = lax.optimization_barrier((grad_in, expert_sum))
     input_grad = grad_state + norm_back(input_wide, first_factor, first_gain, grad_in)
     qkv_grad = outer_scatter(
         jnp.concatenate([wide_sum(query_parts), wide_sum(key_value_parts)], axis=2).astype(BF16)

time: 576 us -> 578 us (level)
  waiting for transfers between devices: 194 us -> 201 us
  local copies, waits for them, and re-layouts: 71.7 us -> 65.8 us
    all_to_all x1, waiting for transfers between devices: 9.15 us -> 0.01 us  [on_device(): expert_sum = lax.all_to_all(expert_sum, PLANE, 0, 0, tiled=True)]
    ppermute x9, waiting for transfers between devices: 22.2 us -> 30.9 us  [outer_shift(): lax.ppermute(x, 'outer', [(i, (i + by) % length) for i in range(length)])]
    all_gather x3, waiting for transfers between devices: 28.7 us -> 36.5 us  [on_device(): lax.all_gather(shard, 'outer')]
    unnamed x110 -> x112, local copies, waits for them, and re-layouts: 20.5 us -> 17.2 us
  transfers between devices with their start and end apart: 63 -> 63, of which waited for: 27 -> 26; matrix products, arithmetic and copies ran while one was open for 21% -> 22% of each run, Pallas kernels for 13% -> 13%
where the time goes in v2:
time: 578 us; the launch traced here: 570 us
  waiting for transfers between devices  201 us (35%)
  starting transfers between devices  107 us (19%)
  Pallas kernels  95.1 us (16%)
  other arithmetic  67.7 us (12%)
  local copies, waits for them, and re-layouts  65.8 us (11%)
  matrix products  18.3 us (3%)
  between operations  15.2 us (3%)
    ppermute x42, waiting for transfers between devices, swap(): return lax.ppermute(x, axis, [(i, length - 1 - i) for i in range(length)])  123 us
    ppermute x42, starting transfers between devices, swap(): return lax.ppermute(x, axis, [(i, length - 1 - i) for i in range(length)])  63.5 us
    pallas_call x2, Pallas kernels, expert_groups(): pl.pallas_call(functools.partial(expert_kernel, capacity=capacity), grid=...  41.6 us
    all_gather x3, waiting for transfers between devices, on_device(): lax.all_gather(shard, 'outer')  36.5 us
    ppermute x9, waiting for transfers between devices, outer_shift(): lax.ppermute(x, 'outer', [(i, (i + by) % length) for i in range(length)])  30.9 us
    ppermute x6, starting transfers between devices, shift_groups(): lax.ppermute(x, DP, [(i, i + by) for i in range(length) if 0 <= i + by <...  18.8 us
    dot_general x10, matrix products, dot(): return lax.dot_general(a, b, (dims, ((), ())), preferred_element_type=F32)  18.3 us
    unnamed x112, local copies, waits for them, and re-layouts  17.2 us
  transfers between devices with their start and end apart: 63, of which 26 were waited for; matrix products, arithmetic and copies ran while one was open for 22% of the time, Pallas kernels for 13%

profile of v2, /device:TPU:0, one launch (start us, length us, event | category | flops | bytes accessed | tf_op | source)
XLA Modules:
  0.0 570.4 jit_solution(7610191475217241007)
XLA Ops:
  8.8 3.0 collective-permute-start
  14.9 2.1 collective-permute-start.1
  17.0 2.6 collective-permute-start.2
  23.7 4.3 all-to-all-start
  30.3 13.7 %collective-permute-done.2 = bf16[96,2048]{1,0:T(8,128)(2,1)S(1)} collective-permute-done((bf16[96,2048]{1,0:T(8,128)(2,1)S(1)}, bf16[96,2048]{1,0:T(8,128)(2,1)S(1)}, u32[]{:S(2)}, u32[]{:S(2)}) %collective-permute-start.2) | collective-permute-done | bytes 393248 | tf_op jit(solution)/shard_map/ppermute | solution.py:89
  44.1 6.2 %all-to-all-done = bf16[8,3,96,384]{3,2,1,0:T(8,128)(2,1)} async-done(((bf16[8,3,96,384]{3,2,1,0:T(8,128)(2,1)}), bf16[8,3,96,384]{3,2,1,0:T(8,128)(2,1)}, u32[]{:S(2)}, u32[]{:S(2)}) %all-to-all-start) | async-done | bytes 1769504 | tf_op jit(solution)/shard_map/all_to_all | solution.py:667
  66.0 2.8 collective-permute-done.7
  69.1 8.0 %scatter_custom_fusion = s32[2048]{0:T(1024)S(1)} fusion(s32[2048]{0:T(1024)S(1)} %compare_select_fusion.1, s32[2048]{0:T(1024)S(1)} %iota.24, s32[]{:T(128)} %constant.894.clone.1), kind=kCustom, calls=%fused_computation.212 | custom fusion | bytes 8196 | tf_op jit(solution)/shard_map/scatter | solution.py:679
  78.4 3.5 collective-permute-start.11
  84.5 3.1 project.2
  87.6 6.5 %collective-permute-start.9 = (bf16[256,512]{1,0:T(8,128)(2,1)}, bf16[256,512]{1,0:T(8,128)(2,1)}, u32[]{:S(2)}, u32[]{:S(2)}) collective-permute-start(bf16[256,512]{1,0:T(8,128)(2,1)} %project.2), channel_id=1, source_target_pairs={{0,2},{2,4},{4,6},{6,8},{8,10},{10,12},{12,14},{14,16},{16,18},{18... | collective-permute-start | bytes 786440 | tf_op jit(solution)/shard_map/ppermute | solution.py:29
  94.0 4.4 collective-permute-start.10
  100.1 4.6 collective-permute-done.10
  104.8 1.9 all-gather.7.cloned.1.call-done
  106.7 1.9 pad_maximum_fusion.2
  108.7 2.0 maximum_select_fusion
  112.7 6.5 %collective-permute-start.16 = (bf16[4,96,768]{2,1,0:T(8,128)(2,1)}, bf16[4,96,768]{2,1,0:T(8,128)(2,1)}, u32[]{:S(2)}, u32[]{:S(2)}) collective-permute-start(bf16[4,96,768]{2,1,0:T(8,128)(2,1)} %get-tuple-element.142), channel_id=1, source_target_pairs={{0,4},{4,0},{1,5},{5,1},{2,6},{6,2},{3,7},{7,3},{8,12},{12,8},{9,1... | collective-permute-start | bytes 1769480 | tf_op jit(solution)/shard_map/ppermute | solution.py:34
  125.7 6.5 %collective-permute-start.19 = (bf16[256,1664]{1,0:T(8,128)(2,1)}, bf16[256,1664]{1,0:T(8,128)(2,1)}, u32[]{:S(2)}, u32[]{:S(2)}) collective-permute-start(bf16[256,1664]{1,0:T(8,128)(2,1)} %fusion.9), channel_id=1, source_target_pairs={{0,4},{4,0},{1,5},{5,1},{2,6},{6,2},{3,7},{7,3},{8,12},{12,8},{9,1... | collective-permute-start | bytes 2555912 | tf_op jit(solution)/shard_map/ppermute | solution.py:34
  133.2 2.0 broadcast_select_fusion.3
  135.5 2.6 maximum_maximum_fusion
  138.4 7.4 %collective-permute-start.17 = (bf16[4,96,768]{2,1,0:T(8,128)(2,1)S(1)}, bf16[4,96,768]{2,1,0:T(8,128)(2,1)S(1)}, u32[]{:S(2)}, u32[]{:S(2)}) collective-permute-start(bf16[4,96,768]{2,1,0:T(8,128)(2,1)S(1)} %copy-done.12), channel_id=1, source_target_pairs={{0,5},{1,4},{4,1},{5,0},{2,7},{3,6},{6,3},{7,2},{8,13},{9,12},{12,... | collective-permute-start | bytes 1769480 | tf_op jit(solution)/shard_map/ppermute | solution.py:34
  147.5 6.5 %project.3.q_ref = bf16[256,1536]{1,0:T(8,128)(2,1)} custom-call(bf16[256,1536]{1,0:T(8,128)(2,1)} %fusion.4.rows_ref, bf16[1536,1536]{1,0:T(8,128)(2,1)} %bitcast.251, f32[256,128]{1,0:T(8,128)} %get-tuple-element.370.cosine_ref, f32[256,128]{1,0:T(8,128)} %get-tuple-element.371.sine_ref), custom_call_target="tpu_custom_call" | custom-call | flops 1000 | bytes 1000 | tf_op jit(solution)/shard_map/project/pallas_call | solution.py:193
  158.1 10.4 %attention.1 = (bf16[256,1536]{1,0:T(8,128)(2,1)}, f32[2,6,256]{2,1,0:T(8,128)}) custom-call(s32[1]{0:T(128)} %bitcast.place_ref, s32[1280,1]{1,0:T(8,128)} %broadcast_in_dim.93.segment_key_ref, s32[1,256]{1,0:T(1,128)} %bitcast.296, bf16[256,1536]{1,0:T(8,128)(2,1)} %project.3.q_ref, bf16[1280,512]{1,0:T(8,128)(2,1)} %constant_dynamic-update-slice_fusion.2.kv_ref), custom_call_target="tpu_custom_call" | custom-call | flops 1000 | bytes 1000 | tf_op jit(solution)/shard_map/attention/pallas_call | solution.py:270
  168.5 14.1 %collective-permute-done.17 = bf16[4,96,768]{2,1,0:T(8,128)(2,1)S(1)} collective-permute-done((bf16[4,96,768]{2,1,0:T(8,128)(2,1)S(1)}, bf16[4,96,768]{2,1,0:T(8,128)(2,1)S(1)}, u32[]{:S(2)}, u32[]{:S(2)}) %collective-permute-start.17) | collective-permute-done | bytes 589856 | tf_op jit(solution)/shard_map/ppermute | solution.py:34
  182.6 4.5 collective-permute-done.18
  189.4 3.4 pad_maximum_fusion
  193.8 2.0 broadcast_select_fusion.1
  196.1 2.6 maximum_maximum_fusion.1
  198.7 3.8 multiply_reduce_fusion.1
  204.9 6.2 %collective-permute-start.23 = (bf16[256,1536]{1,0:T(8,128)(2,1)S(1)}, bf16[256,1536]{1,0:T(8,128)(2,1)}, u32[]{:S(2)}, u32[]{:S(2)}) collective-permute-start(bf16[256,1536]{1,0:T(8,128)(2,1)S(1)} %multiply_convert_fusion), channel_id=1, source_target_pairs={{0,4},{4,0},{1,5},{5,1},{2,6},{6,2},{3,7},{7,3},{8,12},{12,8},{9,1... | collective-permute-start | bytes 2359304 | tf_op jit(solution)/shard_map/ppermute | solution.py:34
  211.2 34.6 %all-gather.11.cloned.1.call-done = bf16[3072,384]{1,0:T(8,128)(2,1)} async-done(((bf16[768,384]{1,0:T(8,128)(2,1)}), bf16[3072,384]{1,0:T(8,128)(2,1)}) %all-gather.11.cloned.1.call-update) | async-done | bytes 2359312 | tf_op jit(solution)/shard_map/all_gather | solution.py:694
  245.7 3.1 pad_maximum_fusion.1
  255.5 20.6 %expert.3 = (bf16[2,512,1536]{2,1,0:T(8,128)(2,1)}, bf16[2,512,1536]{2,1,0:T(8,128)(2,1)}, bf16[512,1536]{1,0:T(8,128)(2,1)}, bf16[512,1536]{1,0:T(8,128)(2,1)},...) custom-call(s32[2,1,512]{2,1,0:T(1,128)} %select_n.419.slot_row_ref, ...), custom_call_target="tpu_custom_call" | custom-call | flops 1000 | bytes 1000 | tf_op jit(solution)/shard_map/expert/pallas_call | solution.py:500
  279.3 21.0 %expert.2 = (bf16[2,512,1536]{2,1,0:T(8,128)(2,1)}, bf16[2,512,1536]{2,1,0:T(8,128)(2,1)}, bf16[512,1536]{1,0:T(8,128)(2,1)}, bf16[512,1536]{1,0:T(8,128)(2,1)},...) custom-call(s32[2,1,512]{2,1,0:T(1,128)} %copy.125.slot_row_ref, ...), custom_call_target="tpu_custom_call" | custom-call | flops 1000 | bytes 1000 | tf_op jit(solution)/shard_map/expert/pallas_call | solution.py:500
  300.4 5.1 fusion.13
  311.5 16.6 %weight_grads.1 = (bf16[1536,2560]{1,0:T(8,128)(2,1)}, bf16[256,1536]{1,0:T(8,128)(2,1)}, bf16[256,1536]{1,0:T(8,128)(2,1)}, bf16[256,1536]{1,0:T(8,128)(2,1)}, bf16[256,1536]{1,0:T(8,128)(2,1)}) custom-call(bf16[512,1536]{1,0:T(8,128)(2,1)} %get-tuple-element.180.refs_0_, bf16[512,1536]{1,0:T(8,128)(2,1)} %get-tuple-element.181.refs_1_, ...), custom_call_target="tpu_custom_call" | custom-call | flops 15000000512 | bytes 50000000 | tf_op jit(solution)/shard_map/weight_grads/pallas_call | solution.py:600
  330.1 14.9 %collective-permute-done.30 = bf16[256,1536]{1,0:T(8,128)(2,1)} collective-permute-done((bf16[256,1536]{1,0:T(8,128)(2,1)}, bf16[256,1536]{1,0:T(8,128)(2,1)}, u32[]{:S(2)}, u32[]{:S(2)}) %collective-permute-start.30) | collective-permute-done | bytes 786464 | tf_op jit(solution)/shard_map/ppermute | solution.py:34
  345.0 2.3 multiply_reduce_fusion
  347.3 3.8 fusion.55
  351.1 2.4 copy.130
  354.7 2.2 convolution_convert_fusion.2
  360.4 4.7 convolution_convert_fusion.4.dout_ref
  365.1 16.9 %attention_back.1 = (bf16[256,1536]{1,0:T(8,128)(2,1)}, bf16[1024,512]{1,0:T(8,128)(2,1)}, f32[256,512]{1,0:T(8,128)}) custom-call(s32[1]{0:T(128)} %bitcast.place_ref, s32[1280,1]{1,0:T(8,128)} %broadcast_in_dim.93.segment_key_ref, s32[1,256]{1,0:T(1,128)} %bitcast.297, bf16[256,1536]{1,0:T(8,128)(2,1)} %project.3.q_ref, ...), custom_call_target="tpu_custom_call" | custom-call | flops 51999997952 | bytes 10000000 | tf_op jit(solution)/shard_map/attention_back/pallas_call | solution.py:359
  382.8 3.8 add_convert_fusion.1
  386.5 8.7 %collective-permute-done.35 = bf16[256,1536]{1,0:T(8,128)(2,1)} collective-permute-done((bf16[256,1536]{1,0:T(8,128)(2,1)}, bf16[256,1536]{1,0:T(8,128)(2,1)}, u32[]{:S(2)}, u32[]{:S(2)}) %collective-permute-start.35) | collective-permute-done | bytes 786464 | tf_op jit(solution)/shard_map/ppermute | solution.py:34
  395.2 2.2 convolution_convert_fusion
  402.3 3.6 dynamic-slice_bitcast_fusion.4
  410.2 2.3 add_convert_fusion
  412.6 3.0 collective-permute-done.36
  415.6 24.9 %collective-permute-done.37 = bf16[4,96,768]{2,1,0:T(8,128)(2,1)S(1)} collective-permute-done((bf16[4,96,768]{2,1,0:T(8,128)(2,1)S(1)}, bf16[4,96,768]{2,1,0:T(8,128)(2,1)S(1)}, u32[]{:S(2)}, u32[]{:S(2)}) %collective-permute-start.37) | collective-permute-done | bytes 589856 | tf_op jit(solution)/shard_map/ppermute | solution.py:34
  444.3 3.4 add_add_fusion
  447.7 1.9 dynamic-slice_bitcast_fusion
  451.1 3.2 collective-permute-start.44
  460.2 5.7 collective-permute-done.43
  465.8 7.8 %collective-permute-done.44 = bf16[4,96,768]{2,1,0:T(8,128)(2,1)} collective-permute-done((bf16[4,96,768]{2,1,0:T(8,128)(2,1)S(1)}, bf16[4,96,768]{2,1,0:T(8,128)(2,1)}, u32[]{:S(2)}, u32[]{:S(2)}) %collective-permute-start.44) | collective-permute-done | bytes 589856 | tf_op jit(solution)/shard_map/ppermute | solution.py:34
  473.6 12.3 %collective-permute-done.45 = bf16[4,96,768]{2,1,0:T(8,128)(2,1)} collective-permute-done((bf16[4,96,768]{2,1,0:T(8,128)(2,1)S(1)}, bf16[4,96,768]{2,1,0:T(8,128)(2,1)}, u32[]{:S(2)}, u32[]{:S(2)}) %collective-permute-start.45) | collective-permute-done | bytes 589856 | tf_op jit(solution)/shard_map/ppermute | solution.py:34
  487.2 4.5 reshape.417
  493.1 4.9 all-to-all-start.1
  499.8 3.3 collective-permute-start.55
  503.4 3.0 collective-permute-start.49
  508.8 19.3 %collective-permute-done.49 = bf16[4,96,256]{2,1,0:T(8,128)(2,1)S(1)} collective-permute-done((bf16[4,96,256]{2,1,0:T(8,128)(2,1)S(1)}, bf16[4,96,256]{2,1,0:T(8,128)(2,1)S(1)}, u32[]{:S(2)}, u32[]{:S(2)}) %collective-permute-start.49) | collective-permute-done | bytes 196640 | tf_op jit(solution)/shard_map/ppermute | solution.py:34
  532.2 2.3 collective-permute-start.51
  536.2 3.3 collective-permute-done.52
  539.5 12.4 %collective-permute-done.51 = bf16[96,1024]{1,0:T(8,128)(2,1)S(1)} collective-permute-done((bf16[96,1024]{1,0:T(8,128)(2,1)S(1)}, bf16[96,1024]{1,0:T(8,128)(2,1)S(1)}, u32[]{:S(2)}, u32[]{:S(2)}) %collective-permute-start.51) | collective-permute-done | bytes 196640 | tf_op jit(solution)/shard_map/ppermute | solution.py:89
  (321 shorter events, 122.0 us)
Async XLA Ops:
  8.8 5.0 collective-permute-start
  14.9 14.4 %collective-permute-start.1 = (bf16[96,2048]{1,0:T(8,128)(2,1)S(1)}, bf16[96,2048]{1,0:T(8,128)(2,1)}, u32[]{:S(2)}, u32[]{:S(2)}) collective-permute-start(bf16[96,2048]{1,0:T(8,128)(2,1)S(1)} %pad_maximum_fusion.7), channel_id=1, source_target_pairs={{0,8},{8,16},{16,24},{24,0},{1,9},{9,17},{17,25},{25,1},{2,10},{10... | collective-permute-start | bytes 1179656 | tf_op jit(solution)/shard_map/ppermute | solution.py:89
  17.0 27.0 %collective-permute-start.2 = (bf16[96,2048]{1,0:T(8,128)(2,1)S(1)}, bf16[96,2048]{1,0:T(8,128)(2,1)S(1)}, u32[]{:S(2)}, u32[]{:S(2)}) collective-permute-start(bf16[96,2048]{1,0:T(8,128)(2,1)S(1)} %pad_maximum_fusion.7), channel_id=1, source_target_pairs={{0,16},{8,24},{16,0},{24,8},{1,17},{9,25},{17,1},{25,9},{2,18},{10... | collective-permute-start | bytes 1179656 | tf_op jit(solution)/shard_map/ppermute | solution.py:89
  19.6 24.4 %collective-permute-start.3 = (bf16[96,2048]{1,0:T(8,128)(2,1)S(1)}, bf16[96,2048]{1,0:T(8,128)(2,1)S(1)}, u32[]{:S(2)}, u32[]{:S(2)}) collective-permute-start(bf16[96,2048]{1,0:T(8,128)(2,1)S(1)} %pad_maximum_fusion.7), channel_id=1, source_target_pairs={{0,24},{8,0},{16,8},{24,16},{1,25},{9,1},{17,9},{25,17},{2,26},{10... | collective-permute-start | bytes 1179656 | tf_op jit(solution)/shard_map/ppermute | solution.py:89
  23.7 26.6 %all-to-all-start = ((bf16[8,3,96,384]{3,2,1,0:T(8,128)(2,1)}), bf16[8,3,96,384]{3,2,1,0:T(8,128)(2,1)}, u32[]{:S(2)}, u32[]{:S(2)}) async-start(bf16[8,3,96,384]{3,2,1,0:T(8,128)(2,1)} %maximum_bitcast_fusion), calls=%async_computation | async-start | bytes 3538944 | tf_op jit(solution)/shard_map/all_to_all | solution.py:667
  28.0 78.7 %all-gather.7.cloned.1.call-start = ((), (), s32[]{:S(2)}) async-start(), calls=%async_computation.4 | async-start | bytes 2949120 | tf_op jit(solution)/shard_map/all_gather | solution.py:694
  54.7 144.1 %all-gather.9.cloned.1.call-start = ((), (), s32[]{:S(2)}) async-start(), calls=%async_computation.5 | async-start | bytes 2949120 | tf_op jit(solution)/shard_map/all_gather | solution.py:694
  56.8 12.0 %collective-permute-start.7 = (bf16[4,96,512]{2,1,0:T(8,128)(2,1)S(1)}, bf16[4,96,512]{2,1,0:T(8,128)(2,1)S(1)}, u32[]{:S(2)}, u32[]{:S(2)}) collective-permute-start(bf16[4,96,512]{2,1,0:T(8,128)(2,1)S(1)} %slice.138), channel_id=1, source_target_pairs={{0,4},{4,0},{1,5},{5,1},{2,6},{6,2},{3,7},{7,3},{8,12},{12,8},{9,1... | collective-permute-start | bytes 1179656 | tf_op jit(solution)/shard_map/ppermute | solution.py:34
  60.6 39.5 %collective-permute-start.4 = (bf16[4,96,768]{2,1,0:T(8,128)(2,1)}, bf16[4,96,768]{2,1,0:T(8,128)(2,1)}, u32[]{:S(2)}, u32[]{:S(2)}) collective-permute-start(bf16[4,96,768]{2,1,0:T(8,128)(2,1)} %get-tuple-element.132), channel_id=1, source_target_pairs={{0,1},{1,0},{2,3},{3,2},{4,5},{5,4},{6,7},{7,6},{8,9},{9,8},{10,11... | collective-permute-start | bytes 1769480 | tf_op jit(solution)/shard_map/ppermute | solution.py:34
  61.3 38.8 %collective-permute-start.5 = (bf16[4,96,768]{2,1,0:T(8,128)(2,1)}, bf16[4,96,768]{2,1,0:T(8,128)(2,1)}, u32[]{:S(2)}, u32[]{:S(2)}) collective-permute-start(bf16[4,96,768]{2,1,0:T(8,128)(2,1)} %get-tuple-element.132), channel_id=1, source_target_pairs={{0,4},{4,0},{1,5},{5,1},{2,6},{6,2},{3,7},{7,3},{8,12},{12,8},{9,1... | collective-permute-start | bytes 1769480 | tf_op jit(solution)/shard_map/ppermute | solution.py:34
  62.8 37.3 %collective-permute-start.6 = (bf16[4,96,768]{2,1,0:T(8,128)(2,1)}, bf16[4,96,768]{2,1,0:T(8,128)(2,1)}, u32[]{:S(2)}, u32[]{:S(2)}) collective-permute-start(bf16[4,96,768]{2,1,0:T(8,128)(2,1)} %get-tuple-element.132), channel_id=1, source_target_pairs={{0,5},{1,4},{4,1},{5,0},{2,7},{3,6},{6,3},{7,2},{8,13},{9,12},{12,... | collective-permute-start | bytes 1769480 | tf_op jit(solution)/shard_map/ppermute | solution.py:34
  64.1 23.4 %collective-permute-start.12 = (s32[512]{0:T(512)}, s32[512]{0:T(512)}, u32[]{:S(2)}, u32[]{:S(2)}) collective-permute-start(s32[512]{0:T(512)} %param.24), channel_id=1, source_target_pairs={{0,2},{2,4},{4,6},{6,8},{8,10},{10,12},{12,14},{14,16},{16,18},{18... | collective-permute-start | bytes 6152 | tf_op jit(solution)/shard_map/ppermute | solution.py:29
  69.0 9.4 %collective-permute-start.8 = (bf16[4,2,96,512]{3,2,1,0:T(8,128)(2,1)S(1)}, bf16[4,2,96,512]{3,2,1,0:T(8,128)(2,1)}, u32[]{:S(2)}, u32[]{:S(2)}) collective-permute-start(bf16[4,2,96,512]{3,2,1,0:T(8,128)(2,1)S(1)} %pad_maximum_fusion.5), channel_id=1, source_target_pairs={{0,2},{2,0},{1,3},{3,1},{4,6},{6,4},{5,7},{7,5},{8,10},{10,8},{9,1... | collective-permute-start | bytes 2359304 | tf_op jit(solution)/shard_map/ppermute | solution.py:34
  78.4 15.6 %collective-permute-start.11 = (s32[512]{0:T(512)}, s32[512]{0:T(512)S(1)}, u32[]{:S(2)}, u32[]{:S(2)}) collective-permute-start(s32[512]{0:T(512)} %param.24), channel_id=1, source_target_pairs={{0,4},{2,6},{4,8},{6,10},{8,12},{10,14},{12,16},{14,18},{16,20},{1... | collective-permute-start | bytes 6152 | tf_op jit(solution)/shard_map/ppermute | solution.py:29
  87.6 12.6 %collective-permute-start.9 = (bf16[256,512]{1,0:T(8,128)(2,1)}, bf16[256,512]{1,0:T(8,128)(2,1)}, u32[]{:S(2)}, u32[]{:S(2)}) collective-permute-start(bf16[256,512]{1,0:T(8,128)(2,1)} %project.2), channel_id=1, source_target_pairs={{0,2},{2,4},{4,6},{6,8},{8,10},{10,12},{12,14},{14,16},{16,18},{18... | collective-permute-start | bytes 786440 | tf_op jit(solution)/shard_map/ppermute | solution.py:29
  94.0 10.7 %collective-permute-start.10 = (bf16[256,512]{1,0:T(8,128)(2,1)}, bf16[256,512]{1,0:T(8,128)(2,1)}, u32[]{:S(2)}, u32[]{:S(2)}) collective-permute-start(bf16[256,512]{1,0:T(8,128)(2,1)} %project.2), channel_id=1, source_target_pairs={{0,4},{2,6},{4,8},{6,10},{8,12},{10,14},{12,16},{14,18},{16,20},{1... | collective-permute-start | bytes 786440 | tf_op jit(solution)/shard_map/ppermute | solution.py:29
  108.6 23.6 %collective-permute-start.13 = (bf16[2,2,4,96,768]{4,3,2,1,0:T(8,128)(2,1)S(1)}, bf16[2,2,4,96,768]{4,3,2,1,0:T(8,128)(2,1)}, u32[]{:S(2)}, u32[]{:S(2)}) collective-permute-start(bf16[2,2,4,96,768]{4,3,2,1,0:T(8,128)(2,1)S(1)} %bitcast.265), channel_id=1, source_target_pairs={{0,2},{2,0},{1,3},{3,1},{4,6},{6,4},{5,7},{7,5},{8,10},{10,8},{9,1... | collective-permute-start | bytes 7077896 | tf_op jit(solution)/shard_map/ppermute | solution.py:34
  110.7 15.0 %collective-permute-start.14 = (bf16[2,256,512]{2,1,0:T(8,128)(2,1)}, bf16[2,256,512]{2,1,0:T(8,128)(2,1)}, u32[]{:S(2)}, u32[]{:S(2)}) collective-permute-start(bf16[2,256,512]{2,1,0:T(8,128)(2,1)} %maximum_select_fusion), channel_id=1, source_target_pairs={{0,1},{1,0},{2,3},{3,2},{4,5},{5,4},{6,7},{7,6},{8,9},{9,8},{10,11... | collective-permute-start | bytes 1572872 | tf_op jit(solution)/shard_map/ppermute | solution.py:34
  112.2 26.2 %collective-permute-start.15 = (bf16[4,96,768]{2,1,0:T(8,128)(2,1)}, bf16[4,96,768]{2,1,0:T(8,128)(2,1)}, u32[]{:S(2)}, u32[]{:S(2)}) collective-permute-start(bf16[4,96,768]{2,1,0:T(8,128)(2,1)} %get-tuple-element.142), channel_id=1, source_target_pairs={{0,1},{1,0},{2,3},{3,2},{4,5},{5,4},{6,7},{7,6},{8,9},{9,8},{10,11... | collective-permute-start | bytes 1769480 | tf_op jit(solution)/shard_map/ppermute | solution.py:34
  112.7 55.7 %collective-permute-start.16 = (bf16[4,96,768]{2,1,0:T(8,128)(2,1)}, bf16[4,96,768]{2,1,0:T(8,128)(2,1)}, u32[]{:S(2)}, u32[]{:S(2)}) collective-permute-start(bf16[4,96,768]{2,1,0:T(8,128)(2,1)} %get-tuple-element.142), channel_id=1, source_target_pairs={{0,4},{4,0},{1,5},{5,1},{2,6},{6,2},{3,7},{7,3},{8,12},{12,8},{9,1... | collective-permute-start | bytes 1769480 | tf_op jit(solution)/shard_map/ppermute | solution.py:34
  119.2 126.5 %all-gather.11.cloned.1.call-start = ((), (), s32[]{:S(2)}) async-start(), calls=%async_computation.6 | async-start | bytes 2949120 | tf_op jit(solution)/shard_map/all_gather | solution.py:694
  121.2 65.9 %collective-permute-start.18 = (bf16[256,1664]{1,0:T(8,128)(2,1)}, bf16[256,1664]{1,0:T(8,128)(2,1)}, u32[]{:S(2)}, u32[]{:S(2)}) collective-permute-start(bf16[256,1664]{1,0:T(8,128)(2,1)} %fusion.9), channel_id=1, source_target_pairs={{0,1},{1,0},{2,3},{3,2},{4,5},{5,4},{6,7},{7,6},{8,9},{9,8},{10,11... | collective-permute-start | bytes 2555912 | tf_op jit(solution)/shard_map/ppermute | solution.py:34
  125.7 61.4 %collective-permute-start.19 = (bf16[256,1664]{1,0:T(8,128)(2,1)}, bf16[256,1664]{1,0:T(8,128)(2,1)}, u32[]{:S(2)}, u32[]{:S(2)}) collective-permute-start(bf16[256,1664]{1,0:T(8,128)(2,1)} %fusion.9), channel_id=1, source_target_pairs={{0,4},{4,0},{1,5},{5,1},{2,6},{6,2},{3,7},{7,3},{8,12},{12,8},{9,1... | collective-permute-start | bytes 2555912 | tf_op jit(solution)/shard_map/ppermute | solution.py:34
  132.3 54.9 %collective-permute-start.20 = (bf16[256,1664]{1,0:T(8,128)(2,1)}, bf16[256,1664]{1,0:T(8,128)(2,1)}, u32[]{:S(2)}, u32[]{:S(2)}) collective-permute-start(bf16[256,1664]{1,0:T(8,128)(2,1)} %fusion.9), channel_id=1, source_target_pairs={{0,5},{1,4},{4,1},{5,0},{2,7},{3,6},{6,3},{7,2},{8,13},{9,12},{12,... | collective-permute-start | bytes 2555912 | tf_op jit(solution)/shard_map/ppermute | solution.py:34
  138.4 44.2 %collective-permute-start.17 = (bf16[4,96,768]{2,1,0:T(8,128)(2,1)S(1)}, bf16[4,96,768]{2,1,0:T(8,128)(2,1)S(1)}, u32[]{:S(2)}, u32[]{:S(2)}) collective-permute-start(bf16[4,96,768]{2,1,0:T(8,128)(2,1)S(1)} %copy-done.12), channel_id=1, source_target_pairs={{0,5},{1,4},{4,1},{5,0},{2,7},{3,6},{6,3},{7,2},{8,13},{9,12},{12,... | collective-permute-start | bytes 1769480 | tf_op jit(solution)/shard_map/ppermute | solution.py:34
  189.0 4.7 collective-permute-start.21
  189.1 298.0 %reduce-scatter.2.cloned.1.call-start = ((), (), s32[]{:S(2)}) async-start(), calls=%async_computation.3 | async-start | bytes 9830400 | tf_op jit(solution)/shard_map/reduce_scatter | solution.py:807
  192.8 58.3 %collective-permute-start.25 = (bf16[2,2,256,1664]{3,2,1,0:T(8,128)(2,1)}, bf16[2,2,256,1664]{3,2,1,0:T(8,128)(2,1)}, u32[]{:S(2)}, u32[]{:S(2)}) collective-permute-start(bf16[2,2,256,1664]{3,2,1,0:T(8,128)(2,1)} %bitcast.66), channel_id=1, source_target_pairs={{0,2},{2,0},{1,3},{3,1},{4,6},{6,4},{5,7},{7,5},{8,10},{10,8},{9,1... | collective-permute-start | bytes 10223624 | tf_op jit(solution)/shard_map/ppermute | solution.py:34
  203.2 45.7 %copy-start.40 = (f32[256]{0:T(256)}, f32[256]{0:T(256)S(1)}, u32[]{:S(2)}) copy-start(f32[256]{0:T(256)S(1)} %get-tuple-element.363) | copy-start | bytes 3076
  203.4 42.4 %collective-permute-start.22 = (bf16[256,1536]{1,0:T(8,128)(2,1)S(1)}, bf16[256,1536]{1,0:T(8,128)(2,1)}, u32[]{:S(2)}, u32[]{:S(2)}) collective-permute-start(bf16[256,1536]{1,0:T(8,128)(2,1)S(1)} %multiply_convert_fusion), channel_id=1, source_target_pairs={{0,1},{1,0},{2,3},{3,2},{4,5},{5,4},{6,7},{7,6},{8,9},{9,8},{10,11... | collective-permute-start | bytes 2359304 | tf_op jit(solution)/shard_map/ppermute | solution.py:34
  204.9 40.8 %collective-permute-start.23 = (bf16[256,1536]{1,0:T(8,128)(2,1)S(1)}, bf16[256,1536]{1,0:T(8,128)(2,1)}, u32[]{:S(2)}, u32[]{:S(2)}) collective-permute-start(bf16[256,1536]{1,0:T(8,128)(2,1)S(1)} %multiply_convert_fusion), channel_id=1, source_target_pairs={{0,4},{4,0},{1,5},{5,1},{2,6},{6,2},{3,7},{7,3},{8,12},{12,8},{9,1... | collective-permute-start | bytes 2359304 | tf_op jit(solution)/shard_map/ppermute | solution.py:34
  211.2 34.6 %collective-permute-start.24 = (bf16[256,1536]{1,0:T(8,128)(2,1)S(1)}, bf16[256,1536]{1,0:T(8,128)(2,1)}, u32[]{:S(2)}, u32[]{:S(2)}) collective-permute-start(bf16[256,1536]{1,0:T(8,128)(2,1)S(1)} %multiply_convert_fusion), channel_id=1, source_target_pairs={{0,5},{1,4},{4,1},{5,0},{2,7},{3,6},{6,3},{7,2},{8,13},{9,12},{12,... | collective-permute-start | bytes 2359304 | tf_op jit(solution)/shard_map/ppermute | solution.py:34
  248.9 6.6 %collective-permute-start.26 = (bf16[2,2,256,1536]{3,2,1,0:T(8,128)(2,1)}, bf16[2,2,256,1536]{3,2,1,0:T(8,128)(2,1)}, u32[]{:S(2)}, u32[]{:S(2)}) collective-permute-start(bf16[2,2,256,1536]{3,2,1,0:T(8,128)(2,1)} %bitcast.85), channel_id=1, source_target_pairs={{0,2},{2,0},{1,3},{3,1},{4,6},{6,4},{5,7},{7,5},{8,10},{10,8},{9,1... | collective-permute-start | bytes 9437192 | tf_op jit(solution)/shard_map/ppermute | solution.py:34
  276.1 24.3 %collective-permute-start.27 = (bf16[4,256,1536]{2,1,0:T(8,128)(2,1)}, bf16[4,256,1536]{2,1,0:T(8,128)(2,1)}, u32[]{:S(2)}, u32[]{:S(2)}) collective-permute-start(bf16[4,256,1536]{2,1,0:T(8,128)(2,1)} %bitcast.301), channel_id=1, source_target_pairs={{0,2},{2,0},{1,3},{3,1},{4,6},{6,4},{5,7},{7,5},{8,10},{10,8},{9,1... | collective-permute-start | bytes 9437192 | tf_op jit(solution)/shard_map/ppermute | solution.py:34
  305.5 6.0 %collective-permute-start.31 = (bf16[4,256,1536]{2,1,0:T(8,128)(2,1)}, bf16[4,256,1536]{2,1,0:T(8,128)(2,1)}, u32[]{:S(2)}, u32[]{:S(2)}) collective-permute-start(bf16[4,256,1536]{2,1,0:T(8,128)(2,1)} %bitcast.93), channel_id=1, source_target_pairs={{0,2},{2,0},{1,3},{3,1},{4,6},{6,4},{5,7},{7,5},{8,10},{10,8},{9,1... | collective-permute-start | bytes 9437192 | tf_op jit(solution)/shard_map/ppermute | solution.py:34
  306.7 23.4 %collective-permute-start.28 = (bf16[256,1536]{1,0:T(8,128)(2,1)}, bf16[256,1536]{1,0:T(8,128)(2,1)}, u32[]{:S(2)}, u32[]{:S(2)}) collective-permute-start(bf16[256,1536]{1,0:T(8,128)(2,1)} %get-tuple-element.177), channel_id=1, source_target_pairs={{0,1},{1,0},{2,3},{3,2},{4,5},{5,4},{6,7},{7,6},{8,9},{9,8},{10,11... | collective-permute-start | bytes 2359304 | tf_op jit(solution)/shard_map/ppermute | solution.py:34
  308.2 21.9 %collective-permute-start.29 = (bf16[256,1536]{1,0:T(8,128)(2,1)}, bf16[256,1536]{1,0:T(8,128)(2,1)}, u32[]{:S(2)}, u32[]{:S(2)}) collective-permute-start(bf16[256,1536]{1,0:T(8,128)(2,1)} %get-tuple-element.178), channel_id=1, source_target_pairs={{0,4},{4,0},{1,5},{5,1},{2,6},{6,2},{3,7},{7,3},{8,12},{12,8},{9,1... | collective-permute-start | bytes 2359304 | tf_op jit(solution)/shard_map/ppermute | solution.py:34
  309.8 35.2 %collective-permute-start.30 = (bf16[256,1536]{1,0:T(8,128)(2,1)}, bf16[256,1536]{1,0:T(8,128)(2,1)}, u32[]{:S(2)}, u32[]{:S(2)}) collective-permute-start(bf16[256,1536]{1,0:T(8,128)(2,1)} %get-tuple-element.179), channel_id=1, source_target_pairs={{0,5},{1,4},{4,1},{5,0},{2,7},{3,6},{6,3},{7,2},{8,13},{9,12},{12,... | collective-permute-start | bytes 2359304 | tf_op jit(solution)/shard_map/ppermute | solution.py:34
  356.9 25.9 %collective-permute-start.32 = (bf16[768,1536]{1,0:T(8,128)(2,1)}, bf16[768,1536]{1,0:T(8,128)(2,1)}, u32[]{:S(2)}, u32[]{:S(2)}) collective-permute-start(bf16[768,1536]{1,0:T(8,128)(2,1)} %convolution_convert_fusion.2), channel_id=1, source_target_pairs={{0,2},{2,0},{1,3},{3,1},{4,6},{6,4},{5,7},{7,5},{8,10},{10,8},{9,1... | collective-permute-start | bytes 7077896 | tf_op jit(solution)/shard_map/ppermute | solution.py:34
  356.9 29.6 %collective-permute-start.33 = (bf16[256,1536]{1,0:T(8,128)(2,1)}, bf16[256,1536]{1,0:T(8,128)(2,1)}, u32[]{:S(2)}, u32[]{:S(2)}) collective-permute-start(bf16[256,1536]{1,0:T(8,128)(2,1)} %get-tuple-element.205), channel_id=1, source_target_pairs={{0,1},{1,0},{2,3},{3,2},{4,5},{5,4},{6,7},{7,6},{8,9},{9,8},{10,11... | collective-permute-start | bytes 2359304 | tf_op jit(solution)/shard_map/ppermute | solution.py:34
  358.4 28.2 %collective-permute-start.34 = (bf16[256,1536]{1,0:T(8,128)(2,1)}, bf16[256,1536]{1,0:T(8,128)(2,1)}, u32[]{:S(2)}, u32[]{:S(2)}) collective-permute-start(bf16[256,1536]{1,0:T(8,128)(2,1)} %get-tuple-element.206), channel_id=1, source_target_pairs={{0,4},{4,0},{1,5},{5,1},{2,6},{6,2},{3,7},{7,3},{8,12},{12,8},{9,1... | collective-permute-start | bytes 2359304 | tf_op jit(solution)/shard_map/ppermute | solution.py:34
  360.0 35.2 %collective-permute-start.35 = (bf16[256,1536]{1,0:T(8,128)(2,1)}, bf16[256,1536]{1,0:T(8,128)(2,1)}, u32[]{:S(2)}, u32[]{:S(2)}) collective-permute-start(bf16[256,1536]{1,0:T(8,128)(2,1)} %get-tuple-element.207), channel_id=1, source_target_pairs={{0,5},{1,4},{4,1},{5,0},{2,7},{3,6},{6,3},{7,2},{8,13},{9,12},{12,... | collective-permute-start | bytes 2359304 | tf_op jit(solution)/shard_map/ppermute | solution.py:34
  397.4 12.8 %collective-permute-start.40 = (bf16[768,1536]{1,0:T(8,128)(2,1)}, bf16[768,1536]{1,0:T(8,128)(2,1)}, u32[]{:S(2)}, u32[]{:S(2)}) collective-permute-start(bf16[768,1536]{1,0:T(8,128)(2,1)} %convolution_convert_fusion), channel_id=1, source_target_pairs={{0,2},{2,0},{1,3},{3,1},{4,6},{6,4},{5,7},{7,5},{8,10},{10,8},{9,1... | collective-permute-start | bytes 7077896 | tf_op jit(solution)/shard_map/ppermute | solution.py:34
  400.8 14.8 %collective-permute-start.36 = (bf16[2,256,512]{2,1,0:T(8,128)(2,1)S(1)}, bf16[2,256,512]{2,1,0:T(8,128)(2,1)S(1)}, u32[]{:S(2)}, u32[]{:S(2)}) collective-permute-start(bf16[2,256,512]{2,1,0:T(8,128)(2,1)S(1)} %pad_maximum_fusion.6), channel_id=1, source_target_pairs={{0,1},{1,0},{2,3},{3,2},{4,5},{5,4},{6,7},{7,6},{8,9},{9,8},{10,11... | collective-permute-start | bytes 1572872 | tf_op jit(solution)/shard_map/ppermute | solution.py:34
  405.9 34.5 %collective-permute-start.37 = (bf16[4,96,768]{2,1,0:T(8,128)(2,1)S(1)}, bf16[4,96,768]{2,1,0:T(8,128)(2,1)S(1)}, u32[]{:S(2)}, u32[]{:S(2)}) collective-permute-start(bf16[4,96,768]{2,1,0:T(8,128)(2,1)S(1)} %get-tuple-element.290), channel_id=1, source_target_pairs={{0,1},{1,0},{2,3},{3,2},{4,5},{5,4},{6,7},{7,6},{8,9},{9,8},{10,11... | collective-permute-start | bytes 1769480 | tf_op jit(solution)/shard_map/ppermute | solution.py:34
  406.5 34.0 %collective-permute-start.38 = (bf16[4,96,768]{2,1,0:T(8,128)(2,1)S(1)}, bf16[4,96,768]{2,1,0:T(8,128)(2,1)S(1)}, u32[]{:S(2)}, u32[]{:S(2)}) collective-permute-start(bf16[4,96,768]{2,1,0:T(8,128)(2,1)S(1)} %get-tuple-element.289), channel_id=1, source_target_pairs={{0,4},{4,0},{1,5},{5,1},{2,6},{6,2},{3,7},{7,3},{8,12},{12,8},{9,1... | collective-permute-start | bytes 1769480 | tf_op jit(solution)/shard_map/ppermute | solution.py:34
  408.2 32.3 %collective-permute-start.39 = (bf16[4,96,768]{2,1,0:T(8,128)(2,1)S(1)}, bf16[4,96,768]{2,1,0:T(8,128)(2,1)S(1)}, u32[]{:S(2)}, u32[]{:S(2)}) collective-permute-start(bf16[4,96,768]{2,1,0:T(8,128)(2,1)S(1)} %get-tuple-element.288), channel_id=1, source_target_pairs={{0,5},{1,4},{4,1},{5,0},{2,7},{3,6},{6,3},{7,2},{8,13},{9,12},{12,... | collective-permute-start | bytes 1769480 | tf_op jit(solution)/shard_map/ppermute | solution.py:34
  441.7 12.7 %collective-permute-start.42 = (bf16[256,512]{1,0:T(8,128)(2,1)S(1)}, bf16[256,512]{1,0:T(8,128)(2,1)S(1)}, u32[]{:S(2)}, u32[]{:S(2)}) collective-permute-start(bf16[256,512]{1,0:T(8,128)(2,1)S(1)} %get-tuple-element.309), channel_id=1, source_target_pairs={{4,0},{6,2},{8,4},{10,6},{12,8},{14,10},{16,12},{18,14},{20,16},{2... | collective-permute-start | bytes 786440 | tf_op jit(solution)/shard_map/ppermute | solution.py:29
  443.0 11.4 %collective-permute-start.41 = (bf16[256,512]{1,0:T(8,128)(2,1)S(1)}, bf16[256,512]{1,0:T(8,128)(2,1)S(1)}, u32[]{:S(2)}, u32[]{:S(2)}) collective-permute-start(bf16[256,512]{1,0:T(8,128)(2,1)S(1)} %get-tuple-element.308), channel_id=1, source_target_pairs={{2,0},{4,2},{6,4},{8,6},{10,8},{12,10},{14,12},{16,14},{18,16},{20... | collective-permute-start | bytes 786440 | tf_op jit(solution)/shard_map/ppermute | solution.py:29
  449.6 16.2 %collective-permute-start.43 = (bf16[4,96,768]{2,1,0:T(8,128)(2,1)S(1)}, bf16[4,96,768]{2,1,0:T(8,128)(2,1)}, u32[]{:S(2)}, u32[]{:S(2)}) collective-permute-start(bf16[4,96,768]{2,1,0:T(8,128)(2,1)S(1)} %get-tuple-element.286), channel_id=1, source_target_pairs={{0,1},{1,0},{2,3},{3,2},{4,5},{5,4},{6,7},{7,6},{8,9},{9,8},{10,11... | collective-permute-start | bytes 1769480 | tf_op jit(solution)/shard_map/ppermute | solution.py:34
  451.1 22.5 %collective-permute-start.44 = (bf16[4,96,768]{2,1,0:T(8,128)(2,1)S(1)}, bf16[4,96,768]{2,1,0:T(8,128)(2,1)}, u32[]{:S(2)}, u32[]{:S(2)}) collective-permute-start(bf16[4,96,768]{2,1,0:T(8,128)(2,1)S(1)} %get-tuple-element.285), channel_id=1, source_target_pairs={{0,4},{4,0},{1,5},{5,1},{2,6},{6,2},{3,7},{7,3},{8,12},{12,8},{9,1... | collective-permute-start | bytes 1769480 | tf_op jit(solution)/shard_map/ppermute | solution.py:34
  454.4 31.5 %collective-permute-start.45 = (bf16[4,96,768]{2,1,0:T(8,128)(2,1)S(1)}, bf16[4,96,768]{2,1,0:T(8,128)(2,1)}, u32[]{:S(2)}, u32[]{:S(2)}) collective-permute-start(bf16[4,96,768]{2,1,0:T(8,128)(2,1)S(1)} %get-tuple-element.284), channel_id=1, source_target_pairs={{0,5},{1,4},{4,1},{5,0},{2,7},{3,6},{6,3},{7,2},{8,13},{9,12},{12,... | collective-permute-start | bytes 1769480 | tf_op jit(solution)/shard_map/ppermute | solution.py:34
  456.0 29.9 %collective-permute-start.46 = (bf16[768,512]{1,0:T(8,128)(2,1)S(1)}, bf16[768,512]{1,0:T(8,128)(2,1)S(1)}, u32[]{:S(2)}, u32[]{:S(2)}) collective-permute-start(bf16[768,512]{1,0:T(8,128)(2,1)S(1)} %convolution_convert_fusion.5), channel_id=1, source_target_pairs={{0,2},{2,0},{1,3},{3,1},{4,6},{6,4},{5,7},{7,5},{8,10},{10,8},{9,1... | collective-permute-start | bytes 2359304 | tf_op jit(solution)/shard_map/ppermute | solution.py:34
  493.1 60.4 %all-to-all-start.1 = ((bf16[8,96,1280]{2,1,0:T(8,128)(2,1)}), bf16[8,96,1280]{2,1,0:T(8,128)(2,1)S(1)}, u32[]{:S(2)}, u32[]{:S(2)}) async-start(bf16[8,96,1280]{2,1,0:T(8,128)(2,1)} %bitcast.269), calls=%async_computation.2 | async-start | bytes 3932160 | tf_op jit(solution)/shard_map/all_to_all | solution.py:861
  499.7 34.8 %collective-permute-start.56 = (bf16[96,768]{1,0:T(8,128)(2,1)S(1)}, bf16[96,768]{1,0:T(8,128)(2,1)S(1)}, u32[]{:S(2)}, u32[]{:S(2)}) collective-permute-start(bf16[96,768]{1,0:T(8,128)(2,1)S(1)} %get-tuple-element.337), channel_id=1, source_target_pairs={{0,24},{8,0},{16,8},{24,16},{1,25},{9,1},{17,9},{25,17},{2,26},{10... | collective-permute-start | bytes 442376 | tf_op jit(solution)/shard_map/ppermute | solution.py:89
  499.8 35.1 %collective-permute-start.55 = (bf16[96,768]{1,0:T(8,128)(2,1)S(1)}, bf16[96,768]{1,0:T(8,128)(2,1)S(1)}, u32[]{:S(2)}, u32[]{:S(2)}) collective-permute-start(bf16[96,768]{1,0:T(8,128)(2,1)S(1)} %get-tuple-element.338), channel_id=1, source_target_pairs={{0,16},{8,24},{16,0},{24,8},{1,17},{9,25},{17,1},{25,9},{2,18},{10... | collective-permute-start | bytes 442376 | tf_op jit(solution)/shard_map/ppermute | solution.py:89
  503.4 24.7 %collective-permute-start.49 = (bf16[4,96,256]{2,1,0:T(8,128)(2,1)S(1)}, bf16[4,96,256]{2,1,0:T(8,128)(2,1)S(1)}, u32[]{:S(2)}, u32[]{:S(2)}) collective-permute-start(bf16[4,96,256]{2,1,0:T(8,128)(2,1)S(1)} %get-tuple-element.328), channel_id=1, source_target_pairs={{0,5},{1,4},{4,1},{5,0},{2,7},{3,6},{6,3},{7,2},{8,13},{9,12},{12,... | collective-permute-start | bytes 589832 | tf_op jit(solution)/shard_map/ppermute | solution.py:34
  506.4 24.5 %collective-permute-start.48 = (bf16[4,96,256]{2,1,0:T(8,128)(2,1)S(1)}, bf16[4,96,256]{2,1,0:T(8,128)(2,1)S(1)}, u32[]{:S(2)}, u32[]{:S(2)}) collective-permute-start(bf16[4,96,256]{2,1,0:T(8,128)(2,1)S(1)} %get-tuple-element.329), channel_id=1, source_target_pairs={{0,4},{4,0},{1,5},{5,1},{2,6},{6,2},{3,7},{7,3},{8,12},{12,8},{9,1... | collective-permute-start | bytes 589832 | tf_op jit(solution)/shard_map/ppermute | solution.py:34
  506.9 24.0 %collective-permute-start.47 = (bf16[4,96,256]{2,1,0:T(8,128)(2,1)S(1)}, bf16[4,96,256]{2,1,0:T(8,128)(2,1)S(1)}, u32[]{:S(2)}, u32[]{:S(2)}) collective-permute-start(bf16[4,96,256]{2,1,0:T(8,128)(2,1)S(1)} %get-tuple-element.327), channel_id=1, source_target_pairs={{0,1},{1,0},{2,3},{3,2},{4,5},{5,4},{6,7},{7,6},{8,9},{9,8},{10,11... | collective-permute-start | bytes 589832 | tf_op jit(solution)/shard_map/ppermute | solution.py:34
  528.1 7.4 %collective-permute-start.54 = (bf16[96,768]{1,0:T(8,128)(2,1)S(1)}, bf16[96,768]{1,0:T(8,128)(2,1)S(1)}, u32[]{:S(2)}, u32[]{:S(2)}) collective-permute-start(bf16[96,768]{1,0:T(8,128)(2,1)S(1)} %get-tuple-element.336), channel_id=1, source_target_pairs={{0,8},{8,16},{16,24},{24,0},{1,9},{9,17},{17,25},{25,1},{2,10},{10... | collective-permute-start | bytes 442376 | tf_op jit(solution)/shard_map/ppermute | solution.py:89
  531.2 8.4 %collective-permute-start.52 = (bf16[96,1024]{1,0:T(8,128)(2,1)S(1)}, bf16[96,1024]{1,0:T(8,128)(2,1)S(1)}, u32[]{:S(2)}, u32[]{:S(2)}) collective-permute-start(bf16[96,1024]{1,0:T(8,128)(2,1)S(1)} %get-tuple-element.326), channel_id=1, source_target_pairs={{0,24},{8,0},{16,8},{24,16},{1,25},{9,1},{17,9},{25,17},{2,26},{10... | collective-permute-start | bytes 589832 | tf_op jit(solution)/shard_map/ppermute | solution.py:89
  532.2 19.7 %collective-permute-start.51 = (bf16[96,1024]{1,0:T(8,128)(2,1)S(1)}, bf16[96,1024]{1,0:T(8,128)(2,1)S(1)}, u32[]{:S(2)}, u32[]{:S(2)}) collective-permute-start(bf16[96,1024]{1,0:T(8,128)(2,1)S(1)} %get-tuple-element.325), channel_id=1, source_target_pairs={{0,16},{8,24},{16,0},{24,8},{1,17},{9,25},{17,1},{25,9},{2,18},{10... | collective-permute-start | bytes 589832 | tf_op jit(solution)/shard_map/ppermute | solution.py:89
  534.5 17.4 %collective-permute-start.50 = (bf16[96,1024]{1,0:T(8,128)(2,1)S(1)}, bf16[96,1024]{1,0:T(8,128)(2,1)S(1)}, u32[]{:S(2)}, u32[]{:S(2)}) collective-permute-start(bf16[96,1024]{1,0:T(8,128)(2,1)S(1)} %get-tuple-element.324), channel_id=1, source_target_pairs={{0,8},{8,16},{16,24},{24,0},{1,9},{9,17},{17,25},{25,1},{2,10},{10... | collective-permute-start | bytes 589832 | tf_op jit(solution)/shard_map/ppermute | solution.py:89
  555.9 7.1 %collective-permute-start.53 = (f32[48,2]{0,1:T(2,128)S(1)}, f32[48,2]{0,1:T(2,128)S(1)}, u32[]{:S(2)}, u32[]{:S(2)}) collective-permute-start(f32[48,2]{0,1:T(2,128)S(1)} %constant_dynamic-slice_fusion.3), channel_id=1, source_target_pairs={{0,1},{1,0},{2,3},{3,2},{4,5},{5,4},{6,7},{7,6},{8,9},{9,8},{10,11... | collective-permute-start | bytes 1160 | tf_op jit(solution)/shard_map/ppermute | solution.py:34
  (47 other events, 390.9 us)
Sparse Core Ops, SparseCore 0:
  54.8 51.8 all-gather.6
  119.3 51.7 all-gather.8
  189.3 56.4 all-gather.10
  328.3 144.3 reduce-scatter.1

commit v3 on v2

--- a/solution.py
+++ b/solution.py
@@ -846,11 +846,11 @@
         grad_key_value.append(grad_own[:, start + HEAD_SIZE : start + 2 * HEAD_SIZE])
     grad_key_value_pre = jnp.concatenate(grad_key_value, axis=1).astype(BF16)
     key_value_total = fold_columns(normed_in, grad_key_value_pre, shard_rows)
-    key_value_total, expert_sum = lax.optimization_barrier((key_value_total, expert_sum))
     key_value_parts = fold_plane(distance_blocks(key_value_total))
     grad_in = dot(grad_query_pre, query_full, ((1,), (1,))) + dot(
         grad_key_value_pre, key_value_full, ((1,), (1,))
     )
+    grad_in, expert_sum = lax.optimization_barrier((grad_in, expert_sum))
     input_grad = grad_state + norm_back(input_wide, first_factor, first_gain, grad_in)
     qkv_grad = outer_scatter(
         jnp.concatenate([wide_sum(query_parts), wide_sum(key_value_parts)], axis=2).astype(BF16)

time: 578 us -> 567 us (0.981)
  waiting for transfers between devices: 201 us -> 190 us
    ppermute x42, waiting for transfers between devices: 123 us -> 111 us  [swap(): return lax.ppermute(x, axis, [(i, length - 1 - i) for i in range(length)])]
    all_to_all x1, waiting for transfers between devices: 0.01 us -> 10.3 us  [on_device(): expert_sum = lax.all_to_all(expert_sum, PLANE, 0, 0, tiled=True)]
    ppermute x9, waiting for transfers between devices: 30.9 us -> 21.4 us  [outer_shift(): lax.ppermute(x, 'outer', [(i, (i + by) % length) for i in range(length)])]
    unnamed x112 -> x100, local copies, waits for them, and re-layouts: 17.2 us -> 16.7 us
  transfers between devices with their start and end apart: 63 -> 63, of which waited for: 26 -> 27; matrix products, arithmetic and copies ran while one was open for 22% -> 24% of each run, Pallas kernels for 13% -> 13%
where the time goes in v3:
time: 567 us; the launch traced here: 560 us
  waiting for transfers between devices  190 us (34%)
  starting transfers between devices  106 us (19%)
  Pallas kernels  95.2 us (17%)
  other arithmetic  67.8 us (12%)
  local copies, waits for them, and re-layouts  66.3 us (12%)
  matrix products  18.3 us (3%)
  between operations  15.3 us (3%)
    ppermute x42, waiting for transfers between devices, swap(): return lax.ppermute(x, axis, [(i, length - 1 - i) for i in range(length)])  111 us
    ppermute x42, starting transfers between devices, swap(): return lax.ppermute(x, axis, [(i, length - 1 - i) for i in range(length)])  65.4 us
    pallas_call x2, Pallas kernels, expert_groups(): pl.pallas_call(functools.partial(expert_kernel, capacity=capacity), grid=...  41.7 us
    all_gather x3, waiting for transfers between devices, on_device(): lax.all_gather(shard, 'outer')  36.5 us
    ppermute x9, waiting for transfers between devices, outer_shift(): lax.ppermute(x, 'outer', [(i, (i + by) % length) for i in range(length)])  21.4 us
    ppermute x6, starting transfers between devices, shift_groups(): lax.ppermute(x, DP, [(i, i + by) for i in range(length) if 0 <= i + by <...  18.8 us
    dot_general x10, matrix products, dot(): return lax.dot_general(a, b, (dims, ((), ())), preferred_element_type=F32)  18.3 us
    pallas_call x1, Pallas kernels, attention_back(): pl.pallas_call(functools.partial(attention_back_kernel, seq_len=seq_len,...  17 us
  transfers between devices with their start and end apart: 63, of which 27 were waited for; matrix products, arithmetic and copies ran while one was open for 24% of the time, Pallas kernels for 13%

profile of v3, /device:TPU:0, one launch (start us, length us, event | category | flops | bytes accessed | tf_op | source)
XLA Modules:
  0.0 559.8 jit_solution(1387769690354460484)
XLA Ops:
  8.8 3.0 collective-permute-start
  14.9 2.1 collective-permute-start.1
  17.0 2.6 collective-permute-start.2
  23.7 4.3 all-to-all-start
  30.3 13.7 %collective-permute-done.2 = bf16[96,2048]{1,0:T(8,128)(2,1)S(1)} collective-permute-done((bf16[96,2048]{1,0:T(8,128)(2,1)S(1)}, bf16[96,2048]{1,0:T(8,128)(2,1)S(1)}, u32[]{:S(2)}, u32[]{:S(2)}) %collective-permute-start.2) | collective-permute-done | bytes 393248 | tf_op jit(solution)/shard_map/ppermute | solution.py:89
  44.1 6.2 %all-to-all-done = bf16[8,3,96,384]{3,2,1,0:T(8,128)(2,1)} async-done(((bf16[8,3,96,384]{3,2,1,0:T(8,128)(2,1)}), bf16[8,3,96,384]{3,2,1,0:T(8,128)(2,1)}, u32[]{:S(2)}, u32[]{:S(2)}) %all-to-all-start) | async-done | bytes 1769504 | tf_op jit(solution)/shard_map/all_to_all | solution.py:667
  65.9 2.8 collective-permute-done.7
  69.0 8.0 %scatter_custom_fusion = s32[2048]{0:T(1024)S(1)} fusion(s32[2048]{0:T(1024)S(1)} %compare_select_fusion.1, s32[2048]{0:T(1024)S(1)} %iota.24, s32[]{:T(128)} %constant.894.clone.1), kind=kCustom, calls=%fused_computation.211 | custom fusion | bytes 8196 | tf_op jit(solution)/shard_map/scatter | solution.py:679
  78.3 3.5 collective-permute-start.11
  84.4 3.1 project.2
  87.5 6.5 %collective-permute-start.9 = (bf16[256,512]{1,0:T(8,128)(2,1)}, bf16[256,512]{1,0:T(8,128)(2,1)}, u32[]{:S(2)}, u32[]{:S(2)}) collective-permute-start(bf16[256,512]{1,0:T(8,128)(2,1)} %project.2), channel_id=1, source_target_pairs={{0,2},{2,4},{4,6},{6,8},{8,10},{10,12},{12,14},{14,16},{16,18},{18... | collective-permute-start | bytes 786440 | tf_op jit(solution)/shard_map/ppermute | solution.py:29
  94.0 4.4 collective-permute-start.10
  100.0 4.7 collective-permute-done.10
  104.7 2.0 all-gather.7.cloned.1.call-done
  106.6 1.9 pad_maximum_fusion.2
  108.6 2.0 maximum_select_fusion
  112.7 6.5 %collective-permute-start.16 = (bf16[4,96,768]{2,1,0:T(8,128)(2,1)}, bf16[4,96,768]{2,1,0:T(8,128)(2,1)}, u32[]{:S(2)}, u32[]{:S(2)}) collective-permute-start(bf16[4,96,768]{2,1,0:T(8,128)(2,1)} %get-tuple-element.142), channel_id=1, source_target_pairs={{0,4},{4,0},{1,5},{5,1},{2,6},{6,2},{3,7},{7,3},{8,12},{12,8},{9,1... | collective-permute-start | bytes 1769480 | tf_op jit(solution)/shard_map/ppermute | solution.py:34
  125.7 6.5 %collective-permute-start.19 = (bf16[256,1664]{1,0:T(8,128)(2,1)}, bf16[256,1664]{1,0:T(8,128)(2,1)}, u32[]{:S(2)}, u32[]{:S(2)}) collective-permute-start(bf16[256,1664]{1,0:T(8,128)(2,1)} %fusion.8), channel_id=1, source_target_pairs={{0,4},{4,0},{1,5},{5,1},{2,6},{6,2},{3,7},{7,3},{8,12},{12,8},{9,1... | collective-permute-start | bytes 2555912 | tf_op jit(solution)/shard_map/ppermute | solution.py:34
  133.1 2.0 broadcast_select_fusion.3
  135.5 2.6 maximum_maximum_fusion
  138.3 7.4 %collective-permute-start.17 = (bf16[4,96,768]{2,1,0:T(8,128)(2,1)S(1)}, bf16[4,96,768]{2,1,0:T(8,128)(2,1)S(1)}, u32[]{:S(2)}, u32[]{:S(2)}) collective-permute-start(bf16[4,96,768]{2,1,0:T(8,128)(2,1)S(1)} %copy-done.14), channel_id=1, source_target_pairs={{0,5},{1,4},{4,1},{5,0},{2,7},{3,6},{6,3},{7,2},{8,13},{9,12},{12,... | collective-permute-start | bytes 1769480 | tf_op jit(solution)/shard_map/ppermute | solution.py:34
  147.4 6.5 %project.3.q_ref = bf16[256,1536]{1,0:T(8,128)(2,1)} custom-call(bf16[256,1536]{1,0:T(8,128)(2,1)} %fusion.3.rows_ref, bf16[1536,1536]{1,0:T(8,128)(2,1)} %bitcast.253, f32[256,128]{1,0:T(8,128)} %get-tuple-element.368.cosine_ref, f32[256,128]{1,0:T(8,128)} %get-tuple-element.369.sine_ref), custom_call_target="tpu_custom_call" | custom-call | flops 1000 | bytes 1000 | tf_op jit(solution)/shard_map/project/pallas_call | solution.py:193
  158.0 10.3 %attention.1 = (bf16[256,1536]{1,0:T(8,128)(2,1)}, f32[2,6,256]{2,1,0:T(8,128)}) custom-call(s32[1]{0:T(128)} %bitcast.place_ref, s32[1280,1]{1,0:T(8,128)} %broadcast_in_dim.93.segment_key_ref, s32[1,256]{1,0:T(1,128)} %bitcast.298, bf16[256,1536]{1,0:T(8,128)(2,1)} %project.3.q_ref, bf16[1280,512]{1,0:T(8,128)(2,1)} %constant_dynamic-update-slice_fusion.2.kv_ref), custom_call_target="tpu_custom_call" | custom-call | flops 1000 | bytes 1000 | tf_op jit(solution)/shard_map/attention/pallas_call | solution.py:270
  168.3 14.2 %collective-permute-done.17 = bf16[4,96,768]{2,1,0:T(8,128)(2,1)S(1)} collective-permute-done((bf16[4,96,768]{2,1,0:T(8,128)(2,1)S(1)}, bf16[4,96,768]{2,1,0:T(8,128)(2,1)S(1)}, u32[]{:S(2)}, u32[]{:S(2)}) %collective-permute-start.17) | collective-permute-done | bytes 589856 | tf_op jit(solution)/shard_map/ppermute | solution.py:34
  182.6 4.5 collective-permute-done.18
  189.4 3.5 pad_maximum_fusion
  193.7 2.0 broadcast_select_fusion.1
  196.1 2.6 maximum_maximum_fusion.1
  198.7 3.8 multiply_reduce_fusion.1
  204.8 6.3 %collective-permute-start.23 = (bf16[256,1536]{1,0:T(8,128)(2,1)S(1)}, bf16[256,1536]{1,0:T(8,128)(2,1)}, u32[]{:S(2)}, u32[]{:S(2)}) collective-permute-start(bf16[256,1536]{1,0:T(8,128)(2,1)S(1)} %multiply_convert_fusion), channel_id=1, source_target_pairs={{0,4},{4,0},{1,5},{5,1},{2,6},{6,2},{3,7},{7,3},{8,12},{12,8},{9,1... | collective-permute-start | bytes 2359304 | tf_op jit(solution)/shard_map/ppermute | solution.py:34
  211.1 34.6 %all-gather.11.cloned.1.call-done = bf16[3072,384]{1,0:T(8,128)(2,1)} async-done(((bf16[768,384]{1,0:T(8,128)(2,1)}), bf16[3072,384]{1,0:T(8,128)(2,1)}) %all-gather.11.cloned.1.call-update) | async-done | bytes 2359312 | tf_op jit(solution)/shard_map/all_gather | solution.py:694
  245.7 3.2 pad_maximum_fusion.1
  255.4 20.6 %expert.3 = (bf16[2,512,1536]{2,1,0:T(8,128)(2,1)}, bf16[2,512,1536]{2,1,0:T(8,128)(2,1)}, bf16[512,1536]{1,0:T(8,128)(2,1)}, bf16[512,1536]{1,0:T(8,128)(2,1)},...) custom-call(s32[2,1,512]{2,1,0:T(1,128)} %select_n.419.slot_row_ref, ...), custom_call_target="tpu_custom_call" | custom-call | flops 1000 | bytes 1000 | tf_op jit(solution)/shard_map/expert/pallas_call | solution.py:500
  279.3 21.1 %expert.2 = (bf16[2,512,1536]{2,1,0:T(8,128)(2,1)}, bf16[2,512,1536]{2,1,0:T(8,128)(2,1)}, bf16[512,1536]{1,0:T(8,128)(2,1)}, bf16[512,1536]{1,0:T(8,128)(2,1)},...) custom-call(s32[2,1,512]{2,1,0:T(1,128)} %copy.125.slot_row_ref, ...), custom_call_target="tpu_custom_call" | custom-call | flops 1000 | bytes 1000 | tf_op jit(solution)/shard_map/expert/pallas_call | solution.py:500
  300.4 5.0 fusion.12
  312.1 16.6 %weight_grads.1 = (bf16[1536,2560]{1,0:T(8,128)(2,1)}, bf16[256,1536]{1,0:T(8,128)(2,1)}, bf16[256,1536]{1,0:T(8,128)(2,1)}, bf16[256,1536]{1,0:T(8,128)(2,1)}, bf16[256,1536]{1,0:T(8,128)(2,1)}) custom-call(bf16[512,1536]{1,0:T(8,128)(2,1)} %get-tuple-element.180.refs_0_, bf16[512,1536]{1,0:T(8,128)(2,1)} %get-tuple-element.181.refs_1_, ...), custom_call_target="tpu_custom_call" | custom-call | flops 15000000512 | bytes 50000000 | tf_op jit(solution)/shard_map/weight_grads/pallas_call | solution.py:600
  328.7 2.0 collective-permute-done.29
  330.7 16.1 %collective-permute-done.30 = bf16[256,1536]{1,0:T(8,128)(2,1)} collective-permute-done((bf16[256,1536]{1,0:T(8,128)(2,1)}, bf16[256,1536]{1,0:T(8,128)(2,1)}, u32[]{:S(2)}, u32[]{:S(2)}) %collective-permute-start.30) | collective-permute-done | bytes 786464 | tf_op jit(solution)/shard_map/ppermute | solution.py:34
  348.0 2.3 multiply_reduce_fusion
  350.4 3.6 fusion.54
  353.9 2.6 copy.130
  357.7 2.2 convolution_convert_fusion.2
  363.4 4.6 convolution_convert_fusion.4.dout_ref
  368.0 17.0 %attention_back.1 = (bf16[256,1536]{1,0:T(8,128)(2,1)}, bf16[1024,512]{1,0:T(8,128)(2,1)}, f32[256,512]{1,0:T(8,128)}) custom-call(s32[1]{0:T(128)} %bitcast.place_ref, s32[1280,1]{1,0:T(8,128)} %broadcast_in_dim.93.segment_key_ref, s32[1,256]{1,0:T(1,128)} %bitcast.299, bf16[256,1536]{1,0:T(8,128)(2,1)} %project.3.q_ref, ...), custom_call_target="tpu_custom_call" | custom-call | flops 51999997952 | bytes 10000000 | tf_op jit(solution)/shard_map/attention_back/pallas_call | solution.py:359
  385.9 3.8 add_convert_fusion.1
  389.6 8.6 %collective-permute-done.35 = bf16[256,1536]{1,0:T(8,128)(2,1)} collective-permute-done((bf16[256,1536]{1,0:T(8,128)(2,1)}, bf16[256,1536]{1,0:T(8,128)(2,1)}, u32[]{:S(2)}, u32[]{:S(2)}) %collective-permute-start.35) | collective-permute-done | bytes 786464 | tf_op jit(solution)/shard_map/ppermute | solution.py:34
  398.2 2.2 convolution_convert_fusion
  405.3 2.8 dynamic-slice_bitcast_fusion.4
  412.5 2.3 add_convert_fusion
  414.8 3.8 collective-permute-done.36
  418.5 24.9 %collective-permute-done.37 = bf16[4,96,768]{2,1,0:T(8,128)(2,1)S(1)} collective-permute-done((bf16[4,96,768]{2,1,0:T(8,128)(2,1)S(1)}, bf16[4,96,768]{2,1,0:T(8,128)(2,1)S(1)}, u32[]{:S(2)}, u32[]{:S(2)}) %collective-permute-start.37) | collective-permute-done | bytes 589856 | tf_op jit(solution)/shard_map/ppermute | solution.py:34
  446.4 3.4 add_add_fusion
  452.5 3.3 collective-permute-start.44
  459.8 2.6 convolution_add_fusion
  462.3 4.7 collective-permute-done.43
  467.0 6.7 %collective-permute-done.44 = bf16[4,96,768]{2,1,0:T(8,128)(2,1)S(1)} collective-permute-done((bf16[4,96,768]{2,1,0:T(8,128)(2,1)S(1)}, bf16[4,96,768]{2,1,0:T(8,128)(2,1)S(1)}, u32[]{:S(2)}, u32[]{:S(2)}) %collective-permute-start.44) | collective-permute-done | bytes 589856 | tf_op jit(solution)/shard_map/ppermute | solution.py:34
  473.7 13.0 %collective-permute-done.45 = bf16[4,96,768]{2,1,0:T(8,128)(2,1)S(1)} collective-permute-done((bf16[4,96,768]{2,1,0:T(8,128)(2,1)S(1)}, bf16[4,96,768]{2,1,0:T(8,128)(2,1)S(1)}, u32[]{:S(2)}, u32[]{:S(2)}) %collective-permute-start.45) | collective-permute-done | bytes 589856 | tf_op jit(solution)/shard_map/ppermute | solution.py:34
  488.5 4.3 collective-permute-start.55
  493.5 3.4 collective-permute-start.49
  498.0 4.8 collective-permute-done.49
  507.6 4.5 reshape.417
  513.6 4.2 all-to-all-start.1
  521.9 5.3 collective-permute-done.50
  531.9 10.3 %all-to-all-done.1 = bf16[8,96,1280]{2,1,0:T(8,128)(2,1)S(1)} async-done(((bf16[8,96,1280]{2,1,0:T(8,128)(2,1)}), bf16[8,96,1280]{2,1,0:T(8,128)(2,1)S(1)}, u32[]{:S(2)}, u32[]{:S(2)}) %all-to-all-start.1) | async-done | bytes 1966112 | tf_op jit(solution)/shard_map/all_to_all | solution.py:861
  (310 shorter events, 124.8 us)
Async XLA Ops:
  8.8 5.0 collective-permute-start
  12.6 42.9 %copy-start.29 = (f32[1536]{0:T(1024)}, f32[1536]{0:T(1024)S(1)}, u32[]{:S(2)}) copy-start(f32[1536]{0:T(1024)S(1)} %get-tuple-element.267) | copy-start | bytes 18436
  14.9 14.4 %collective-permute-start.1 = (bf16[96,2048]{1,0:T(8,128)(2,1)S(1)}, bf16[96,2048]{1,0:T(8,128)(2,1)}, u32[]{:S(2)}, u32[]{:S(2)}) collective-permute-start(bf16[96,2048]{1,0:T(8,128)(2,1)S(1)} %pad_maximum_fusion.7), channel_id=1, source_target_pairs={{0,8},{8,16},{16,24},{24,0},{1,9},{9,17},{17,25},{25,1},{2,10},{10... | collective-permute-start | bytes 1179656 | tf_op jit(solution)/shard_map/ppermute | solution.py:89
  17.0 27.0 %collective-permute-start.2 = (bf16[96,2048]{1,0:T(8,128)(2,1)S(1)}, bf16[96,2048]{1,0:T(8,128)(2,1)S(1)}, u32[]{:S(2)}, u32[]{:S(2)}) collective-permute-start(bf16[96,2048]{1,0:T(8,128)(2,1)S(1)} %pad_maximum_fusion.7), channel_id=1, source_target_pairs={{0,16},{8,24},{16,0},{24,8},{1,17},{9,25},{17,1},{25,9},{2,18},{10... | collective-permute-start | bytes 1179656 | tf_op jit(solution)/shard_map/ppermute | solution.py:89
  19.6 24.4 %collective-permute-start.3 = (bf16[96,2048]{1,0:T(8,128)(2,1)S(1)}, bf16[96,2048]{1,0:T(8,128)(2,1)S(1)}, u32[]{:S(2)}, u32[]{:S(2)}) collective-permute-start(bf16[96,2048]{1,0:T(8,128)(2,1)S(1)} %pad_maximum_fusion.7), channel_id=1, source_target_pairs={{0,24},{8,0},{16,8},{24,16},{1,25},{9,1},{17,9},{25,17},{2,26},{10... | collective-permute-start | bytes 1179656 | tf_op jit(solution)/shard_map/ppermute | solution.py:89
  23.7 26.6 %all-to-all-start = ((bf16[8,3,96,384]{3,2,1,0:T(8,128)(2,1)}), bf16[8,3,96,384]{3,2,1,0:T(8,128)(2,1)}, u32[]{:S(2)}, u32[]{:S(2)}) async-start(bf16[8,3,96,384]{3,2,1,0:T(8,128)(2,1)} %maximum_bitcast_fusion), calls=%async_computation | async-start | bytes 3538944 | tf_op jit(solution)/shard_map/all_to_all | solution.py:667
  28.0 78.6 %all-gather.7.cloned.1.call-start = ((), (), s32[]{:S(2)}) async-start(), calls=%async_computation.4 | async-start | bytes 2949120 | tf_op jit(solution)/shard_map/all_gather | solution.py:694
  54.6 144.0 %all-gather.9.cloned.1.call-start = ((), (), s32[]{:S(2)}) async-start(), calls=%async_computation.5 | async-start | bytes 2949120 | tf_op jit(solution)/shard_map/all_gather | solution.py:694
  56.7 12.0 %collective-permute-start.7 = (bf16[4,96,512]{2,1,0:T(8,128)(2,1)S(1)}, bf16[4,96,512]{2,1,0:T(8,128)(2,1)S(1)}, u32[]{:S(2)}, u32[]{:S(2)}) collective-permute-start(bf16[4,96,512]{2,1,0:T(8,128)(2,1)S(1)} %slice.138), channel_id=1, source_target_pairs={{0,4},{4,0},{1,5},{5,1},{2,6},{6,2},{3,7},{7,3},{8,12},{12,8},{9,1... | collective-permute-start | bytes 1179656 | tf_op jit(solution)/shard_map/ppermute | solution.py:34
  60.5 39.4 %collective-permute-start.4 = (bf16[4,96,768]{2,1,0:T(8,128)(2,1)}, bf16[4,96,768]{2,1,0:T(8,128)(2,1)}, u32[]{:S(2)}, u32[]{:S(2)}) collective-permute-start(bf16[4,96,768]{2,1,0:T(8,128)(2,1)} %get-tuple-element.132), channel_id=1, source_target_pairs={{0,1},{1,0},{2,3},{3,2},{4,5},{5,4},{6,7},{7,6},{8,9},{9,8},{10,11... | collective-permute-start | bytes 1769480 | tf_op jit(solution)/shard_map/ppermute | solution.py:34
  61.2 38.7 %collective-permute-start.5 = (bf16[4,96,768]{2,1,0:T(8,128)(2,1)}, bf16[4,96,768]{2,1,0:T(8,128)(2,1)}, u32[]{:S(2)}, u32[]{:S(2)}) collective-permute-start(bf16[4,96,768]{2,1,0:T(8,128)(2,1)} %get-tuple-element.132), channel_id=1, source_target_pairs={{0,4},{4,0},{1,5},{5,1},{2,6},{6,2},{3,7},{7,3},{8,12},{12,8},{9,1... | collective-permute-start | bytes 1769480 | tf_op jit(solution)/shard_map/ppermute | solution.py:34
  62.7 37.2 %collective-permute-start.6 = (bf16[4,96,768]{2,1,0:T(8,128)(2,1)}, bf16[4,96,768]{2,1,0:T(8,128)(2,1)}, u32[]{:S(2)}, u32[]{:S(2)}) collective-permute-start(bf16[4,96,768]{2,1,0:T(8,128)(2,1)} %get-tuple-element.132), channel_id=1, source_target_pairs={{0,5},{1,4},{4,1},{5,0},{2,7},{3,6},{6,3},{7,2},{8,13},{9,12},{12,... | collective-permute-start | bytes 1769480 | tf_op jit(solution)/shard_map/ppermute | solution.py:34
  64.0 23.4 %collective-permute-start.12 = (s32[512]{0:T(512)}, s32[512]{0:T(512)}, u32[]{:S(2)}, u32[]{:S(2)}) collective-permute-start(s32[512]{0:T(512)} %param.24), channel_id=1, source_target_pairs={{0,2},{2,4},{4,6},{6,8},{8,10},{10,12},{12,14},{14,16},{16,18},{18... | collective-permute-start | bytes 6152 | tf_op jit(solution)/shard_map/ppermute | solution.py:29
  68.9 9.4 %collective-permute-start.8 = (bf16[4,2,96,512]{3,2,1,0:T(8,128)(2,1)S(1)}, bf16[4,2,96,512]{3,2,1,0:T(8,128)(2,1)}, u32[]{:S(2)}, u32[]{:S(2)}) collective-permute-start(bf16[4,2,96,512]{3,2,1,0:T(8,128)(2,1)S(1)} %pad_maximum_fusion.5), channel_id=1, source_target_pairs={{0,2},{2,0},{1,3},{3,1},{4,6},{6,4},{5,7},{7,5},{8,10},{10,8},{9,1... | collective-permute-start | bytes 2359304 | tf_op jit(solution)/shard_map/ppermute | solution.py:34
  78.3 15.7 %collective-permute-start.11 = (s32[512]{0:T(512)}, s32[512]{0:T(512)S(1)}, u32[]{:S(2)}, u32[]{:S(2)}) collective-permute-start(s32[512]{0:T(512)} %param.24), channel_id=1, source_target_pairs={{0,4},{2,6},{4,8},{6,10},{8,12},{10,14},{12,16},{14,18},{16,20},{1... | collective-permute-start | bytes 6152 | tf_op jit(solution)/shard_map/ppermute | solution.py:29
  87.5 12.5 %collective-permute-start.9 = (bf16[256,512]{1,0:T(8,128)(2,1)}, bf16[256,512]{1,0:T(8,128)(2,1)}, u32[]{:S(2)}, u32[]{:S(2)}) collective-permute-start(bf16[256,512]{1,0:T(8,128)(2,1)} %project.2), channel_id=1, source_target_pairs={{0,2},{2,4},{4,6},{6,8},{8,10},{10,12},{12,14},{14,16},{16,18},{18... | collective-permute-start | bytes 786440 | tf_op jit(solution)/shard_map/ppermute | solution.py:29
  94.0 10.7 %collective-permute-start.10 = (bf16[256,512]{1,0:T(8,128)(2,1)}, bf16[256,512]{1,0:T(8,128)(2,1)}, u32[]{:S(2)}, u32[]{:S(2)}) collective-permute-start(bf16[256,512]{1,0:T(8,128)(2,1)} %project.2), channel_id=1, source_target_pairs={{0,4},{2,6},{4,8},{6,10},{8,12},{10,14},{12,16},{14,18},{16,20},{1... | collective-permute-start | bytes 786440 | tf_op jit(solution)/shard_map/ppermute | solution.py:29
  108.6 23.7 %collective-permute-start.13 = (bf16[2,2,4,96,768]{4,3,2,1,0:T(8,128)(2,1)S(1)}, bf16[2,2,4,96,768]{4,3,2,1,0:T(8,128)(2,1)}, u32[]{:S(2)}, u32[]{:S(2)}) collective-permute-start(bf16[2,2,4,96,768]{4,3,2,1,0:T(8,128)(2,1)S(1)} %bitcast.267), channel_id=1, source_target_pairs={{0,2},{2,0},{1,3},{3,1},{4,6},{6,4},{5,7},{7,5},{8,10},{10,8},{9,1... | collective-permute-start | bytes 7077896 | tf_op jit(solution)/shard_map/ppermute | solution.py:34
  110.6 15.0 %collective-permute-start.14 = (bf16[2,256,512]{2,1,0:T(8,128)(2,1)}, bf16[2,256,512]{2,1,0:T(8,128)(2,1)}, u32[]{:S(2)}, u32[]{:S(2)}) collective-permute-start(bf16[2,256,512]{2,1,0:T(8,128)(2,1)} %maximum_select_fusion), channel_id=1, source_target_pairs={{0,1},{1,0},{2,3},{3,2},{4,5},{5,4},{6,7},{7,6},{8,9},{9,8},{10,11... | collective-permute-start | bytes 1572872 | tf_op jit(solution)/shard_map/ppermute | solution.py:34
  112.1 26.2 %collective-permute-start.15 = (bf16[4,96,768]{2,1,0:T(8,128)(2,1)}, bf16[4,96,768]{2,1,0:T(8,128)(2,1)}, u32[]{:S(2)}, u32[]{:S(2)}) collective-permute-start(bf16[4,96,768]{2,1,0:T(8,128)(2,1)} %get-tuple-element.142), channel_id=1, source_target_pairs={{0,1},{1,0},{2,3},{3,2},{4,5},{5,4},{6,7},{7,6},{8,9},{9,8},{10,11... | collective-permute-start | bytes 1769480 | tf_op jit(solution)/shard_map/ppermute | solution.py:34
  112.7 55.7 %collective-permute-start.16 = (bf16[4,96,768]{2,1,0:T(8,128)(2,1)}, bf16[4,96,768]{2,1,0:T(8,128)(2,1)}, u32[]{:S(2)}, u32[]{:S(2)}) collective-permute-start(bf16[4,96,768]{2,1,0:T(8,128)(2,1)} %get-tuple-element.142), channel_id=1, source_target_pairs={{0,4},{4,0},{1,5},{5,1},{2,6},{6,2},{3,7},{7,3},{8,12},{12,8},{9,1... | collective-permute-start | bytes 1769480 | tf_op jit(solution)/shard_map/ppermute | solution.py:34
  119.2 126.5 %all-gather.11.cloned.1.call-start = ((), (), s32[]{:S(2)}) async-start(), calls=%async_computation.6 | async-start | bytes 2949120 | tf_op jit(solution)/shard_map/all_gather | solution.py:694
  121.2 65.8 %collective-permute-start.18 = (bf16[256,1664]{1,0:T(8,128)(2,1)}, bf16[256,1664]{1,0:T(8,128)(2,1)}, u32[]{:S(2)}, u32[]{:S(2)}) collective-permute-start(bf16[256,1664]{1,0:T(8,128)(2,1)} %fusion.8), channel_id=1, source_target_pairs={{0,1},{1,0},{2,3},{3,2},{4,5},{5,4},{6,7},{7,6},{8,9},{9,8},{10,11... | collective-permute-start | bytes 2555912 | tf_op jit(solution)/shard_map/ppermute | solution.py:34
  125.7 61.4 %collective-permute-start.19 = (bf16[256,1664]{1,0:T(8,128)(2,1)}, bf16[256,1664]{1,0:T(8,128)(2,1)}, u32[]{:S(2)}, u32[]{:S(2)}) collective-permute-start(bf16[256,1664]{1,0:T(8,128)(2,1)} %fusion.8), channel_id=1, source_target_pairs={{0,4},{4,0},{1,5},{5,1},{2,6},{6,2},{3,7},{7,3},{8,12},{12,8},{9,1... | collective-permute-start | bytes 2555912 | tf_op jit(solution)/shard_map/ppermute | solution.py:34
  132.2 54.9 %collective-permute-start.20 = (bf16[256,1664]{1,0:T(8,128)(2,1)}, bf16[256,1664]{1,0:T(8,128)(2,1)}, u32[]{:S(2)}, u32[]{:S(2)}) collective-permute-start(bf16[256,1664]{1,0:T(8,128)(2,1)} %fusion.8), channel_id=1, source_target_pairs={{0,5},{1,4},{4,1},{5,0},{2,7},{3,6},{6,3},{7,2},{8,13},{9,12},{12,... | collective-permute-start | bytes 2555912 | tf_op jit(solution)/shard_map/ppermute | solution.py:34
  138.3 44.3 %collective-permute-start.17 = (bf16[4,96,768]{2,1,0:T(8,128)(2,1)S(1)}, bf16[4,96,768]{2,1,0:T(8,128)(2,1)S(1)}, u32[]{:S(2)}, u32[]{:S(2)}) collective-permute-start(bf16[4,96,768]{2,1,0:T(8,128)(2,1)S(1)} %copy-done.14), channel_id=1, source_target_pairs={{0,5},{1,4},{4,1},{5,0},{2,7},{3,6},{6,3},{7,2},{8,13},{9,12},{12,... | collective-permute-start | bytes 1769480 | tf_op jit(solution)/shard_map/ppermute | solution.py:34
  189.0 4.7 collective-permute-start.21
  189.1 318.5 %reduce-scatter.2.cloned.1.call-start = ((), (), s32[]{:S(2)}) async-start(), calls=%async_computation.3 | async-start | bytes 9830400 | tf_op jit(solution)/shard_map/reduce_scatter | solution.py:807
  192.8 58.2 %collective-permute-start.25 = (bf16[2,2,256,1664]{3,2,1,0:T(8,128)(2,1)}, bf16[2,2,256,1664]{3,2,1,0:T(8,128)(2,1)}, u32[]{:S(2)}, u32[]{:S(2)}) collective-permute-start(bf16[2,2,256,1664]{3,2,1,0:T(8,128)(2,1)} %bitcast.66), channel_id=1, source_target_pairs={{0,2},{2,0},{1,3},{3,1},{4,6},{6,4},{5,7},{7,5},{8,10},{10,8},{9,1... | collective-permute-start | bytes 10223624 | tf_op jit(solution)/shard_map/ppermute | solution.py:34
  203.2 42.4 %collective-permute-start.22 = (bf16[256,1536]{1,0:T(8,128)(2,1)S(1)}, bf16[256,1536]{1,0:T(8,128)(2,1)}, u32[]{:S(2)}, u32[]{:S(2)}) collective-permute-start(bf16[256,1536]{1,0:T(8,128)(2,1)S(1)} %multiply_convert_fusion), channel_id=1, source_target_pairs={{0,1},{1,0},{2,3},{3,2},{4,5},{5,4},{6,7},{7,6},{8,9},{9,8},{10,11... | collective-permute-start | bytes 2359304 | tf_op jit(solution)/shard_map/ppermute | solution.py:34
  204.8 40.9 %collective-permute-start.23 = (bf16[256,1536]{1,0:T(8,128)(2,1)S(1)}, bf16[256,1536]{1,0:T(8,128)(2,1)}, u32[]{:S(2)}, u32[]{:S(2)}) collective-permute-start(bf16[256,1536]{1,0:T(8,128)(2,1)S(1)} %multiply_convert_fusion), channel_id=1, source_target_pairs={{0,4},{4,0},{1,5},{5,1},{2,6},{6,2},{3,7},{7,3},{8,12},{12,8},{9,1... | collective-permute-start | bytes 2359304 | tf_op jit(solution)/shard_map/ppermute | solution.py:34
  211.1 34.6 %collective-permute-start.24 = (bf16[256,1536]{1,0:T(8,128)(2,1)S(1)}, bf16[256,1536]{1,0:T(8,128)(2,1)}, u32[]{:S(2)}, u32[]{:S(2)}) collective-permute-start(bf16[256,1536]{1,0:T(8,128)(2,1)S(1)} %multiply_convert_fusion), channel_id=1, source_target_pairs={{0,5},{1,4},{4,1},{5,0},{2,7},{3,6},{6,3},{7,2},{8,13},{9,12},{12,... | collective-permute-start | bytes 2359304 | tf_op jit(solution)/shard_map/ppermute | solution.py:34
  248.8 6.6 %collective-permute-start.26 = (bf16[2,2,256,1536]{3,2,1,0:T(8,128)(2,1)}, bf16[2,2,256,1536]{3,2,1,0:T(8,128)(2,1)}, u32[]{:S(2)}, u32[]{:S(2)}) collective-permute-start(bf16[2,2,256,1536]{3,2,1,0:T(8,128)(2,1)} %bitcast.85), channel_id=1, source_target_pairs={{0,2},{2,0},{1,3},{3,1},{4,6},{6,4},{5,7},{7,5},{8,10},{10,8},{9,1... | collective-permute-start | bytes 9437192 | tf_op jit(solution)/shard_map/ppermute | solution.py:34
  276.0 24.4 %collective-permute-start.27 = (bf16[4,256,1536]{2,1,0:T(8,128)(2,1)}, bf16[4,256,1536]{2,1,0:T(8,128)(2,1)}, u32[]{:S(2)}, u32[]{:S(2)}) collective-permute-start(bf16[4,256,1536]{2,1,0:T(8,128)(2,1)} %bitcast.303), channel_id=1, source_target_pairs={{0,2},{2,0},{1,3},{3,1},{4,6},{6,4},{5,7},{7,5},{8,10},{10,8},{9,1... | collective-permute-start | bytes 9437192 | tf_op jit(solution)/shard_map/ppermute | solution.py:34
  305.5 6.6 %collective-permute-start.31 = (bf16[4,256,1536]{2,1,0:T(8,128)(2,1)}, bf16[4,256,1536]{2,1,0:T(8,128)(2,1)}, u32[]{:S(2)}, u32[]{:S(2)}) collective-permute-start(bf16[4,256,1536]{2,1,0:T(8,128)(2,1)} %bitcast.93), channel_id=1, source_target_pairs={{0,2},{2,0},{1,3},{3,1},{4,6},{6,4},{5,7},{7,5},{8,10},{10,8},{9,1... | collective-permute-start | bytes 9437192 | tf_op jit(solution)/shard_map/ppermute | solution.py:34
  308.6 20.1 %collective-permute-start.28 = (bf16[256,1536]{1,0:T(8,128)(2,1)}, bf16[256,1536]{1,0:T(8,128)(2,1)S(1)}, u32[]{:S(2)}, u32[]{:S(2)}) collective-permute-start(bf16[256,1536]{1,0:T(8,128)(2,1)} %get-tuple-element.177), channel_id=1, source_target_pairs={{0,1},{1,0},{2,3},{3,2},{4,5},{5,4},{6,7},{7,6},{8,9},{9,8},{10,11... | collective-permute-start | bytes 2359304 | tf_op jit(solution)/shard_map/ppermute | solution.py:34
  310.0 20.7 %collective-permute-start.29 = (bf16[256,1536]{1,0:T(8,128)(2,1)}, bf16[256,1536]{1,0:T(8,128)(2,1)}, u32[]{:S(2)}, u32[]{:S(2)}) collective-permute-start(bf16[256,1536]{1,0:T(8,128)(2,1)} %get-tuple-element.178), channel_id=1, source_target_pairs={{0,4},{4,0},{1,5},{5,1},{2,6},{6,2},{3,7},{7,3},{8,12},{12,8},{9,1... | collective-permute-start | bytes 2359304 | tf_op jit(solution)/shard_map/ppermute | solution.py:34
  311.7 35.2 %collective-permute-start.30 = (bf16[256,1536]{1,0:T(8,128)(2,1)}, bf16[256,1536]{1,0:T(8,128)(2,1)}, u32[]{:S(2)}, u32[]{:S(2)}) collective-permute-start(bf16[256,1536]{1,0:T(8,128)(2,1)} %get-tuple-element.179), channel_id=1, source_target_pairs={{0,5},{1,4},{4,1},{5,0},{2,7},{3,6},{6,3},{7,2},{8,13},{9,12},{12,... | collective-permute-start | bytes 2359304 | tf_op jit(solution)/shard_map/ppermute | solution.py:34
  359.9 25.9 %collective-permute-start.32 = (bf16[768,1536]{1,0:T(8,128)(2,1)}, bf16[768,1536]{1,0:T(8,128)(2,1)}, u32[]{:S(2)}, u32[]{:S(2)}) collective-permute-start(bf16[768,1536]{1,0:T(8,128)(2,1)} %convolution_convert_fusion.2), channel_id=1, source_target_pairs={{0,2},{2,0},{1,3},{3,1},{4,6},{6,4},{5,7},{7,5},{8,10},{10,8},{9,1... | collective-permute-start | bytes 7077896 | tf_op jit(solution)/shard_map/ppermute | solution.py:34
  359.9 29.7 %collective-permute-start.33 = (bf16[256,1536]{1,0:T(8,128)(2,1)}, bf16[256,1536]{1,0:T(8,128)(2,1)}, u32[]{:S(2)}, u32[]{:S(2)}) collective-permute-start(bf16[256,1536]{1,0:T(8,128)(2,1)} %get-tuple-element.205), channel_id=1, source_target_pairs={{0,1},{1,0},{2,3},{3,2},{4,5},{5,4},{6,7},{7,6},{8,9},{9,8},{10,11... | collective-permute-start | bytes 2359304 | tf_op jit(solution)/shard_map/ppermute | solution.py:34
  361.4 28.2 %collective-permute-start.34 = (bf16[256,1536]{1,0:T(8,128)(2,1)}, bf16[256,1536]{1,0:T(8,128)(2,1)}, u32[]{:S(2)}, u32[]{:S(2)}) collective-permute-start(bf16[256,1536]{1,0:T(8,128)(2,1)} %get-tuple-element.206), channel_id=1, source_target_pairs={{0,4},{4,0},{1,5},{5,1},{2,6},{6,2},{3,7},{7,3},{8,12},{12,8},{9,1... | collective-permute-start | bytes 2359304 | tf_op jit(solution)/shard_map/ppermute | solution.py:34
  363.0 35.2 %collective-permute-start.35 = (bf16[256,1536]{1,0:T(8,128)(2,1)}, bf16[256,1536]{1,0:T(8,128)(2,1)}, u32[]{:S(2)}, u32[]{:S(2)}) collective-permute-start(bf16[256,1536]{1,0:T(8,128)(2,1)} %get-tuple-element.207), channel_id=1, source_target_pairs={{0,5},{1,4},{4,1},{5,0},{2,7},{3,6},{6,3},{7,2},{8,13},{9,12},{12,... | collective-permute-start | bytes 2359304 | tf_op jit(solution)/shard_map/ppermute | solution.py:34
  400.4 12.0 %collective-permute-start.40 = (bf16[768,1536]{1,0:T(8,128)(2,1)}, bf16[768,1536]{1,0:T(8,128)(2,1)}, u32[]{:S(2)}, u32[]{:S(2)}) collective-permute-start(bf16[768,1536]{1,0:T(8,128)(2,1)} %convolution_convert_fusion), channel_id=1, source_target_pairs={{0,2},{2,0},{1,3},{3,1},{4,6},{6,4},{5,7},{7,5},{8,10},{10,8},{9,1... | collective-permute-start | bytes 7077896 | tf_op jit(solution)/shard_map/ppermute | solution.py:34
  403.7 14.8 %collective-permute-start.36 = (bf16[2,256,512]{2,1,0:T(8,128)(2,1)S(1)}, bf16[2,256,512]{2,1,0:T(8,128)(2,1)S(1)}, u32[]{:S(2)}, u32[]{:S(2)}) collective-permute-start(bf16[2,256,512]{2,1,0:T(8,128)(2,1)S(1)} %pad_maximum_fusion.6), channel_id=1, source_target_pairs={{0,1},{1,0},{2,3},{3,2},{4,5},{5,4},{6,7},{7,6},{8,9},{9,8},{10,11... | collective-permute-start | bytes 1572872 | tf_op jit(solution)/shard_map/ppermute | solution.py:34
  408.1 35.3 %collective-permute-start.37 = (bf16[4,96,768]{2,1,0:T(8,128)(2,1)S(1)}, bf16[4,96,768]{2,1,0:T(8,128)(2,1)S(1)}, u32[]{:S(2)}, u32[]{:S(2)}) collective-permute-start(bf16[4,96,768]{2,1,0:T(8,128)(2,1)S(1)} %get-tuple-element.290), channel_id=1, source_target_pairs={{0,1},{1,0},{2,3},{3,2},{4,5},{5,4},{6,7},{7,6},{8,9},{9,8},{10,11... | collective-permute-start | bytes 1769480 | tf_op jit(solution)/shard_map/ppermute | solution.py:34
  408.7 34.7 %collective-permute-start.38 = (bf16[4,96,768]{2,1,0:T(8,128)(2,1)S(1)}, bf16[4,96,768]{2,1,0:T(8,128)(2,1)S(1)}, u32[]{:S(2)}, u32[]{:S(2)}) collective-permute-start(bf16[4,96,768]{2,1,0:T(8,128)(2,1)S(1)} %get-tuple-element.289), channel_id=1, source_target_pairs={{0,4},{4,0},{1,5},{5,1},{2,6},{6,2},{3,7},{7,3},{8,12},{12,8},{9,1... | collective-permute-start | bytes 1769480 | tf_op jit(solution)/shard_map/ppermute | solution.py:34
  410.4 33.0 %collective-permute-start.39 = (bf16[4,96,768]{2,1,0:T(8,128)(2,1)S(1)}, bf16[4,96,768]{2,1,0:T(8,128)(2,1)S(1)}, u32[]{:S(2)}, u32[]{:S(2)}) collective-permute-start(bf16[4,96,768]{2,1,0:T(8,128)(2,1)S(1)} %get-tuple-element.288), channel_id=1, source_target_pairs={{0,5},{1,4},{4,1},{5,0},{2,7},{3,6},{6,3},{7,2},{8,13},{9,12},{12,... | collective-permute-start | bytes 1769480 | tf_op jit(solution)/shard_map/ppermute | solution.py:34
  443.7 12.0 %collective-permute-start.42 = (bf16[256,512]{1,0:T(8,128)(2,1)S(1)}, bf16[256,512]{1,0:T(8,128)(2,1)S(1)}, u32[]{:S(2)}, u32[]{:S(2)}) collective-permute-start(bf16[256,512]{1,0:T(8,128)(2,1)S(1)} %get-tuple-element.309), channel_id=1, source_target_pairs={{4,0},{6,2},{8,4},{10,6},{12,8},{14,10},{16,12},{18,14},{20,16},{2... | collective-permute-start | bytes 786440 | tf_op jit(solution)/shard_map/ppermute | solution.py:29
  445.0 10.7 %collective-permute-start.41 = (bf16[256,512]{1,0:T(8,128)(2,1)S(1)}, bf16[256,512]{1,0:T(8,128)(2,1)S(1)}, u32[]{:S(2)}, u32[]{:S(2)}) collective-permute-start(bf16[256,512]{1,0:T(8,128)(2,1)S(1)} %get-tuple-element.308), channel_id=1, source_target_pairs={{2,0},{4,2},{6,4},{8,6},{10,8},{12,10},{14,12},{16,14},{18,16},{20... | collective-permute-start | bytes 786440 | tf_op jit(solution)/shard_map/ppermute | solution.py:29
  450.9 16.1 %collective-permute-start.43 = (bf16[4,96,768]{2,1,0:T(8,128)(2,1)S(1)}, bf16[4,96,768]{2,1,0:T(8,128)(2,1)S(1)}, u32[]{:S(2)}, u32[]{:S(2)}) collective-permute-start(bf16[4,96,768]{2,1,0:T(8,128)(2,1)S(1)} %get-tuple-element.286), channel_id=1, source_target_pairs={{0,1},{1,0},{2,3},{3,2},{4,5},{5,4},{6,7},{7,6},{8,9},{9,8},{10,11... | collective-permute-start | bytes 1769480 | tf_op jit(solution)/shard_map/ppermute | solution.py:34
  452.5 21.3 %collective-permute-start.44 = (bf16[4,96,768]{2,1,0:T(8,128)(2,1)S(1)}, bf16[4,96,768]{2,1,0:T(8,128)(2,1)S(1)}, u32[]{:S(2)}, u32[]{:S(2)}) collective-permute-start(bf16[4,96,768]{2,1,0:T(8,128)(2,1)S(1)} %get-tuple-element.285), channel_id=1, source_target_pairs={{0,4},{4,0},{1,5},{5,1},{2,6},{6,2},{3,7},{7,3},{8,12},{12,8},{9,1... | collective-permute-start | bytes 1769480 | tf_op jit(solution)/shard_map/ppermute | solution.py:34
  455.7 31.0 %collective-permute-start.45 = (bf16[4,96,768]{2,1,0:T(8,128)(2,1)S(1)}, bf16[4,96,768]{2,1,0:T(8,128)(2,1)S(1)}, u32[]{:S(2)}, u32[]{:S(2)}) collective-permute-start(bf16[4,96,768]{2,1,0:T(8,128)(2,1)S(1)} %get-tuple-element.284), channel_id=1, source_target_pairs={{0,5},{1,4},{4,1},{5,0},{2,7},{3,6},{6,3},{7,2},{8,13},{9,12},{12,... | collective-permute-start | bytes 1769480 | tf_op jit(solution)/shard_map/ppermute | solution.py:34
  458.8 34.1 %collective-permute-start.46 = (bf16[768,512]{1,0:T(8,128)(2,1)S(1)}, bf16[768,512]{1,0:T(8,128)(2,1)S(1)}, u32[]{:S(2)}, u32[]{:S(2)}) collective-permute-start(bf16[768,512]{1,0:T(8,128)(2,1)S(1)} %convolution_convert_fusion.5), channel_id=1, source_target_pairs={{0,2},{2,0},{1,3},{3,1},{4,6},{6,4},{5,7},{7,5},{8,10},{10,8},{9,1... | collective-permute-start | bytes 2359304 | tf_op jit(solution)/shard_map/ppermute | solution.py:34
  487.9 29.9 %collective-permute-start.56 = (bf16[96,768]{1,0:T(8,128)(2,1)}, bf16[96,768]{1,0:T(8,128)(2,1)}, u32[]{:S(2)}, u32[]{:S(2)}) collective-permute-start(bf16[96,768]{1,0:T(8,128)(2,1)} %get-tuple-element.337), channel_id=1, source_target_pairs={{0,24},{8,0},{16,8},{24,16},{1,25},{9,1},{17,9},{25,17},{2,26},{10... | collective-permute-start | bytes 442376 | tf_op jit(solution)/shard_map/ppermute | solution.py:89
  488.5 30.1 %collective-permute-start.55 = (bf16[96,768]{1,0:T(8,128)(2,1)}, bf16[96,768]{1,0:T(8,128)(2,1)}, u32[]{:S(2)}, u32[]{:S(2)}) collective-permute-start(bf16[96,768]{1,0:T(8,128)(2,1)} %get-tuple-element.338), channel_id=1, source_target_pairs={{0,16},{8,24},{16,0},{24,8},{1,17},{9,25},{17,1},{25,9},{2,18},{10... | collective-permute-start | bytes 442376 | tf_op jit(solution)/shard_map/ppermute | solution.py:89
  493.5 9.3 %collective-permute-start.49 = (bf16[4,96,256]{2,1,0:T(8,128)(2,1)S(1)}, bf16[4,96,256]{2,1,0:T(8,128)(2,1)S(1)}, u32[]{:S(2)}, u32[]{:S(2)}) collective-permute-start(bf16[4,96,256]{2,1,0:T(8,128)(2,1)S(1)} %get-tuple-element.328), channel_id=1, source_target_pairs={{0,5},{1,4},{4,1},{5,0},{2,7},{3,6},{6,3},{7,2},{8,13},{9,12},{12,... | collective-permute-start | bytes 589832 | tf_op jit(solution)/shard_map/ppermute | solution.py:34
  496.9 7.6 %collective-permute-start.48 = (bf16[4,96,256]{2,1,0:T(8,128)(2,1)S(1)}, bf16[4,96,256]{2,1,0:T(8,128)(2,1)S(1)}, u32[]{:S(2)}, u32[]{:S(2)}) collective-permute-start(bf16[4,96,256]{2,1,0:T(8,128)(2,1)S(1)} %get-tuple-element.329), channel_id=1, source_target_pairs={{0,4},{4,0},{1,5},{5,1},{2,6},{6,2},{3,7},{7,3},{8,12},{12,8},{9,1... | collective-permute-start | bytes 589832 | tf_op jit(solution)/shard_map/ppermute | solution.py:34
  496.9 8.3 %collective-permute-start.47 = (bf16[4,96,256]{2,1,0:T(8,128)(2,1)S(1)}, bf16[4,96,256]{2,1,0:T(8,128)(2,1)S(1)}, u32[]{:S(2)}, u32[]{:S(2)}) collective-permute-start(bf16[4,96,256]{2,1,0:T(8,128)(2,1)S(1)} %get-tuple-element.327), channel_id=1, source_target_pairs={{0,1},{1,0},{2,3},{3,2},{4,5},{5,4},{6,7},{7,6},{8,9},{9,8},{10,11... | collective-permute-start | bytes 589832 | tf_op jit(solution)/shard_map/ppermute | solution.py:34
  502.7 15.8 %collective-permute-start.54 = (bf16[96,768]{1,0:T(8,128)(2,1)}, bf16[96,768]{1,0:T(8,128)(2,1)}, u32[]{:S(2)}, u32[]{:S(2)}) collective-permute-start(bf16[96,768]{1,0:T(8,128)(2,1)} %get-tuple-element.336), channel_id=1, source_target_pairs={{0,8},{8,16},{16,24},{24,0},{1,9},{9,17},{17,25},{25,1},{2,10},{10... | collective-permute-start | bytes 442376 | tf_op jit(solution)/shard_map/ppermute | solution.py:89
  506.3 14.2 %collective-permute-start.52 = (bf16[96,1024]{1,0:T(8,128)(2,1)}, bf16[96,1024]{1,0:T(8,128)(2,1)}, u32[]{:S(2)}, u32[]{:S(2)}) collective-permute-start(bf16[96,1024]{1,0:T(8,128)(2,1)} %get-tuple-element.326), channel_id=1, source_target_pairs={{0,24},{8,0},{16,8},{24,16},{1,25},{9,1},{17,9},{25,17},{2,26},{10... | collective-permute-start | bytes 589832 | tf_op jit(solution)/shard_map/ppermute | solution.py:89
  507.6 14.3 %collective-permute-start.51 = (bf16[96,1024]{1,0:T(8,128)(2,1)}, bf16[96,1024]{1,0:T(8,128)(2,1)}, u32[]{:S(2)}, u32[]{:S(2)}) collective-permute-start(bf16[96,1024]{1,0:T(8,128)(2,1)} %get-tuple-element.325), channel_id=1, source_target_pairs={{0,16},{8,24},{16,0},{24,8},{1,17},{9,25},{17,1},{25,9},{2,18},{10... | collective-permute-start | bytes 589832 | tf_op jit(solution)/shard_map/ppermute | solution.py:89
  513.6 28.6 %all-to-all-start.1 = ((bf16[8,96,1280]{2,1,0:T(8,128)(2,1)}), bf16[8,96,1280]{2,1,0:T(8,128)(2,1)S(1)}, u32[]{:S(2)}, u32[]{:S(2)}) async-start(bf16[8,96,1280]{2,1,0:T(8,128)(2,1)} %bitcast.271), calls=%async_computation.2 | async-start | bytes 3932160 | tf_op jit(solution)/shard_map/all_to_all | solution.py:861
  517.8 9.4 %collective-permute-start.50 = (bf16[96,1024]{1,0:T(8,128)(2,1)}, bf16[96,1024]{1,0:T(8,128)(2,1)S(1)}, u32[]{:S(2)}, u32[]{:S(2)}) collective-permute-start(bf16[96,1024]{1,0:T(8,128)(2,1)} %get-tuple-element.324), channel_id=1, source_target_pairs={{0,8},{8,16},{16,24},{24,0},{1,9},{9,17},{17,25},{25,1},{2,10},{10... | collective-permute-start | bytes 589832 | tf_op jit(solution)/shard_map/ppermute | solution.py:89
  544.5 7.7 %collective-permute-start.53 = (f32[48,2]{0,1:T(2,128)S(1)}, f32[48,2]{0,1:T(2,128)S(1)}, u32[]{:S(2)}, u32[]{:S(2)}) collective-permute-start(f32[48,2]{0,1:T(2,128)S(1)} %constant_dynamic-slice_fusion.3), channel_id=1, source_target_pairs={{0,1},{1,0},{2,3},{3,2},{4,5},{5,4},{6,7},{7,6},{8,9},{9,8},{10,11... | collective-permute-start | bytes 1160 | tf_op jit(solution)/shard_map/ppermute | solution.py:34
  (41 other events, 273.1 us)
Sparse Core Ops, SparseCore 0:
  54.8 51.8 all-gather.6
  119.3 51.7 all-gather.8
  189.2 56.4 all-gather.10
  347.0 145.8 reduce-scatter.1
